TPU v7x, 32 devices: a whole 2x2x4 slice. The times are simulated.
32 devices in a mesh: gx: 8 (over z, x), gy: 4 (over y, core).
Axes of the slice: x: 2, y: 2, z: 4, core: 2. Of those that a mesh axis runs over, the one named last changes fastest.
Arguments:
- guess: float32 [128, 128, 256], P('gx', 'gy'), may hold values from -6 to 6
- right_side: float32 [128, 128, 256], P('gx', 'gy'), may hold values from -6 to 6
- coefficient: float32 [128, 128, 256], P('gx', 'gy'), may hold values from 0.3 to 3
Outputs:
- solution: float32 [128, 128, 256], P('gx', 'gy')
All inputs are finite; a program needn't handle non-finite values.
Results may differ from a plain program's by a relative error of at most 0.0001.
Values sent between devices are 32-bit elements; how exact they have to be, the bound alone decides.
No kernel may reach another device: no remote copies, remote signals or barrier semaphores. Data moves between devices by JAX's collectives and lax.ppermute only.
A program may use at most 128 MiB of HBM per device.

v0:
```python
from functools import partial

import jax
import jax.numpy as jnp
from jax import lax
from jax.sharding import PartitionSpec as P

LEVELS = 4
SWEEPS = 3
CHEB = 8


RELAX_WEIGHT = 0.7
CHEBY_LOWER = 0.08
CHEBY_UPPER = 2.0


def padded_2(block, sides, width):
    for axis, dim in sides:
        count = lax.axis_size(axis)
        forward = [(i, i + 1) for i in range(count - 1)]
        backward = [(target, source) for source, target in forward]
        low = lax.ppermute(
            lax.slice_in_dim(block, block.shape[dim] - width, None, axis=dim), axis, forward
        )
        high = lax.ppermute(lax.slice_in_dim(block, 0, width, axis=dim), axis, backward)
        block = jnp.concatenate([low, block, high], axis=dim)
    return block


def shifted(x, axis, by):
    peers = lax.axis_size(axis)
    pairs = [(i, i + by) for i in range(peers) if 0 <= i + by < peers]
    return lax.ppermute(x, axis, pairs)


def offset_view(array, direction, offset):
    selector = [slice(1, -1), slice(1, -1), slice(1, -1)]
    selector[direction] = slice(1 + offset, array.shape[direction] - 1 + offset)
    return array[tuple(selector)]


def apply_operator(padded_field, padded_coef, factor):
    center_coef = padded_coef[1:-1, 1:-1, 1:-1]
    center_value = padded_field[1:-1, 1:-1, 1:-1]
    summed = jnp.zeros(center_value.shape, jnp.float32)
    for direction in range(3):
        for offset in (-1, 1):
            near_coef = offset_view(padded_coef, direction, offset)
            near_value = offset_view(padded_field, direction, offset)
            summed = summed + 0.5 * (center_coef + near_coef) * (center_value - near_value)
    return factor * summed


def diagonal_of(padded_coef, factor):
    center_coef = padded_coef[1:-1, 1:-1, 1:-1]
    summed = jnp.zeros(center_coef.shape, jnp.float32)
    for direction in range(3):
        for offset in (-1, 1):
            summed = summed + 0.5 * (center_coef + offset_view(padded_coef, direction, offset))
    return factor * summed


def zero_pad(array):
    return jnp.pad(array, 1)


def depth_pad(array):
    return jnp.pad(array, ((0, 0), (0, 0), (1, 1)))


def fine_pad(field):
    padded = padded_2(field, (("gx", 0), ("gy", 1)), 1)
    return depth_pad(padded)


def coarse_pad(field, group_size, columns):
    below = shifted(field[-1:], "gx", group_size)
    above = shifted(field[:1], "gx", -group_size)
    widened = jnp.concatenate((below, field, above), 0)
    padded = padded_2(widened, (("gy", 1),), 1)
    return depth_pad(padded)


def smooth(iterate, source, padded_coef, diagonal, factor, pad_field, zero_start):
    for sweep_index in range(SWEEPS):
        if sweep_index == 0 and zero_start:
            iterate = RELAX_WEIGHT * source / diagonal
        else:
            image = apply_operator(pad_field(iterate), padded_coef, factor)
            iterate = iterate + RELAX_WEIGHT * (source - image) / diagonal
    return iterate


def restrict(array):
    extent = array.shape
    blocks = array.reshape(extent[0] // 2, 2, extent[1] // 2, 2, extent[2] // 2, 2)
    return blocks.mean(axis=(1, 3, 5))


def prolong(array):
    return jnp.repeat(jnp.repeat(jnp.repeat(array, 2, 0), 2, 1), 2, 2)


def chebyshev(source, padded_coef, diagonal, factor):
    center_value = (CHEBY_UPPER + CHEBY_LOWER) / 2.0
    half_width = (CHEBY_UPPER - CHEBY_LOWER) / 2.0
    ratio_sigma = center_value / half_width
    weight_old = 1.0 / ratio_sigma
    iterate = jnp.zeros(source.shape, jnp.float32)
    residual = source
    direction_field = residual / diagonal / center_value
    for step_index in range(CHEB):
        iterate = iterate + direction_field
        residual = residual - apply_operator(zero_pad(direction_field), padded_coef, factor)
        weight_new = 1.0 / (2.0 * ratio_sigma - weight_old)
        direction_field = (
            weight_new * weight_old * direction_field
            + 2.0 * weight_new / half_width * (residual / diagonal)
        )
        weight_old = weight_new
    return iterate


def gather_rows(source, coarse_coef):
    stacked = lax.all_gather(jnp.stack((source, coarse_coef)), "gy", axis=2, tiled=True)
    return (stacked[0], stacked[1])


def widen(source, coarse_coef, group_size, rows_whole, level_index, columns):
    if level_index == LEVELS - 1:
        source, coarse_coef = (
            lax.all_gather(source, "gx", axis=0, tiled=True),
            lax.all_gather(coarse_coef, "gx", axis=0, tiled=True),
        )
        source, coarse_coef = gather_rows(source, coarse_coef)
        return (source, coarse_coef, columns, True)
    return (source, coarse_coef, group_size, rows_whole)


def narrow(correction, small_group, large_group):
    ratio = large_group // small_group
    if ratio == 1:
        return correction
    portion = correction.shape[0] // ratio
    position = lax.axis_index("gx") // small_group % ratio
    return lax.dynamic_slice_in_dim(correction, position * portion, portion, 0)


def body(guess, right_side, coefficient):
    columns = lax.axis_size("gx")
    padded_coef = fine_pad(coefficient)
    diagonal = diagonal_of(padded_coef, 1.0)
    fine_post = partial(
        smooth,
        source=right_side,
        padded_coef=padded_coef,
        diagonal=diagonal,
        factor=1.0,
        pad_field=fine_pad,
        zero_start=False,
    )
    iterate = fine_post(guess)
    entries = [(iterate, fine_post)]
    group_sizes = [1]
    row_flags = [False]
    residual = right_side - apply_operator(fine_pad(iterate), padded_coef, 1.0)
    coarse_coef = coefficient
    group_size = 1
    rows_whole = False
    for level_index in range(1, LEVELS):
        factor = 0.25**level_index
        source, coarse_coef, group_size, rows_whole = widen(
            restrict(residual), restrict(coarse_coef), group_size, rows_whole, level_index, columns
        )
        group_sizes.append(group_size)
        row_flags.append(rows_whole)
        if rows_whole:
            pad_field = zero_pad
        else:
            pad_field = partial(coarse_pad, group_size=group_size, columns=columns)
        padded_coef = pad_field(coarse_coef)
        diagonal = diagonal_of(padded_coef, factor)
        iterate = smooth(
            jnp.zeros_like(source), source, padded_coef, diagonal, factor, pad_field, True
        )
        residual = source - apply_operator(pad_field(iterate), padded_coef, factor)
        post = partial(
            smooth,
            source=source,
            padded_coef=padded_coef,
            diagonal=diagonal,
            factor=factor,
            pad_field=pad_field,
            zero_start=False,
        )
        entries.append((iterate, post))
    factor = 0.25**LEVELS
    source, coarse_coef, group_size, rows_whole = widen(
        restrict(residual), restrict(coarse_coef), group_size, rows_whole, LEVELS, columns
    )
    group_sizes.append(group_size)
    row_flags.append(True)
    padded_coef = zero_pad(coarse_coef)
    diagonal = diagonal_of(padded_coef, factor)
    correction = chebyshev(source, padded_coef, diagonal, factor)
    for level_index in range(LEVELS - 1, -1, -1):
        iterate, post = entries[level_index]
        correction = narrow(correction, group_sizes[level_index], group_sizes[level_index + 1])
        if row_flags[level_index + 1] and (not row_flags[level_index]):
            row_count = correction.shape[1] // lax.axis_size("gy")
            correction = lax.dynamic_slice_in_dim(
                correction, lax.axis_index("gy") * row_count, row_count, 1
            )
        iterate = iterate + prolong(correction)
        correction = post(iterate)
    return correction


def solution(mesh):
    return jax.shard_map(
        body,
        mesh=mesh,
        in_specs=(P("gx", "gy", None), P("gx", "gy", None), P("gx", "gy", None)),
        out_specs=P("gx", "gy", None),
        check_vma=False,
    )
```

profile of v0, /device:TPU:0, one launch (start us, length us, event | category | flops | bytes accessed | tf_op | source)
XLA Modules:
  0.0 580.4 jit_solution(11061112940361889687)
XLA Ops:
  0.8 4.8 collective-permute-start
  7.8 4.5 collective-permute-start.1
  28.5 5.0 collective-permute-start.8
  35.0 5.1 collective-permute-done.9
  44.8 34.9 %reshape.60 = f32[8,2,16,2,128,2]{5,4,3,2,1,0:T(8,128)} reshape(f32[16,32,256]{2,1,0:T(8,128)S(1)} %copy-done) | data formatting | bytes 1048576 | tf_op jit(solution)/shard_map/reshape | solution.py:97
  79.6 12.2 %reduce_sum.73 = f32[8,16,128]{2,1,0:T(8,128)S(1)} reduce(f32[8,2,16,2,128,2]{5,4,3,2,1,0:T(8,128)} %reshape.60, f32[]{:T(128)} %constant.93.clone.1), dimensions={1,3,5}, to_apply=%region_1.2 | reduce | flops 114688 | bytes 589828 | tf_op jit(solution)/shard_map/reduce_sum | solution.py:98
  94.2 4.5 collective-permute-start.12
  100.3 4.2 collective-permute-done.13
  114.3 4.5 collective-permute-start.16
  120.2 4.9 collective-permute-start.22
  126.4 4.8 collective-permute-start.18
  137.5 35.6 %reshape.59 = f32[8,2,16,2,128,2]{5,4,3,2,1,0:T(8,128)} reshape(f32[16,32,256]{2,1,0:T(8,128)} %fusion.60) | data formatting | bytes 1048576 | tf_op jit(solution)/shard_map/reshape | solution.py:97
  173.1 12.2 %reduce_sum.72 = f32[8,16,128]{2,1,0:T(8,128)S(1)} reduce(f32[8,2,16,2,128,2]{5,4,3,2,1,0:T(8,128)} %reshape.59, f32[]{:T(128)} %constant.93.clone.1), dimensions={1,3,5}, to_apply=%region_0.1 | reduce | flops 114688 | bytes 589828 | tf_op jit(solution)/shard_map/reduce_sum | solution.py:98
  186.5 5.4 collective-permute-start.24
  193.3 5.1 collective-permute-done.25
  203.1 5.6 div.140
  213.4 4.5 collective-permute-start.28
  233.0 4.5 collective-permute-start.32
  238.9 4.9 collective-permute-start.38
  245.1 4.8 collective-permute-start.34
  254.6 5.6 reshape.61
  263.0 5.4 collective-permute-start.40
  269.8 5.1 collective-permute-done.41
  282.0 4.8 collective-permute-start.44
  303.5 30.4 %all_gather.10 = f32[16,4,32]{2,1,0:T(4,128)S(1)} all-gather(f32[2,4,32]{2,1,0:T(4,128)S(1)} %broadcast_multiply_fusion.4), channel_id=1, replica_groups=mesh['gx'=8,'gy'=4] {'gx'}, dimensions={0}, use_global_device_ids=true | all-gather | bytes 9216 | tf_op jit(solution)/shard_map/all_gather | solution.py:134
  336.6 4.2 collective-permute-done.51
  343.6 30.4 %all_gather.9 = f32[16,4,32]{2,1,0:T(4,128)S(1)} all-gather(f32[2,4,32]{2,1,0:T(4,128)S(1)} %broadcast_multiply_fusion.5), channel_id=1, replica_groups=mesh['gx'=8,'gy'=4] {'gx'}, dimensions={0}, use_global_device_ids=true | all-gather | bytes 9216 | tf_op jit(solution)/shard_map/all_gather | solution.py:133
  374.0 6.8 %all_gather.11 = f32[2,16,16,32]{3,1,0,2:T(8,128)S(1)} all-gather(f32[2,16,4,32]{3,1,0,2:T(8,128)S(1)} %copy.363), channel_id=1, replica_groups=mesh['gx'=8,'gy'=4] {'gy'}, dimensions={2}, use_global_device_ids=true | all-gather | bytes 81920 | tf_op jit(solution)/shard_map/all_gather | solution.py:126
  483.1 4.6 collective-permute-start.68
  500.5 4.8 collective-permute-start.72
  527.0 4.5 collective-permute-start.76
  533.2 4.4 collective-permute-done.77
  (438 shorter events, 294.6 us)
Async XLA Ops:
  0.8 12.8 %collective-permute-start = (f32[1,32,256]{2,1,0:T(8,128)S(1)}, f32[1,32,256]{2,1,0:T(8,128)S(1)}, u32[]{:S(2)}, u32[]{:S(2)}) collective-permute-start(f32[1,32,256]{2,1,0:T(8,128)S(1)} %get-tuple-element.75), channel_id=1, source_target_pairs={{0,4},{4,8},{8,12},{12,16},{16,20},{20,24},{24,28},{1,5},{5,9},{9,... | collective-permute-start | bytes 98312 | tf_op jit(solution)/shard_map/ppermute | solution.py:23
  5.7 9.1 %collective-permute-start.2 = (f32[1,32,256]{2,1,0:T(8,128)S(1)}, f32[1,32,256]{2,1,0:T(8,128)S(1)}, u32[]{:S(2)}, u32[]{:S(2)}) collective-permute-start(f32[1,32,256]{2,1,0:T(8,128)S(1)} %get-tuple-element.74), channel_id=1, source_target_pairs={{4,0},{8,4},{12,8},{16,12},{20,16},{24,20},{28,24},{5,1},{9,5},{13... | collective-permute-start | bytes 98312 | tf_op jit(solution)/shard_map/ppermute | solution.py:26
  7.8 9.6 %collective-permute-start.1 = (f32[1,32,256]{2,1,0:T(8,128)S(1)}, f32[1,32,256]{2,1,0:T(8,128)S(1)}, u32[]{:S(2)}, u32[]{:S(2)}) collective-permute-start(f32[1,32,256]{2,1,0:T(8,128)S(1)} %get-tuple-element.77), channel_id=1, source_target_pairs={{0,4},{4,8},{8,12},{12,16},{16,20},{20,24},{24,28},{1,5},{5,9},{9,... | collective-permute-start | bytes 98312 | tf_op jit(solution)/shard_map/ppermute | solution.py:23
  14.8 8.8 %collective-permute-start.4 = (f32[18,1,256]{2,1,0:T(1,128)S(1)}, f32[18,1,256]{2,1,0:T(1,128)S(1)}, u32[]{:S(2)}, u32[]{:S(2)}) collective-permute-start(f32[18,1,256]{2,1,0:T(1,128)S(1)} %get-tuple-element.59), channel_id=1, source_target_pairs={{0,1},{1,2},{2,3},{4,5},{5,6},{6,7},{8,9},{9,10},{10,11},{12,13},{... | collective-permute-start | bytes 55304 | tf_op jit(solution)/shard_map/ppermute | solution.py:23
  16.1 7.5 %collective-permute-start.6 = (f32[18,1,256]{2,1,0:T(1,128)S(1)}, f32[18,1,256]{2,1,0:T(1,128)S(1)}, u32[]{:S(2)}, u32[]{:S(2)}) collective-permute-start(f32[18,1,256]{2,1,0:T(1,128)S(1)} %get-tuple-element.58), channel_id=1, source_target_pairs={{1,0},{2,1},{3,2},{5,4},{6,5},{7,6},{9,8},{10,9},{11,10},{13,12},{... | collective-permute-start | bytes 55304 | tf_op jit(solution)/shard_map/ppermute | solution.py:26
  28.5 6.6 %collective-permute-start.8 = (f32[1,32,256]{2,1,0:T(8,128)S(1)}, f32[1,32,256]{2,1,0:T(8,128)S(1)}, u32[]{:S(2)}, u32[]{:S(2)}) collective-permute-start(f32[1,32,256]{2,1,0:T(8,128)S(1)} %get-tuple-element.72), channel_id=1, source_target_pairs={{0,4},{4,8},{8,12},{12,16},{16,20},{20,24},{24,28},{1,5},{5,9},{9,... | collective-permute-start | bytes 98312 | tf_op jit(solution)/shard_map/ppermute | solution.py:23
  33.5 6.7 %collective-permute-start.9 = (f32[1,32,256]{2,1,0:T(8,128)S(1)}, f32[1,32,256]{2,1,0:T(8,128)S(1)}, u32[]{:S(2)}, u32[]{:S(2)}) collective-permute-start(f32[1,32,256]{2,1,0:T(8,128)S(1)} %get-tuple-element.73), channel_id=1, source_target_pairs={{4,0},{8,4},{12,8},{16,12},{20,16},{24,20},{28,24},{5,1},{9,5},{13... | collective-permute-start | bytes 98312 | tf_op jit(solution)/shard_map/ppermute | solution.py:26
  40.2 51.6 %collective-permute-start.10 = (f32[18,1,256]{2,1,0:T(1,128)S(1)}, f32[18,1,256]{2,1,0:T(1,128)S(1)}, u32[]{:S(2)}, u32[]{:S(2)}) collective-permute-start(f32[18,1,256]{2,1,0:T(1,128)S(1)} %get-tuple-element.56), channel_id=1, source_target_pairs={{0,1},{1,2},{2,3},{4,5},{5,6},{6,7},{8,9},{9,10},{10,11},{12,13},{... | collective-permute-start | bytes 55304 | tf_op jit(solution)/shard_map/ppermute | solution.py:23
  43.5 48.4 %collective-permute-start.11 = (f32[18,1,256]{2,1,0:T(1,128)S(1)}, f32[18,1,256]{2,1,0:T(1,128)S(1)}, u32[]{:S(2)}, u32[]{:S(2)}) collective-permute-start(f32[18,1,256]{2,1,0:T(1,128)S(1)} %get-tuple-element.57), channel_id=1, source_target_pairs={{1,0},{2,1},{3,2},{5,4},{6,5},{7,6},{9,8},{10,9},{11,10},{13,12},{... | collective-permute-start | bytes 55304 | tf_op jit(solution)/shard_map/ppermute | solution.py:26
  104.6 8.4 %collective-permute-start.14 = (f32[18,1,256]{2,1,0:T(1,128)S(1)}, f32[18,1,256]{2,1,0:T(1,128)S(1)}, u32[]{:S(2)}, u32[]{:S(2)}) collective-permute-start(f32[18,1,256]{2,1,0:T(1,128)S(1)} %get-tuple-element.54), channel_id=1, source_target_pairs={{0,1},{1,2},{2,3},{4,5},{5,6},{6,7},{8,9},{9,10},{10,11},{12,13},{... | collective-permute-start | bytes 55304 | tf_op jit(solution)/shard_map/ppermute | solution.py:23
  108.5 11.7 %collective-permute-start.20 = (f32[1,16,128]{2,1,0:T(8,128)S(1)}, f32[1,16,128]{2,1,0:T(8,128)S(1)}, u32[]{:S(2)}, u32[]{:S(2)}) collective-permute-start(f32[1,16,128]{2,1,0:T(8,128)S(1)} %get-tuple-element.109), channel_id=1, source_target_pairs={{0,4},{4,8},{8,12},{12,16},{16,20},{20,24},{24,28},{1,5},{5,9},{9,... | collective-permute-start | bytes 24584 | tf_op jit(solution)/shard_map/ppermute | solution.py:34
  111.7 8.5 %collective-permute-start.21 = (f32[1,16,128]{2,1,0:T(8,128)S(1)}, f32[1,16,128]{2,1,0:T(8,128)S(1)}, u32[]{:S(2)}, u32[]{:S(2)}) collective-permute-start(f32[1,16,128]{2,1,0:T(8,128)S(1)} %get-tuple-element.108), channel_id=1, source_target_pairs={{4,0},{8,4},{12,8},{16,12},{20,16},{24,20},{28,24},{5,1},{9,5},{13... | collective-permute-start | bytes 24584 | tf_op jit(solution)/shard_map/ppermute | solution.py:34
  114.3 12.1 %collective-permute-start.16 = (f32[1,32,256]{2,1,0:T(8,128)S(1)}, f32[1,32,256]{2,1,0:T(8,128)S(1)}, u32[]{:S(2)}, u32[]{:S(2)}) collective-permute-start(f32[1,32,256]{2,1,0:T(8,128)S(1)} %get-tuple-element.68), channel_id=1, source_target_pairs={{0,4},{4,8},{8,12},{12,16},{16,20},{20,24},{24,28},{1,5},{5,9},{9,... | collective-permute-start | bytes 98312 | tf_op jit(solution)/shard_map/ppermute | solution.py:23
  118.8 7.5 %collective-permute-start.17 = (f32[1,32,256]{2,1,0:T(8,128)S(1)}, f32[1,32,256]{2,1,0:T(8,128)S(1)}, u32[]{:S(2)}, u32[]{:S(2)}) collective-permute-start(f32[1,32,256]{2,1,0:T(8,128)S(1)} %get-tuple-element.69), channel_id=1, source_target_pairs={{4,0},{8,4},{12,8},{16,12},{20,16},{24,20},{28,24},{5,1},{9,5},{13... | collective-permute-start | bytes 98312 | tf_op jit(solution)/shard_map/ppermute | solution.py:26
  120.2 12.4 %collective-permute-start.22 = (f32[10,1,128]{2,1,0:T(1,128)S(1)}, f32[10,1,128]{2,1,0:T(1,128)S(1)}, u32[]{:S(2)}, u32[]{:S(2)}) collective-permute-start(f32[10,1,128]{2,1,0:T(1,128)S(1)} %get-tuple-element.95), channel_id=1, source_target_pairs={{0,1},{1,2},{2,3},{4,5},{5,6},{6,7},{8,9},{9,10},{10,11},{12,13},{... | collective-permute-start | bytes 15368 | tf_op jit(solution)/shard_map/ppermute | solution.py:23
  125.0 7.5 %collective-permute-start.23 = (f32[10,1,128]{2,1,0:T(1,128)S(1)}, f32[10,1,128]{2,1,0:T(1,128)S(1)}, u32[]{:S(2)}, u32[]{:S(2)}) collective-permute-start(f32[10,1,128]{2,1,0:T(1,128)S(1)} %get-tuple-element.94), channel_id=1, source_target_pairs={{1,0},{2,1},{3,2},{5,4},{6,5},{7,6},{9,8},{10,9},{11,10},{13,12},{... | collective-permute-start | bytes 15368 | tf_op jit(solution)/shard_map/ppermute | solution.py:26
  126.4 7.0 %collective-permute-start.18 = (f32[18,1,256]{2,1,0:T(1,128)S(1)}, f32[18,1,256]{2,1,0:T(1,128)S(1)}, u32[]{:S(2)}, u32[]{:S(2)}) collective-permute-start(f32[18,1,256]{2,1,0:T(1,128)S(1)} %get-tuple-element.52), channel_id=1, source_target_pairs={{0,1},{1,2},{2,3},{4,5},{5,6},{6,7},{8,9},{9,10},{10,11},{12,13},{... | collective-permute-start | bytes 55304 | tf_op jit(solution)/shard_map/ppermute | solution.py:23
  186.5 6.8 %collective-permute-start.24 = (f32[1,16,128]{2,1,0:T(8,128)S(1)}, f32[1,16,128]{2,1,0:T(8,128)S(1)}, u32[]{:S(2)}, u32[]{:S(2)}) collective-permute-start(f32[1,16,128]{2,1,0:T(8,128)S(1)} %get-tuple-element.106), channel_id=1, source_target_pairs={{0,4},{4,8},{8,12},{12,16},{16,20},{20,24},{24,28},{1,5},{5,9},{9,... | collective-permute-start | bytes 24584 | tf_op jit(solution)/shard_map/ppermute | solution.py:34
  198.4 13.5 %collective-permute-start.26 = (f32[10,1,128]{2,1,0:T(1,128)S(1)}, f32[10,1,128]{2,1,0:T(1,128)S(1)}, u32[]{:S(2)}, u32[]{:S(2)}) collective-permute-start(f32[10,1,128]{2,1,0:T(1,128)S(1)} %get-tuple-element.92), channel_id=1, source_target_pairs={{0,1},{1,2},{2,3},{4,5},{5,6},{6,7},{8,9},{9,10},{10,11},{12,13},{... | collective-permute-start | bytes 15368 | tf_op jit(solution)/shard_map/ppermute | solution.py:23
  201.7 10.2 %collective-permute-start.27 = (f32[10,1,128]{2,1,0:T(1,128)S(1)}, f32[10,1,128]{2,1,0:T(1,128)S(1)}, u32[]{:S(2)}, u32[]{:S(2)}) collective-permute-start(f32[10,1,128]{2,1,0:T(1,128)S(1)} %get-tuple-element.93), channel_id=1, source_target_pairs={{1,0},{2,1},{3,2},{5,4},{6,5},{7,6},{9,8},{10,9},{11,10},{13,12},{... | collective-permute-start | bytes 15368 | tf_op jit(solution)/shard_map/ppermute | solution.py:26
  223.5 8.4 %collective-permute-start.30 = (f32[10,1,128]{2,1,0:T(1,128)S(1)}, f32[10,1,128]{2,1,0:T(1,128)S(1)}, u32[]{:S(2)}, u32[]{:S(2)}) collective-permute-start(f32[10,1,128]{2,1,0:T(1,128)S(1)} %get-tuple-element.90), channel_id=1, source_target_pairs={{0,1},{1,2},{2,3},{4,5},{5,6},{6,7},{8,9},{9,10},{10,11},{12,13},{... | collective-permute-start | bytes 15368 | tf_op jit(solution)/shard_map/ppermute | solution.py:23
  227.4 11.5 %collective-permute-start.36 = (f32[1,8,64]{2,1,0:T(8,128)S(1)}, f32[1,8,64]{2,1,0:T(8,128)S(1)}, u32[]{:S(2)}, u32[]{:S(2)}) collective-permute-start(f32[1,8,64]{2,1,0:T(8,128)S(1)} %get-tuple-element.137), channel_id=1, source_target_pairs={{0,4},{4,8},{8,12},{12,16},{16,20},{20,24},{24,28},{1,5},{5,9},{9,... | collective-permute-start | bytes 6152 | tf_op jit(solution)/shard_map/ppermute | solution.py:34
  230.6 8.3 %collective-permute-start.37 = (f32[1,8,64]{2,1,0:T(8,128)S(1)}, f32[1,8,64]{2,1,0:T(8,128)S(1)}, u32[]{:S(2)}, u32[]{:S(2)}) collective-permute-start(f32[1,8,64]{2,1,0:T(8,128)S(1)} %get-tuple-element.136), channel_id=1, source_target_pairs={{4,0},{8,4},{12,8},{16,12},{20,16},{24,20},{28,24},{5,1},{9,5},{13... | collective-permute-start | bytes 6152 | tf_op jit(solution)/shard_map/ppermute | solution.py:34
  233.0 12.1 %collective-permute-start.32 = (f32[1,16,128]{2,1,0:T(8,128)S(1)}, f32[1,16,128]{2,1,0:T(8,128)S(1)}, u32[]{:S(2)}, u32[]{:S(2)}) collective-permute-start(f32[1,16,128]{2,1,0:T(8,128)S(1)} %get-tuple-element.102), channel_id=1, source_target_pairs={{0,4},{4,8},{8,12},{12,16},{16,20},{20,24},{24,28},{1,5},{5,9},{9,... | collective-permute-start | bytes 24584 | tf_op jit(solution)/shard_map/ppermute | solution.py:34
  237.6 7.5 %collective-permute-start.33 = (f32[1,16,128]{2,1,0:T(8,128)S(1)}, f32[1,16,128]{2,1,0:T(8,128)S(1)}, u32[]{:S(2)}, u32[]{:S(2)}) collective-permute-start(f32[1,16,128]{2,1,0:T(8,128)S(1)} %get-tuple-element.103), channel_id=1, source_target_pairs={{4,0},{8,4},{12,8},{16,12},{20,16},{24,20},{28,24},{5,1},{9,5},{13... | collective-permute-start | bytes 24584 | tf_op jit(solution)/shard_map/ppermute | solution.py:34
  238.9 12.4 %collective-permute-start.38 = (f32[6,1,64]{2,1,0:T(1,128)S(1)}, f32[6,1,64]{2,1,0:T(1,128)S(1)}, u32[]{:S(2)}, u32[]{:S(2)}) collective-permute-start(f32[6,1,64]{2,1,0:T(1,128)S(1)} %get-tuple-element.123), channel_id=1, source_target_pairs={{0,1},{1,2},{2,3},{4,5},{5,6},{6,7},{8,9},{9,10},{10,11},{12,13},{... | collective-permute-start | bytes 4616 | tf_op jit(solution)/shard_map/ppermute | solution.py:23
  243.8 7.5 %collective-permute-start.39 = (f32[6,1,64]{2,1,0:T(1,128)S(1)}, f32[6,1,64]{2,1,0:T(1,128)S(1)}, u32[]{:S(2)}, u32[]{:S(2)}) collective-permute-start(f32[6,1,64]{2,1,0:T(1,128)S(1)} %get-tuple-element.122), channel_id=1, source_target_pairs={{1,0},{2,1},{3,2},{5,4},{6,5},{7,6},{9,8},{10,9},{11,10},{13,12},{... | collective-permute-start | bytes 4616 | tf_op jit(solution)/shard_map/ppermute | solution.py:26
  245.1 6.9 %collective-permute-start.34 = (f32[10,1,128]{2,1,0:T(1,128)S(1)}, f32[10,1,128]{2,1,0:T(1,128)S(1)}, u32[]{:S(2)}, u32[]{:S(2)}) collective-permute-start(f32[10,1,128]{2,1,0:T(1,128)S(1)} %get-tuple-element.88), channel_id=1, source_target_pairs={{0,1},{1,2},{2,3},{4,5},{5,6},{6,7},{8,9},{9,10},{10,11},{12,13},{... | collective-permute-start | bytes 15368 | tf_op jit(solution)/shard_map/ppermute | solution.py:23
  263.0 6.8 %collective-permute-start.40 = (f32[1,8,64]{2,1,0:T(8,128)S(1)}, f32[1,8,64]{2,1,0:T(8,128)S(1)}, u32[]{:S(2)}, u32[]{:S(2)}) collective-permute-start(f32[1,8,64]{2,1,0:T(8,128)S(1)} %get-tuple-element.134), channel_id=1, source_target_pairs={{0,4},{4,8},{8,12},{12,16},{16,20},{20,24},{24,28},{1,5},{5,9},{9,... | collective-permute-start | bytes 6152 | tf_op jit(solution)/shard_map/ppermute | solution.py:34
  282.0 8.6 %collective-permute-start.44 = (f32[1,8,64]{2,1,0:T(8,128)S(1)}, f32[1,8,64]{2,1,0:T(8,128)S(1)}, u32[]{:S(2)}, u32[]{:S(2)}) collective-permute-start(f32[1,8,64]{2,1,0:T(8,128)S(1)} %get-tuple-element.132), channel_id=1, source_target_pairs={{0,4},{4,8},{8,12},{12,16},{16,20},{20,24},{24,28},{1,5},{5,9},{9,... | collective-permute-start | bytes 6152 | tf_op jit(solution)/shard_map/ppermute | solution.py:34
  299.4 34.6 %collective-permute-start.48 = (f32[1,8,64]{2,1,0:T(8,128)S(1)}, f32[1,8,64]{2,1,0:T(8,128)S(1)}, u32[]{:S(2)}, u32[]{:S(2)}) collective-permute-start(f32[1,8,64]{2,1,0:T(8,128)S(1)} %get-tuple-element.130), channel_id=1, source_target_pairs={{0,4},{4,8},{8,12},{12,16},{16,20},{20,24},{24,28},{1,5},{5,9},{9,... | collective-permute-start | bytes 6152 | tf_op jit(solution)/shard_map/ppermute | solution.py:34
  302.2 31.7 %collective-permute-start.49 = (f32[1,8,64]{2,1,0:T(8,128)S(1)}, f32[1,8,64]{2,1,0:T(8,128)S(1)}, u32[]{:S(2)}, u32[]{:S(2)}) collective-permute-start(f32[1,8,64]{2,1,0:T(8,128)S(1)} %get-tuple-element.131), channel_id=1, source_target_pairs={{4,0},{8,4},{12,8},{16,12},{20,16},{24,20},{28,24},{5,1},{9,5},{13... | collective-permute-start | bytes 6152 | tf_op jit(solution)/shard_map/ppermute | solution.py:34
  (120 other events, 1825.7 us)
where the time goes:
time: 587 us; the launch traced here: 580 us
  starting transfers between devices  213 us (36%)
  local copies, waits for them, and re-layouts  116 us (20%)
  waiting for transfers between devices  106 us (18%)
  other arithmetic  75.1 us (13%)
  blocking collectives  67.6 us (12%)
    ppermute x30, starting transfers between devices, padded_2(): lax.ppermute(lax.slice_in_dim(block, block.shape[dim] - width, None, axis...  102 us
    reshape x5, local copies, waits for them, and re-layouts, restrict(): array.reshape(extent[0] // 2, 2, extent[1] // 2, 2, extent[2] // 2, 2)  80.7 us
    ppermute x28, starting transfers between devices, shifted(): return lax.ppermute(x, axis, pairs)  72.4 us
    ppermute x30, waiting for transfers between devices, padded_2(): lax.ppermute(lax.slice_in_dim(block, 0, width, axis=dim), axis, backward)  64.2 us
    ppermute x28, waiting for transfers between devices, shifted(): return lax.ppermute(x, axis, pairs)  40.8 us
    ppermute x30, starting transfers between devices, padded_2(): lax.ppermute(lax.slice_in_dim(block, 0, width, axis=dim), axis, backward)  39.3 us
    reduce_sum x8, other arithmetic, restrict(): return blocks.mean(axis=(1, 3, 5))  37.2 us
    all_gather x1, blocking collectives, widen(): lax.all_gather(coarse_coef, 'gx', axis=0, tiled=True)  30.4 us
  transfers between devices with their start and end apart: 88, of which 36 were waited for; matrix products, arithmetic and copies ran while one was open for 11% of the time, Pallas kernels for 0%

commit v1 on v0

v1 whole, which is shorter than its diff:
```python
from functools import partial

import jax
import jax.numpy as jnp
from jax import lax
from jax.experimental import pallas as pl
from jax.experimental.pallas import tpu as pltpu
from jax.sharding import PartitionSpec as P

LEVELS = 4
SWEEPS = 3
CHEB = 8

RELAX_WEIGHT = 0.7
CHEBY_LOWER = 0.08
CHEBY_UPPER = 2.0

F32 = jnp.float32
LANES = 128
FINE = SWEEPS + 1
COARSE = 8
SOURCE = COARSE - 1
POST = SWEEPS
VMEM_LIMIT = 56 * 1024 * 1024


def dot(a, b):
    return jnp.dot(a, b, precision=lax.Precision.HIGHEST, preferred_element_type=F32)


def iota(shape, dim):
    return lax.broadcasted_iota(jnp.int32, shape, dim)


def vmem(*shape):
    return pltpu.VMEM(shape, F32)


def roll(x, by, axis):
    return pltpu.roll(x, by % x.shape[axis], axis)


def weigh(coef, weights, scaled, diag, source, first, last, depth, row_edges, scale, omega):
    rows, lanes = coef.shape[1:]
    lane = iota((1, lanes), 1) % depth
    front, back = lane == 0, lane == depth - 1
    row = iota((rows, 1), 0)

    def step(p, carry):
        c = coef[p]
        lower, upper = coef[p - 1], coef[p + 1]
        left, right = roll(c, 1, 0), roll(c, -1, 0)
        near, far = roll(c, 1, 1), roll(c, -1, 1)
        near, far = jnp.where(front, 0.0, near), jnp.where(back, 0.0, far)
        if row_edges:
            left, right = jnp.where(row == 0, 0.0, left), jnp.where(row == rows - 1, 0.0, right)
        total = 6.0 * c + ((lower + upper) + (left + right) + (near + far))
        inverse = jnp.where(c > 0.0, omega / total, 0.0)
        weights[0, p] = (c + lower) * inverse
        weights[1, p] = (c + upper) * inverse
        left, right = (c + left) * inverse, (c + right) * inverse
        if row_edges:
            left, right = jnp.where(row == 0, 0.0, left), jnp.where(row == rows - 1, 0.0, right)
        weights[2, p] = left
        weights[3, p] = right
        weights[4, p] = jnp.where(front, 0.0, (c + near) * inverse)
        weights[5, p] = jnp.where(back, 0.0, (c + far) * inverse)
        scaled[p] = source(p) * inverse * (2.0 / scale)
        if diag is not None:
            diag[p] = total * (0.5 * scale / omega)
        return carry

    lax.fori_loop(first, last, step, 0)


def neighbours(field, weights, p):
    v = field[p]
    total = weights[0, p] * field[p - 1] + weights[1, p] * field[p + 1]
    total += weights[2, p] * roll(v, 1, 0) + weights[3, p] * roll(v, -1, 0)
    return v, total + (weights[4, p] * roll(v, 1, 1) + weights[5, p] * roll(v, -1, 1))


def sweep(field, out, weights, scaled, first, last):
    def step(p, carry):
        v, total = neighbours(field, weights, p)
        out[p] = (1.0 - RELAX_WEIGHT) * v + (scaled[p] + total)
        return carry

    lax.fori_loop(first, last, step, 0)


def residual(field, weights, scaled, diag, p):
    v, total = neighbours(field, weights, p)
    return (scaled[p] + total - RELAX_WEIGHT * v) * diag[p]


def halve_lanes(lanes, width, offset=0):
    return jnp.where(iota((lanes, width), 0) // 2 + offset == iota((lanes, width), 1), 0.125, 0.0).astype(F32)


def pair_rows(ref, count):
    return ref[pl.ds(0, count, stride=2), :] + ref[pl.ds(1, count, stride=2), :]


def fine_pre_kernel(guess, source, coef, low, high, left, right,
                    out, weights, scaled, up, down, b1, c1, v, c, w, diag, pairs, halved):
    nx, ny, nz = guess.shape
    planes = nx + 2 * FINE

    def fill(target, own, base, width):
        at = FINE - width
        count = nx + 2 * width
        offset = sum(nx + 2 * k for k in base)
        message = sum(base)

        def rest(k, carry):
            target[at + k, ny:] = jnp.concatenate((right[offset + k], left[offset + k]), 0)
            return carry

        lax.fori_loop(0, count, rest, 0)

        def main(k, carry):
            target[FINE + k, :ny] = own[k]
            return carry

        lax.fori_loop(0, nx, main, 0)
        for k in range(width):
            target[at + k, :ny] = low[message + k]
            target[FINE + nx + k, :ny] = high[message + k]

    fill(v, guess, (), FINE)
    fill(scaled, source, (FINE,), FINE - 1)
    fill(c, coef, (FINE, FINE - 1), FINE)
    weigh(c, weights, scaled, diag, lambda p: scaled[p], 1, planes - 1, nz, False, 1.0, RELAX_WEIGHT)
    sweep(v, w, weights, scaled, 1, planes - 1)
    sweep(w, v, weights, scaled, 2, planes - 2)
    sweep(v, w, weights, scaled, 3, planes - 3)

    def copy(p, carry):
        out[p] = w[FINE + p, :ny]
        return carry

    lax.fori_loop(0, nx, copy, 0)

    matrix = halve_lanes(nz, nz // 2)

    def halve(fetch, out):
        def step(q, carry):
            pairs[pl.ds(pl.multiple_of(q * ny, ny), ny), :] = fetch(2 * q) + fetch(2 * q + 1)
            return carry

        lax.fori_loop(0, nx // 2, step, 0)
        halved[...] = dot(pairs[...], matrix)
        out[...] = pair_rows(halved, nx * ny // 4).reshape(out.shape)

    halve(lambda k: residual(w, weights, scaled, diag, FINE + k)[:ny], b1)
    halve(lambda k: coef[k], c1)

    n1 = nx // 2
    r1 = ny // 2
    up[:SOURCE] = b1[n1 - SOURCE:]
    down[:SOURCE] = b1[:SOURCE]
    up[SOURCE:SOURCE + COARSE] = c1[n1 - COARSE:]
    down[SOURCE:SOURCE + COARSE] = c1[:COARSE]
    at = SOURCE + COARSE
    for k in range(POST):
        for i in range(2):
            for j in range(2):
                rows, lanes = pl.ds(i * r1, r1), pl.ds(j * (nz // 2), nz // 2)
                up[at] = w[FINE + nx - POST + k, rows, lanes]
                down[at] = w[FINE + k, rows, lanes]
                at += 1


def rows_kernel(b1, c1, v, low, high, up, down):
    n1, r1, half = b1.shape
    nx, ny = 2 * n1, 2 * r1

    def edge(take, at):
        up[at] = take(r1 - COARSE, COARSE)
        down[at] = take(0, COARSE)

    at = 0
    for k in range(SOURCE):
        edge(lambda s, n: low[k, pl.ds(s, n), :], at)
        edge(lambda s, n: high[k, pl.ds(s, n), :], at + SOURCE + n1)
        at += 1
    for k in range(n1):
        edge(lambda s, n: b1[k, pl.ds(s, n), :], at)
        at += 1
    at += SOURCE
    for k in range(COARSE):
        edge(lambda s, n: low[SOURCE + k, pl.ds(s, n), :], at)
        edge(lambda s, n: high[SOURCE + k, pl.ds(s, n), :], at + COARSE + n1)
        at += 1
    for k in range(n1):
        edge(lambda s, n: c1[k, pl.ds(s, n), :], at)
        at += 1
    at += COARSE
    base = SOURCE + COARSE
    for k in range(POST):
        for j in range(2):
            rows = pl.ds(j * FINE, FINE)
            up[at, rows, :] = low[base + 4 * k + 2 + j, r1 - FINE:, :]
            down[at, rows, :] = low[base + 4 * k + j, :FINE, :]
            up[at + POST + nx, rows, :] = high[base + 4 * k + 2 + j, r1 - FINE:, :]
            down[at + POST + nx, rows, :] = high[base + 4 * k + j, :FINE, :]
        at += 1

    def own(k, carry):
        for j in range(2):
            rows, lanes = pl.ds(j * FINE, FINE), pl.ds(j * half, half)
            up[at + k, rows, :] = v[k, ny - FINE:, lanes]
            down[at + k, rows, :] = v[k, :FINE, lanes]
        return carry

    lax.fori_loop(0, nx, own, 0)


def coarse_pre_kernel(b1, c1, low, high, left, right,
                      v, weights, scaled, send, c, w, diag, halved, c2):
    n1, r1, lanes = b1.shape
    planes = n1 + 2 * COARSE
    scale = 0.25

    def fill(target, own, base, offset, width):
        at = COARSE - width

        def rest(k, carry):
            target[at + k, r1:] = jnp.concatenate((right[offset + k], left[offset + k]), 0)
            return carry

        lax.fori_loop(0, n1 + 2 * width, rest, 0)
        for k in range(n1):
            target[COARSE + k, :r1] = own[k]
        for k in range(width):
            target[at + k, :r1] = low[base + k]
            target[COARSE + n1 + k, :r1] = high[base + k]

    fill(scaled, b1, 0, 0, SOURCE)
    fill(c, c1, SOURCE, n1 + 2 * SOURCE, COARSE)
    weigh(c, weights, scaled, diag, lambda p: scaled[p], 1, planes - 1, lanes, False, scale, RELAX_WEIGHT)
    sweep(scaled, w, weights, scaled, 2, planes - 2)
    sweep(w, v, weights, scaled, 3, planes - 3)

    n2, r2 = n1 // 2, r1 // 2
    matrix = jnp.concatenate((halve_lanes(lanes, LANES), halve_lanes(lanes, LANES, lanes // 2)), 0)

    def halve(fetch):
        wide = jnp.concatenate(
            [
                jnp.concatenate(
                    [fetch(2 * (q + g * (n2 // 2))) + fetch(2 * (q + g * (n2 // 2)) + 1) for g in range(2)], 1
                )
                for q in range(n2 // 2)
            ],
            0,
        )
        halved[...] = dot(wide, matrix)
        return pair_rows(halved, n2 // 2 * r2).reshape(n2 // 2, r2, LANES)

    c2[...] = halve(lambda k: c1[k])
    b2 = halve(lambda k: residual(v, weights, scaled, diag, COARSE + k)[:r1])
    half = n2 // 2
    for d in range(send.shape[0]):
        send[d, :half] = b2
        send[d, half:] = c2[...]


def pads(ref, depth, count):
    lanes = ref.shape[2]
    lane = iota((1, lanes), 1)
    ref[0] = jnp.where(lane < depth, 0.0, roll(ref[count], depth, 1))
    ref[count + 1] = jnp.where(lane >= lanes - depth, 0.0, roll(ref[1], -depth, 1))


def regroup(depth):
    source, target = iota((2 * LANES, LANES), 0), iota((2 * LANES, LANES), 1)
    group, lane = source // LANES, source % LANES
    block, z = lane // depth, lane % depth
    return (2 * block + group) * (depth // 2) + z // 2 == target


def solve_kernel(place_ref, gathered, v1, w1, s1, v0, w0, s0, low, high, left, right, out,
                 c2, a2, y2, g2, s2, d2, c3, a3, y3, g3, s3, d3, c4, b4, y4, g4, s4,
                 wide2, thin2, wide3, thin3, spread, u1, t1, u0, t0, *, gx, gy):
    half = gathered.shape[1] // 2
    r2 = gathered.shape[2]
    n2, m2 = 2 * half, s2.shape[0] - 2
    rows2 = s2.shape[1]
    depth2 = LANES // 2
    lane = iota((1, LANES), 1)

    def unpack(i, carry):
        for j in range(gy):
            for k in range(half):
                for which, target in enumerate((s2, c2)):
                    one = gathered[i * gy + j, which * half + k]
                    two = gathered[(i + gx // 2) * gy + j, which * half + k]
                    rows = pl.ds(j * r2, r2)
                    target[1 + i * n2 + k, rows, :] = jnp.where(lane < depth2, one, roll(two, depth2, 1))
                    target[1 + i * n2 + half + k, rows, :] = jnp.where(lane < depth2, roll(one, depth2, 1), two)
        return carry

    lax.fori_loop(0, gx // 2, unpack, 0)

    def level_in(c, source, weights, scaled, diag, depth, scale, omega):
        count = c.shape[0] - 2
        pads(c, depth, count)
        weigh(c, weights, scaled, diag, source, 1, count + 1, depth, True, scale, omega)

    def smooth(first, other, weights, scaled, depth, count, sweeps):
        for _ in range(sweeps):
            pads(first, depth, count)
            sweep(first, other, weights, scaled, 1, count + 1)
            first, other = other, first
        return first, other

    def down(fetch, wide, thin, depth, out, count, scale=1.0):
        rows = wide.shape[0] // (count // 4)
        for m in range(count // 4):
            for g in range(2):
                at = g * (count // 2) + 2 * m + 1
                wide[m * rows:(m + 1) * rows, g * LANES:(g + 1) * LANES] = fetch(at) + fetch(at + 1)
        thin[...] = dot(wide[...], jnp.where(regroup(depth), 0.125, 0.0).astype(F32))
        total = pair_rows(thin, thin.shape[0] // 2)
        out[1:1 + count // 4] = total.reshape(count // 4, rows // 2, LANES)

    def up(coarse, wide, thin, depth, fine, count):
        rows = wide.shape[0] // (count // 4)
        matrix = jnp.where(regroup(depth), 1.0, 0.0).astype(F32)
        for g in range(2):
            part = matrix[g * LANES:(g + 1) * LANES]
            x = coarse[1:1 + count // 4].reshape(thin.shape[0] // 2, LANES)
            x = lax.dot_general(x, part, (((1,), (1,)), ((), ())), precision=lax.Precision.HIGHEST,
                                preferred_element_type=F32)
            thin[pl.ds(0, thin.shape[0] // 2, stride=2), :] = x
            thin[pl.ds(1, thin.shape[0] // 2, stride=2), :] = x
            for m in range(count // 4):
                value = thin[m * rows:(m + 1) * rows, :]
                for k in range(2):
                    at = g * (count // 2) + 2 * m + 1 + k
                    fine[at] = fine[at] + value

    m3, m4 = c3.shape[0] - 2, c4.shape[0] - 2
    level_in(c2, lambda p: s2[p], g2, s2, d2, depth2, 0.25**2, RELAX_WEIGHT)
    for p in range(1, m2 + 1):
        a2[p] = s2[p]
    x2, z2 = smooth(a2, y2, g2, s2, depth2, m2, SWEEPS - 1)
    pads(x2, depth2, m2)
    down(lambda p: residual(x2, g2, s2, d2, p), wide2, thin2, depth2, s3, m2)
    down(lambda p: c2[p], wide2, thin2, depth2, c3, m2)

    depth3, depth4 = depth2 // 2, depth2 // 4
    level_in(c3, lambda p: s3[p], g3, s3, d3, depth3, 0.25**3, RELAX_WEIGHT)
    for p in range(1, m3 + 1):
        a3[p] = s3[p]
    x3, z3 = smooth(a3, y3, g3, s3, depth3, m3, SWEEPS - 1)
    pads(x3, depth3, m3)
    down(lambda p: residual(x3, g3, s3, d3, p), wide3, thin3, depth3, s4, m3)
    down(lambda p: c3[p], wide3, thin3, depth3, c4, m3)

    level_in(c4, lambda p: s4[p], g4, s4, None, depth4, 0.25**4, 1.0)
    theta, delta = (CHEBY_UPPER + CHEBY_LOWER) / 2.0, (CHEBY_UPPER - CHEBY_LOWER) / 2.0
    sigma = theta / delta
    rho = 1.0 / sigma
    res = [s4[p] for p in range(1, m4 + 1)]
    direction = [r / theta for r in res]
    total = [jnp.zeros_like(r) for r in res]
    for _ in range(CHEB):
        for p in range(m4):
            total[p] = total[p] + direction[p]
            y4[1 + p] = direction[p]
        pads(y4, depth4, m4)
        for p in range(m4):
            _, near = neighbours(y4, g4, 1 + p)
            res[p] = res[p] - (direction[p] - near)
        rho_new = 1.0 / (2.0 * sigma - rho)
        direction = [rho_new * rho * d + (2.0 * rho_new / delta) * r for d, r in zip(direction, res)]
        rho = rho_new
    for p in range(m4):
        b4[1 + p] = total[p]

    up(b4, wide3, thin3, depth3, x3, m3)
    x3, z3 = smooth(x3, z3, g3, s3, depth3, m3, SWEEPS)
    up(x3, wide2, thin2, depth2, x2, m2)
    x2, z2 = smooth(x2, z2, g2, s2, depth2, m2, SWEEPS)

    at_x, at_y = place_ref[0], place_ref[1]
    planes1, rows1, lanes1 = v1.shape
    n1 = planes1 - 2 * COARSE
    r1 = rows1 - 2 * COARSE
    y = iota((rows1, rows2), 0)
    y = jnp.where(y < r1 + COARSE, y, y - rows1) + r1 * at_y
    pick = jnp.where((y >= 0) & (y // 2 == iota((rows1, rows2), 1)), 1.0, 0.0).astype(F32)
    for h in range(2):
        source, target = iota((LANES, lanes1), 0), iota((LANES, lanes1), 1)
        spread[h] = jnp.where(source == h * depth2 + target // 2, 1.0, 0.0).astype(F32)

    reach = SWEEPS + 2
    for t in range(-((reach + 1) // 2), (n1 + reach + 1) // 2):
        x = at_x * n2 + t
        inside = jnp.where((x >= 0) & (x < gx * n2), 1.0, 0.0).astype(F32)
        x = jnp.clip(x, 0, gx * n2 - 1)
        block = x // m2
        plane = x2[1 + x - block * m2]
        value = dot(dot(pick, plane), spread[block]) * inside
        for k in range(2):
            p = COARSE + 2 * t + k
            u1[p] = v1[p] + value
    sweep(u1, t1, w1, s1, COARSE - 4, COARSE + n1 + 4)
    sweep(t1, u1, w1, s1, COARSE - 3, COARSE + n1 + 3)
    sweep(u1, t1, w1, s1, COARSE - 2, COARSE + n1 + 2)

    nx, ny, nz = v0.shape
    rows0 = u0.shape[1]

    def own(k, carry):
        u0[FINE + k, :ny] = v0[k]
        return carry

    lax.fori_loop(0, nx, own, 0)
    base = SOURCE + COARSE
    for k in range(POST):
        for i in range(2):
            for j in range(2):
                rows, lanes = pl.ds(i * r1, r1), pl.ds(j * lanes1, lanes1)
                u0[FINE - POST + k, rows, lanes] = low[base + 4 * k + 2 * i + j]
                u0[FINE + nx + k, rows, lanes] = high[base + 4 * k + 2 * i + j]
    base = 2 * n1 + 2 * SOURCE + 2 * COARSE

    def sides(k, carry):
        for j in range(2):
            rows, lanes = pl.ds(j * FINE, FINE), pl.ds(j * lanes1, lanes1)
            u0[FINE - POST + k, ny:, lanes] = jnp.concatenate((right[base + k, rows, :], left[base + k, rows, :]), 0)
        return carry

    lax.fori_loop(0, nx + 2 * POST, sides, 0)

    y = iota((rows0, rows1), 0)
    y = jnp.where(y < ny + FINE, y, y - rows0)
    y = jnp.where(y >= 0, y // 2, rows1 - (1 - y) // 2)
    pick = jnp.where(y == iota((rows0, rows1), 1), 1.0, 0.0).astype(F32)
    source, target = iota((lanes1, nz), 0), iota((lanes1, nz), 1)
    widen = jnp.where(source == target // 2, 1.0, 0.0).astype(F32)

    def add(t, carry):
        value = dot(dot(pick, t1[COARSE - 2 + t]), widen)
        for k in range(2):
            p = FINE - 4 + 2 * t + k
            u0[p] = u0[p] + value
        return carry

    lax.fori_loop(0, n1 + 4, add, 0)
    sweep(u0, t0, w0, s0, FINE - 2, FINE + nx + 2)
    sweep(t0, u0, w0, s0, FINE - 1, FINE + nx + 1)

    def last(p, carry):
        v, total = neighbours(u0, w0, p)
        out[p - FINE] = ((1.0 - RELAX_WEIGHT) * v + (s0[p] + total))[:ny]
        return carry

    lax.fori_loop(FINE, FINE + nx, last, 0)


def call(kernel, outs, scratch, *args, scalars=0):
    specs = [pl.BlockSpec(memory_space=pltpu.SMEM if k < scalars else pltpu.VMEM) for k in range(len(args))]
    return pl.pallas_call(
        kernel,
        out_shape=outs,
        in_specs=specs,
        out_specs=[pl.BlockSpec(memory_space=pltpu.VMEM) for _ in outs],
        scratch_shapes=scratch,
        compiler_params=pltpu.CompilerParams(vmem_limit_bytes=VMEM_LIMIT),
    )(*args)


def shape(*dims):
    return jax.ShapeDtypeStruct(dims, F32)


def exchange(up, down, axis):
    count = lax.axis_size(axis)
    forward = [(i, i + 1) for i in range(count - 1)]
    backward = [(target, source) for source, target in forward]
    return lax.ppermute(up, axis, forward), lax.ppermute(down, axis, backward)


def body(guess, right_side, coefficient):
    gx, gy = lax.axis_size("gx"), lax.axis_size("gy")
    nx, ny, nz = guess.shape
    fields = ((guess, FINE), (right_side, FINE - 1), (coefficient, FINE))
    low, high = exchange(
        jnp.concatenate([f[nx - k:] for f, k in fields], 0), jnp.concatenate([f[:k] for f, k in fields], 0), "gx"
    )

    def rows(cut):
        parts, at = [], 0
        for f, k in fields:
            parts += [cut(low[at:at + k]), cut(f), cut(high[at:at + k])]
            at += k
        return jnp.concatenate(parts, 0)

    left, right = exchange(rows(lambda f: f[:, ny - FINE:]), rows(lambda f: f[:, :FINE]), "gy")

    planes0, rows0 = nx + 2 * FINE, ny + 2 * FINE
    block0 = (planes0, rows0, nz)
    n1, r1, z1 = nx // 2, ny // 2, nz // 2
    message = (SOURCE + COARSE + 4 * POST, r1, z1)
    v0, w0, s0, up, down, b1, c1 = call(
        fine_pre_kernel,
        (shape(nx, ny, nz), shape(6, *block0), shape(*block0), shape(*message), shape(*message),
         shape(n1, r1, z1), shape(n1, r1, z1)),
        (vmem(*block0), vmem(*block0), vmem(*block0), vmem(*block0), vmem(n1 * ny, nz), vmem(n1 * ny, z1)),
        guess, right_side, coefficient, low, high, left, right,
    )
    low, high = exchange(up, down, "gx")
    count = 3 * n1 + 2 * SOURCE + 2 * COARSE + 2 * POST + n1
    up, down = call(rows_kernel, (shape(count, COARSE, z1),) * 2, (), b1, c1, v0, low, high)
    left, right = exchange(up, down, "gy")

    block1 = (n1 + 2 * COARSE, r1 + 2 * COARSE, z1)
    n2, r2 = n1 // 2, r1 // 2
    chunk = (n2, r2, LANES)
    v1, w1, s1, send = call(
        coarse_pre_kernel,
        (shape(*block1), shape(6, *block1), shape(*block1), shape(gx * gy, *chunk)),
        (vmem(*block1), vmem(*block1), vmem(*block1), vmem(n2 // 2 * r1, LANES), vmem(n2 // 2, r2, LANES)),
        b1, c1, low, high, left, right,
    )
    gathered = lax.all_to_all(send, ("gx", "gy"), 0, 0)
    place_at = jnp.stack((lax.axis_index("gx"), lax.axis_index("gy"))).astype(jnp.int32)

    m2, rows2 = gx * n2 // 2, gy * r2
    m3, rows3 = m2 // 4, rows2 // 2
    m4, rows4 = m3 // 4, rows3 // 2
    level2, level3, level4 = (m2 + 2, rows2, LANES), (m3 + 2, rows3, LANES), (m4 + 2, rows4, LANES)
    scratch = [
        vmem(*level2), vmem(*level2), vmem(*level2), vmem(6, *level2), vmem(*level2), vmem(*level2),
        vmem(*level3), vmem(*level3), vmem(*level3), vmem(6, *level3), vmem(*level3), vmem(*level3),
        vmem(*level4), vmem(*level4), vmem(*level4), vmem(6, *level4), vmem(*level4),
        vmem(m3 * rows2, 2 * LANES), vmem(m3 * rows2, LANES),
        vmem(m4 * rows3, 2 * LANES), vmem(m4 * rows3, LANES),
        vmem(2, LANES, z1), vmem(*block1), vmem(*block1), vmem(*block0), vmem(*block0),
    ]
    (out,) = call(
        partial(solve_kernel, gx=gx, gy=gy), (shape(nx, ny, nz),), scratch,
        place_at, gathered, v1, w1, s1, v0, w0, s0, low, high, left, right, scalars=1,
    )
    return out


def solution(mesh):
    return jax.shard_map(
        body,
        mesh=mesh,
        in_specs=(P("gx", "gy", None), P("gx", "gy", None), P("gx", "gy", None)),
        out_specs=P("gx", "gy", None),
        check_vma=False,
    )
```

time: 587 us -> 143 us (0.24); the launches traced: 580 us -> 143 us
  starting transfers between devices: 213 us -> 31 us
  local copies, waits for them, and re-layouts: 116 us -> 8.36 us
  other arithmetic: 75.1 us -> 0.71 us
  blocking collectives: 67.6 us -> 0 us
  waiting for transfers between devices: 106 us -> 41.9 us
  Pallas kernels: 0 us -> 60.5 us
    ppermute x88 -> x8, starting transfers between devices: 213 us -> 22.3 us  [exchange(): return (lax.ppermute(up, axis, forward), lax.ppermute(down, axis, backward))]
    reshape x12 -> x0, local copies, waits for them, and re-layouts: 89.3 us -> none  [the longest x5 80.7 us: restrict(): array.reshape(extent[0] // 2, 2, extent[1] // 2, 2, extent[2] // 2, 2)]
    ppermute x88 -> x8, waiting for transfers between devices: 106 us -> 27 us  [exchange(): return (lax.ppermute(up, axis, forward), lax.ppermute(down, axis, backward))]
    all_gather x3 -> x0, blocking collectives: 67.6 us -> none  [the longest x1 30.4 us: widen(): lax.all_gather(coarse_coef, 'gx', axis=0, tiled=True)]
    pallas_call x0 -> x4, Pallas kernels: none -> 60.5 us  [call(): pl.pallas_call(kernel, out_shape=outs, in_specs=specs, out_specs=[pl.Bloc...]
    reduce_sum x8 -> x0, other arithmetic: 37.2 us -> none  [restrict(): return blocks.mean(axis=(1, 3, 5))]
    add x33 -> x0, other arithmetic: 20.6 us -> none  [the longest x21 15.1 us: smooth(): iterate = iterate + RELAX_WEIGHT * (source - image) / diagonal]
    all_to_all x0 -> x1, waiting for transfers between devices: none -> 14.9 us  [body(): gathered = lax.all_to_all(send, ('gx', 'gy'), 0, 0)]
  transfers between devices with their start and end apart: 88 -> 9, of which waited for: 36 -> 7; matrix products, arithmetic and copies ran while one was open for 11% -> 1% of each run, Pallas kernels for 0% -> 0%
where the time goes in v1:
time: 143 us
  Pallas kernels  60.5 us (42%)
  waiting for transfers between devices  41.9 us (29%)
  starting transfers between devices  31 us (22%)
  local copies, waits for them, and re-layouts  8.36 us (6%)
    pallas_call x4, Pallas kernels, call(): pl.pallas_call(kernel, out_shape=outs, in_specs=specs, out_specs=[pl.Bloc...  60.5 us
    ppermute x8, waiting for transfers between devices, exchange(): return (lax.ppermute(up, axis, forward), lax.ppermute(down, axis, backward))  27 us
    ppermute x8, starting transfers between devices, exchange(): return (lax.ppermute(up, axis, forward), lax.ppermute(down, axis, backward))  22.3 us
    all_to_all x1, waiting for transfers between devices, body(): gathered = lax.all_to_all(send, ('gx', 'gy'), 0, 0)  14.9 us
    all_to_all x1, starting transfers between devices, body(): gathered = lax.all_to_all(send, ('gx', 'gy'), 0, 0)  8.73 us
    unnamed x26, local copies, waits for them, and re-layouts  6.26 us
  transfers between devices with their start and end apart: 9, of which 7 were waited for; matrix products, arithmetic and copies ran while one was open for 1% of the time, Pallas kernels for 0%

profile of v1, /device:TPU:0, one launch (start us, length us, event | category | flops | bytes accessed | tf_op | source)
XLA Modules:
  0.0 142.7 jit_solution(16693852820724236150)
XLA Ops:
  0.0 1.0 fusion.1
  1.0 1.1 fusion
  2.1 4.9 %collective-permute-start = (f32[11,32,256]{2,1,0:T(8,128)S(1)}, f32[11,32,256]{2,1,0:T(8,128)S(1)}, u32[]{:S(2)}, u32[]{:S(2)}) collective-permute-start(f32[11,32,256]{2,1,0:T(8,128)S(1)} %pad_maximum_fusion), channel_id=1, source_target_pairs={{0,4},{4,8},{8,12},{12,16},{16,20},{20,24},{24,28},{1,5},{5,9},{9,... | collective-permute-start | bytes 1081352 | tf_op jit(solution)/shard_map/ppermute | solution.py:486
  7.0 1.3 collective-permute-start.1
  8.3 14.0 %collective-permute-done.low = f32[11,32,256]{2,1,0:T(8,128)S(1)} collective-permute-done((f32[11,32,256]{2,1,0:T(8,128)S(1)}, f32[11,32,256]{2,1,0:T(8,128)S(1)}, u32[]{:S(2)}, u32[]{:S(2)}) %collective-permute-start) | collective-permute-done | bytes 360480 | tf_op jit(solution)/shard_map/ppermute | solution.py:486
  22.4 1.1 slice_dynamic-update-slice_fusion.2
  23.5 0.0 collective-permute-done.1.high
  23.6 1.1 slice_dynamic-update-slice_fusion.1
  24.7 1.0 slice_dynamic-update-slice_fusion
  25.7 1.3 collective-permute-start.2
  27.1 1.3 collective-permute-start.3
  28.4 0.0 collective-permute-done.2.left
  28.4 3.9 %collective-permute-done.3.right = f32[70,4,256]{2,1,0:T(4,128)S(1)} collective-permute-done((f32[70,4,256]{2,1,0:T(4,128)S(1)}, f32[70,4,256]{2,1,0:T(4,128)S(1)}, u32[]{:S(2)}, u32[]{:S(2)}) %collective-permute-start.3) | collective-permute-done | bytes 286752 | tf_op jit(solution)/shard_map/ppermute | solution.py:486
  32.3 0.7 copy-done.8
  33.0 16.1 %shard_map.37 = (f32[16,32,256]{2,1,0:T(8,128)}, f32[6,24,40,256]{3,2,1,0:T(8,128)}, f32[24,40,256]{2,1,0:T(8,128)}, f32[27,16,128]{2,1,0:T(8,128)}, f32[27,16,1...) custom-call(f32[16,32,256]{2,1,0:T(8,128)} %guess.1, f32[16,32,256]{2,1,0:T(8,128)} %source.1, ...), custom_call_target="tpu_custom_call" | custom-call | tf_op jit(solution)/shard_map/pallas_call | solution.py:468
  49.1 4.4 %collective-permute-start.4 = (f32[27,16,128]{2,1,0:T(8,128)}, f32[27,16,128]{2,1,0:T(8,128)S(1)}, u32[]{:S(2)}, u32[]{:S(2)}) collective-permute-start(f32[27,16,128]{2,1,0:T(8,128)} %get-tuple-element.20), channel_id=1, source_target_pairs={{0,4},{4,8},{8,12},{12,16},{16,20},{20,24},{24,28},{1,5},{5,9},{9,... | collective-permute-start | bytes 663560 | tf_op jit(solution)/shard_map/ppermute | solution.py:486
  53.5 1.3 collective-permute-start.5
  54.8 2.4 %collective-permute-done.4.low = f32[27,16,128]{2,1,0:T(8,128)S(1)} collective-permute-done((f32[27,16,128]{2,1,0:T(8,128)}, f32[27,16,128]{2,1,0:T(8,128)S(1)}, u32[]{:S(2)}, u32[]{:S(2)}) %collective-permute-start.4) | collective-permute-done | bytes 221216 | tf_op jit(solution)/shard_map/ppermute | solution.py:486
  57.2 4.3 %collective-permute-done.5.high = f32[27,16,128]{2,1,0:T(8,128)S(1)} collective-permute-done((f32[27,16,128]{2,1,0:T(8,128)}, f32[27,16,128]{2,1,0:T(8,128)S(1)}, u32[]{:S(2)}, u32[]{:S(2)}) %collective-permute-start.5) | collective-permute-done | bytes 221216 | tf_op jit(solution)/shard_map/ppermute | solution.py:486
  61.5 0.7 copy-done.2
  62.2 2.2 %shard_map.38 = (f32[68,8,128]{2,1,0:T(8,128)}, f32[68,8,128]{2,1,0:T(8,128)}) custom-call(f32[8,16,128]{2,1,0:T(8,128)} %get-tuple-element.18.b1, f32[8,16,128]{2,1,0:T(8,128)} %get-tuple-element.19.c1, f32[16,32,256]{2,1,0:T(8,128)} %get-tuple-element.22.v.v0, f32[27,16,128]{2,1,0:T(8,128)} %copy-done.1, f32[27,16,128]{2,1,0:T(8,128)} %copy-done.2), custom_call_target="tpu_custom_call" | custom-call | tf_op jit(solution)/shard_map/pallas_call | solution.py:468
  64.4 6.6 %collective-permute-start.6 = (f32[68,8,128]{2,1,0:T(8,128)}, f32[68,8,128]{2,1,0:T(8,128)S(1)}, u32[]{:S(2)}, u32[]{:S(2)}) collective-permute-start(f32[68,8,128]{2,1,0:T(8,128)} %get-tuple-element.23), channel_id=1, source_target_pairs={{0,1},{1,2},{2,3},{4,5},{5,6},{6,7},{8,9},{9,10},{10,11},{12,13},{... | collective-permute-start | bytes 835592 | tf_op jit(solution)/shard_map/ppermute | solution.py:486
  71.0 1.3 collective-permute-start.7
  72.3 0.1 collective-permute-done.6.left
  72.4 2.3 %collective-permute-done.7.right = f32[68,8,128]{2,1,0:T(8,128)S(1)} collective-permute-done((f32[68,8,128]{2,1,0:T(8,128)}, f32[68,8,128]{2,1,0:T(8,128)S(1)}, u32[]{:S(2)}, u32[]{:S(2)}) %collective-permute-start.7) | collective-permute-done | bytes 278560 | tf_op jit(solution)/shard_map/ppermute | solution.py:486
  74.7 0.7 copy-done.4
  75.4 8.5 %shard_map.39 = (f32[24,32,128]{2,1,0:T(8,128)}, f32[6,24,32,128]{3,2,1,0:T(8,128)}, f32[24,32,128]{2,1,0:T(8,128)}, f32[32,4,8,128]{3,2,1,0:T(8,128)}) custom-call(f32[8,16,128]{2,1,0:T(8,128)} %get-tuple-element.18.b1, f32[8,16,128]{2,1,0:T(8,128)} %get-tuple-element.19.c1, f32[27,16,128]{2,1,0:T(8,128)} %copy-done.1, f32[27,16,128]{2,1,0:T(8,128)} %copy-done.2, ...), custom_call_target="tpu_custom_call" | custom-call | tf_op jit(solution)/shard_map/pallas_call | solution.py:468
  83.8 8.7 %all-to-all-start = ((f32[32,4,8,128]{3,2,1,0:T(8,128)}), f32[32,4,8,128]{3,2,1,0:T(8,128)S(1)}, u32[]{:S(2)}, u32[]{:S(2)}) async-start(f32[32,4,8,128]{3,2,1,0:T(8,128)} %get-tuple-element.25), calls=%async_computation | async-start | bytes 1048576 | tf_op jit(solution)/shard_map/all_to_all | solution.py:531
  92.6 0.7 pad_add_fusion.place_ref
  93.3 14.9 %all-to-all-done.gathered = f32[32,4,8,128]{3,2,1,0:T(8,128)S(1)} async-done(((f32[32,4,8,128]{3,2,1,0:T(8,128)}), f32[32,4,8,128]{3,2,1,0:T(8,128)S(1)}, u32[]{:S(2)}, u32[]{:S(2)}) %all-to-all-start) | async-done | bytes 524320 | tf_op jit(solution)/shard_map/all_to_all | solution.py:531
  108.1 0.8 copy-done
  109.0 33.8 %shard_map.40 = f32[16,32,256]{2,1,0:T(8,128)} custom-call(s32[2]{0:T(128)} %pad_add_fusion.place_ref, f32[32,4,8,128]{3,2,1,0:T(8,128)} %copy-done, f32[24,32,128]{2,1,0:T(8,128)} %get-tuple-element.26.v1, f32[6,24,32,128]{3,2,1,0:T(8,128)} %get-tuple-element.27.w1, f32[24,32,128]{2,1,0:T(8,128)} %get-tuple-element.28.s1, ...), custom_call_target="tpu_custom_call" | custom-call | tf_op jit(solution)/shard_map/pallas_call | solution.py:468
  (22 shorter events, 0.2 us)
Async XLA Ops:
  2.1 20.2 %collective-permute-start = (f32[11,32,256]{2,1,0:T(8,128)S(1)}, f32[11,32,256]{2,1,0:T(8,128)S(1)}, u32[]{:S(2)}, u32[]{:S(2)}) collective-permute-start(f32[11,32,256]{2,1,0:T(8,128)S(1)} %pad_maximum_fusion), channel_id=1, source_target_pairs={{0,4},{4,8},{8,12},{12,16},{16,20},{20,24},{24,28},{1,5},{5,9},{9,... | collective-permute-start | bytes 1081352 | tf_op jit(solution)/shard_map/ppermute | solution.py:486
  7.0 16.5 %collective-permute-start.1 = (f32[11,32,256]{2,1,0:T(8,128)S(1)}, f32[11,32,256]{2,1,0:T(8,128)S(1)}, u32[]{:S(2)}, u32[]{:S(2)}) collective-permute-start(f32[11,32,256]{2,1,0:T(8,128)S(1)} %pad_maximum_fusion.1), channel_id=1, source_target_pairs={{4,0},{8,4},{12,8},{16,12},{20,16},{24,20},{28,24},{5,1},{9,5},{13... | collective-permute-start | bytes 1081352 | tf_op jit(solution)/shard_map/ppermute | solution.py:486
  22.4 9.9 %copy-start.5 = (f32[11,32,256]{2,1,0:T(8,128)}, f32[11,32,256]{2,1,0:T(8,128)S(1)}, u32[]{:S(2)}) copy-start(f32[11,32,256]{2,1,0:T(8,128)S(1)} %collective-permute-done.low) | copy-start | bytes 1081348
  23.5 8.7 %copy-start.6 = (f32[11,32,256]{2,1,0:T(8,128)}, f32[11,32,256]{2,1,0:T(8,128)S(1)}, u32[]{:S(2)}) copy-start(f32[11,32,256]{2,1,0:T(8,128)S(1)} %collective-permute-done.1.high) | copy-start | bytes 1081348
  25.7 2.6 %collective-permute-start.2 = (f32[70,4,256]{2,1,0:T(4,128)S(1)}, f32[70,4,256]{2,1,0:T(4,128)S(1)}, u32[]{:S(2)}, u32[]{:S(2)}) collective-permute-start(f32[70,4,256]{2,1,0:T(4,128)S(1)} %get-tuple-element.44), channel_id=1, source_target_pairs={{0,1},{1,2},{2,3},{4,5},{5,6},{6,7},{8,9},{9,10},{10,11},{12,13},{... | collective-permute-start | bytes 860168 | tf_op jit(solution)/shard_map/ppermute | solution.py:486
  27.1 5.2 %collective-permute-start.3 = (f32[70,4,256]{2,1,0:T(4,128)S(1)}, f32[70,4,256]{2,1,0:T(4,128)S(1)}, u32[]{:S(2)}, u32[]{:S(2)}) collective-permute-start(f32[70,4,256]{2,1,0:T(4,128)S(1)} %get-tuple-element.43), channel_id=1, source_target_pairs={{1,0},{2,1},{3,2},{5,4},{6,5},{7,6},{9,8},{10,9},{11,10},{13,12},{... | collective-permute-start | bytes 860168 | tf_op jit(solution)/shard_map/ppermute | solution.py:486
  28.4 3.9 %copy-start.7 = (f32[70,4,256]{2,1,0:T(4,128)}, f32[70,4,256]{2,1,0:T(4,128)S(1)}, u32[]{:S(2)}) copy-start(f32[70,4,256]{2,1,0:T(4,128)S(1)} %collective-permute-done.2.left) | copy-start | bytes 860164
  32.3 0.7 copy-start.8
  49.1 8.1 %collective-permute-start.4 = (f32[27,16,128]{2,1,0:T(8,128)}, f32[27,16,128]{2,1,0:T(8,128)S(1)}, u32[]{:S(2)}, u32[]{:S(2)}) collective-permute-start(f32[27,16,128]{2,1,0:T(8,128)} %get-tuple-element.20), channel_id=1, source_target_pairs={{0,4},{4,8},{8,12},{12,16},{16,20},{20,24},{24,28},{1,5},{5,9},{9,... | collective-permute-start | bytes 663560 | tf_op jit(solution)/shard_map/ppermute | solution.py:486
  53.5 8.0 %collective-permute-start.5 = (f32[27,16,128]{2,1,0:T(8,128)}, f32[27,16,128]{2,1,0:T(8,128)S(1)}, u32[]{:S(2)}, u32[]{:S(2)}) collective-permute-start(f32[27,16,128]{2,1,0:T(8,128)} %get-tuple-element.21), channel_id=1, source_target_pairs={{4,0},{8,4},{12,8},{16,12},{20,16},{24,20},{28,24},{5,1},{9,5},{13... | collective-permute-start | bytes 663560 | tf_op jit(solution)/shard_map/ppermute | solution.py:486
  57.2 4.3 %copy-start.1 = (f32[27,16,128]{2,1,0:T(8,128)}, f32[27,16,128]{2,1,0:T(8,128)S(1)}, u32[]{:S(2)}) copy-start(f32[27,16,128]{2,1,0:T(8,128)S(1)} %collective-permute-done.4.low) | copy-start | bytes 663556
  61.5 0.7 copy-start.2
  64.4 7.9 %collective-permute-start.6 = (f32[68,8,128]{2,1,0:T(8,128)}, f32[68,8,128]{2,1,0:T(8,128)S(1)}, u32[]{:S(2)}, u32[]{:S(2)}) collective-permute-start(f32[68,8,128]{2,1,0:T(8,128)} %get-tuple-element.23), channel_id=1, source_target_pairs={{0,1},{1,2},{2,3},{4,5},{5,6},{6,7},{8,9},{9,10},{10,11},{12,13},{... | collective-permute-start | bytes 835592 | tf_op jit(solution)/shard_map/ppermute | solution.py:486
  71.0 3.7 %collective-permute-start.7 = (f32[68,8,128]{2,1,0:T(8,128)}, f32[68,8,128]{2,1,0:T(8,128)S(1)}, u32[]{:S(2)}, u32[]{:S(2)}) collective-permute-start(f32[68,8,128]{2,1,0:T(8,128)} %get-tuple-element.24), channel_id=1, source_target_pairs={{1,0},{2,1},{3,2},{5,4},{6,5},{7,6},{9,8},{10,9},{11,10},{13,12},{... | collective-permute-start | bytes 835592 | tf_op jit(solution)/shard_map/ppermute | solution.py:486
  72.4 2.3 %copy-start.3 = (f32[68,8,128]{2,1,0:T(8,128)}, f32[68,8,128]{2,1,0:T(8,128)S(1)}, u32[]{:S(2)}) copy-start(f32[68,8,128]{2,1,0:T(8,128)S(1)} %collective-permute-done.6.left) | copy-start | bytes 835588
  74.7 0.7 copy-start.4
  83.8 24.3 %all-to-all-start = ((f32[32,4,8,128]{3,2,1,0:T(8,128)}), f32[32,4,8,128]{3,2,1,0:T(8,128)S(1)}, u32[]{:S(2)}, u32[]{:S(2)}) async-start(f32[32,4,8,128]{3,2,1,0:T(8,128)} %get-tuple-element.25), calls=%async_computation | async-start | bytes 1048576 | tf_op jit(solution)/shard_map/all_to_all | solution.py:531
  108.1 0.8 copy-start

commit v2 on v1

v2 whole, which is shorter than its diff:
```python
from functools import partial

import jax
import jax.numpy as jnp
from jax import lax
from jax.experimental import pallas as pl
from jax.experimental.pallas import tpu as pltpu
from jax.sharding import PartitionSpec as P

LEVELS = 4
SWEEPS = 3
CHEB = 8

RELAX_WEIGHT = 0.7
CHEBY_LOWER = 0.08
CHEBY_UPPER = 2.0

F32 = jnp.float32
LANES = 128
FINE = SWEEPS + 1
COARSE = 8
SOURCE = COARSE - 1
POST = SWEEPS
BLOCK = 24
VMEM_LIMIT = 56 * 1024 * 1024


def dot(a, b):
    return jnp.dot(a, b, precision=lax.Precision.HIGHEST, preferred_element_type=F32)


def iota(shape, dim):
    return lax.broadcasted_iota(jnp.int32, shape, dim)


def vmem(*shape):
    return pltpu.VMEM(shape, F32)


def roll(x, by, axis):
    return pltpu.roll(x, by % x.shape[axis], axis)


def planes(first, last, step):
    if last - first <= BLOCK:
        for p in range(first, last):
            step(p)
    else:
        lax.fori_loop(first, last, lambda p, carry: (step(p), carry)[1], 0, unroll=4)


def lane_before(x, t, lane):
    moved = roll(x[t], 1, 1)
    return moved if len(x) == 1 else jnp.where(lane == 0, roll(x[t - 1], 1, 1), moved)


def lane_after(x, t, lane):
    moved = roll(x[t], -1, 1)
    return moved if len(x) == 1 else jnp.where(lane == LANES - 1, roll(x[(t + 1) % len(x)], -1, 1), moved)


def weigh(fetch, source, level, first, last, depth, row_edges, scale, omega):
    wx, wy, wz, gain, scaled, total = level
    count, pieces = wy.shape[1:3]
    lane = iota((8, LANES), 1)
    front, back = lane % depth == 0, lane % depth == depth - 1
    top, bottom = iota((8, LANES), 0) == 0, iota((8, LANES), 0) == 7

    def step(p):
        for j in range(count):
            c = [fetch(p, j, t) for t in range(pieces)]
            for t in range(pieces):
                x = c[t]
                lower, upper = fetch(p - 1, j, t), fetch(p + 1, j, t)
                left = fetch(p, j - 1, t) if j else roll(fetch(p, count - 1, t), 1, 0)
                right = fetch(p, j + 1, t) if j < count - 1 else roll(fetch(p, 0, t), -1, 0)
                if row_edges and j == 0:
                    left = jnp.where(top, 0.0, left)
                if row_edges and j == count - 1:
                    right = jnp.where(bottom, 0.0, right)
                near, far = lane_before(c, t, lane), lane_after(c, t, lane)
                if t == 0:
                    near = jnp.where(front, 0.0, near)
                if t == pieces - 1:
                    far = jnp.where(back, 0.0, far)
                below, beside, before = x + lower, x + left, x + near
                s = (below + beside + before) + (3.0 * x + (upper + right + far))
                wx[p, j, t] = below
                if last is not None:
                    wx[p + 1, j, t] = x + upper
                wy[p, j, t] = jnp.where(top, 0.0, beside) if row_edges and j == 0 else beside
                wz[p, j, t] = jnp.where(front, 0.0, before) if t == 0 else before
                gain[p, j, t] = jnp.where(x > 0.0, omega / s, 0.0)
                scaled[p, j, t] = source(p, j, t) * (2.0 / scale)
                if total is not None:
                    total[p, j, t] = s

    planes(first, last, step)


def around(fetch, level, p, finish):
    wx, wy, wz = level[:3]
    count, pieces = wy.shape[1:3]
    lane = iota((8, LANES), 1)
    v = [[fetch(p, j, t) for t in range(pieces)] for j in range(count)]
    beside = [wy[p, 0, t] for t in range(pieces)]
    wrap = [roll(beside[t] * v[0][t], -1, 0) for t in range(pieces)]
    for j in range(count):
        ahead = [wy[p, j + 1, t] for t in range(pieces)] if j < count - 1 else None
        before = [wz[p, j, t] for t in range(pieces)]
        flow = [before[t] * v[j][t] for t in range(pieces)]
        for t in range(pieces):
            total = wx[p, j, t] * fetch(p - 1, j, t) + wx[p + 1, j, t] * fetch(p + 1, j, t)
            total += beside[t] * (v[j - 1][t] if j else roll(v[count - 1][t], 1, 0))
            total += ahead[t] * v[j + 1][t] if j < count - 1 else wrap[t]
            total += before[t] * lane_before(v[j], t, lane) + lane_after(flow, t, lane)
            finish(j, t, v[j][t], total)
        beside = ahead


def reader(ref):
    return lambda p, j, t: ref[p, j, t]


def sweep(fetch, out, level, first, last):
    gain, scaled = level[3:5]

    def step(p):
        def finish(j, t, v, total):
            out[p, j, t] = (1.0 - RELAX_WEIGHT) * v + gain[p, j, t] * (scaled[p, j, t] + total)

        around(fetch, level, p, finish)

    planes(first, last, step)


def start(out, level, first, last):
    gain, scaled = level[3:5]

    def step(p):
        for j in range(out.shape[1]):
            for t in range(out.shape[2]):
                out[p, j, t] = gain[p, j, t] * scaled[p, j, t]

    planes(first, last, step)


def residual(fetch, level, p):
    scaled, total = level[4:6]
    found = {}

    def finish(j, t, v, near):
        found[j, t] = (scaled[p, j, t] + near) - v * total[p, j, t]

    around(fetch, level, p, finish)
    return found


def halve_lanes(lanes, width, value, offset=0):
    return jnp.where(iota((lanes, width), 0) // 2 + offset == iota((lanes, width), 1), value, 0.0).astype(F32)


def even_odd(ref, count):
    return ref[pl.ds(0, count, stride=2), :] + ref[pl.ds(1, count, stride=2), :]


def fine_pre_kernel(guess, source, coef, low, high, left, right,
                    out, wx, wy, wz, gain, scaled, up, down, b1, c1,
                    field, force, c, v, w, total, *pairs):
    nx, ny, nz = guess.shape
    pieces = nz // LANES
    rows = ny + 2 * FINE
    count = rows // 8
    planes0 = nx + 2 * FINE
    level = (wx, wy, wz, gain, scaled, total)

    def fill(target, own, base, width):
        at = FINE - width
        offset = sum(nx + 2 * k for k in base)
        message = sum(base)

        def rest(k):
            side = jnp.concatenate((right[offset + k], left[offset + k]), 0)
            for t in range(pieces):
                target[at + k, t, ny:] = side[:, t * LANES:(t + 1) * LANES]

        planes(0, nx + 2 * width, rest)

        def main(k):
            for t in range(pieces):
                target[FINE + k, t, :ny] = own[k, :, t * LANES:(t + 1) * LANES]

        planes(0, nx, main)
        for k in range(width):
            for t in range(pieces):
                lanes = slice(t * LANES, (t + 1) * LANES)
                target[at + k, t, :ny] = low[message + k, :, lanes]
                target[FINE + nx + k, t, :ny] = high[message + k, :, lanes]

    def spaced(ref):
        return lambda p, j, t: ref[p, t, pl.ds(j, 8, stride=count), :]

    fill(field, guess, (), FINE)
    fill(force, source, (FINE,), FINE - 1)
    fill(c, coef, (FINE, FINE - 1), FINE)
    def arrange(p):
        for j in range(count):
            for t in range(pieces):
                w[p, j, t] = spaced(c)(p, j, t)

    planes(0, planes0, arrange)
    weigh(reader(w), spaced(force), level, 1, planes0 - 1, LANES, False, 1.0, RELAX_WEIGHT)

    def arrange_field(p):
        for j in range(count):
            for t in range(pieces):
                v[p, j, t] = spaced(field)(p, j, t)

    planes(0, planes0, arrange_field)
    sweep(reader(v), w, level, 1, planes0 - 1)
    sweep(reader(w), v, level, 2, planes0 - 2)
    sweep(reader(v), w, level, 3, planes0 - 3)

    def put(k):
        for t in range(pieces):
            for j in range(count):
                field[k, t, pl.ds(j, 8, stride=count), :] = w[FINE + k, j, t]
            out[k, :, t * LANES:(t + 1) * LANES] = field[k, t, :ny]

    planes(0, nx, put)

    n1, r1 = nx // 2, ny // 2

    def coarsen(value):
        wide = jnp.concatenate(
            [jnp.concatenate([even_odd(pairs[t].at[pl.ds(q * rows, ny)], r1) for t in range(pieces)], 1) for q in range(n1)], 0
        )
        return dot(wide, halve_lanes(nz, nz // 2, value)).reshape(n1, r1, nz // 2)

    def halve(q):
        one, two = (residual(reader(w), level, FINE + 2 * q + k) for k in range(2))
        for j in range(count):
            for t in range(pieces):
                pairs[t][pl.ds(q * rows + j, 8, stride=count), :] = one[j, t] + two[j, t]

    planes(0, n1, halve)
    b1[...] = coarsen(0.125 * 0.5)
    for q in range(n1):
        for t in range(pieces):
            lanes = slice(t * LANES, (t + 1) * LANES)
            pairs[t][q * rows:q * rows + ny, :] = coef[2 * q, :, lanes] + coef[2 * q + 1, :, lanes]
    c1[...] = coarsen(0.125)

    up[:SOURCE] = b1[n1 - SOURCE:]
    down[:SOURCE] = b1[:SOURCE]
    up[SOURCE:SOURCE + COARSE] = c1[n1 - COARSE:]
    down[SOURCE:SOURCE + COARSE] = c1[:COARSE]
    at = SOURCE + COARSE
    for k in range(POST):
        for i in range(2):
            for j in range(2):
                here, lanes = pl.ds(i * r1, r1), pl.ds(j * (nz // 2), nz // 2)
                up[at] = out[nx - POST + k, here, lanes]
                down[at] = out[k, here, lanes]
                at += 1


def rows_kernel(b1, c1, v, low, high, up, down):
    n1, r1, half = b1.shape
    nx, ny = 2 * n1, 2 * r1

    def edge(take, at):
        up[at] = take(r1 - COARSE, COARSE)
        down[at] = take(0, COARSE)

    at = 0
    for k in range(SOURCE):
        edge(lambda s, n: low[k, pl.ds(s, n), :], at)
        edge(lambda s, n: high[k, pl.ds(s, n), :], at + SOURCE + n1)
        at += 1
    for k in range(n1):
        edge(lambda s, n: b1[k, pl.ds(s, n), :], at)
        at += 1
    at += SOURCE
    for k in range(COARSE):
        edge(lambda s, n: low[SOURCE + k, pl.ds(s, n), :], at)
        edge(lambda s, n: high[SOURCE + k, pl.ds(s, n), :], at + COARSE + n1)
        at += 1
    for k in range(n1):
        edge(lambda s, n: c1[k, pl.ds(s, n), :], at)
        at += 1
    at += COARSE
    base = SOURCE + COARSE
    for k in range(POST):
        for j in range(2):
            rows = pl.ds(j * FINE, FINE)
            up[at, rows, :] = low[base + 4 * k + 2 + j, r1 - FINE:, :]
            down[at, rows, :] = low[base + 4 * k + j, :FINE, :]
            up[at + POST + nx, rows, :] = high[base + 4 * k + 2 + j, r1 - FINE:, :]
            down[at + POST + nx, rows, :] = high[base + 4 * k + j, :FINE, :]
        at += 1

    def own(k):
        for j in range(2):
            rows, lanes = pl.ds(j * FINE, FINE), pl.ds(j * half, half)
            up[at + k, rows, :] = v[k, ny - FINE:, lanes]
            down[at + k, rows, :] = v[k, :FINE, lanes]

    planes(0, nx, own)


def coarse_pre_kernel(b1, c1, low, high, left, right,
                      v, wx, wy, wz, gain, scaled, send, field, c, w, total, upper, lower):
    n1, r1, lanes = b1.shape
    rows = r1 + 2 * COARSE
    count = rows // 8
    planes1 = n1 + 2 * COARSE
    scale = 0.25
    level = (wx, wy, wz, gain, scaled, total)

    def fill(target, own, base, offset, width):
        at = COARSE - width
        for k in range(n1 + 2 * width):
            target[at + k, r1:r1 + COARSE] = right[offset + k]
            target[at + k, r1 + COARSE:] = left[offset + k]
        for k in range(n1):
            target[COARSE + k, :r1] = own[k]
        for k in range(width):
            target[at + k, :r1] = low[base + k]
            target[COARSE + n1 + k, :r1] = high[base + k]

    def spaced(ref):
        return lambda p, j, t: ref[p, pl.ds(j, 8, stride=count), :]

    fill(field, b1, 0, 0, SOURCE)
    fill(c, c1, SOURCE, n1 + 2 * SOURCE, COARSE)
    for p in range(planes1):
        for j in range(count):
            w[p, j, 0] = spaced(c)(p, j, 0)
    weigh(reader(w), spaced(field), level, 1, planes1 - 1, lanes, False, scale, RELAX_WEIGHT)
    start(v, level, 1, planes1 - 1)
    sweep(reader(v), w, level, 2, planes1 - 2)
    sweep(reader(w), v, level, 3, planes1 - 3)

    n2, r2 = n1 // 2, r1 // 2
    half = n2 // 2

    def coarsen(value):
        matrix = jnp.concatenate((halve_lanes(lanes, LANES, value), halve_lanes(lanes, LANES, value, lanes // 2)), 0)
        return dot(jnp.concatenate((lower[...], upper[...]), 1), matrix).reshape(half, r2, LANES)

    for q in range(n2):
        one, two = (residual(reader(v), level, COARSE + 2 * q + k) for k in range(2))
        target = lower if q < half else upper
        for j in range(count // 2):
            value = (one[2 * j, 0] + two[2 * j, 0]) + (one[2 * j + 1, 0] + two[2 * j + 1, 0])
            target[pl.ds(q % half * r2 + j, r1 // count, stride=count // 2), :] = value[:r1 // count]
    b2 = coarsen(0.125 * 0.5 * scale)
    for q in range(n2):
        target = lower if q < half else upper
        field[q, :r1] = c1[2 * q] + c1[2 * q + 1]
        target[q % half * r2:(q % half + 1) * r2, :] = even_odd(field.at[q], r2)
    c2 = coarsen(0.125)
    for d in range(send.shape[0]):
        send[d, :half] = b2
        send[d, half:] = c2


def pads(ref, depth):
    last = ref.shape[0] - 1
    for j in range(ref.shape[1]):
        ref[0, j, 0] = roll(ref[last - 1, j, 0], depth, 1)
        ref[last, j, 0] = roll(ref[1, j, 0], -depth, 1)


def regroup(depth):
    source, target = iota((2 * LANES, LANES), 0), iota((2 * LANES, LANES), 1)
    group, lane = source // LANES, source % LANES
    block, z = lane // depth, lane % depth
    return (2 * block + group) * (depth // 2) + z // 2 == target


def solve_kernel(place_ref, gathered, v1, wx1, wy1, wz1, gain1, scaled1, v0, wx0, wy0, wz0, gain0, scaled0,
                 low, high, left, right, out,
                 c2, a2, y2, n2, l2x, l2y, l2z, l2g, l2s, l2t,
                 c3, b3, a3, y3, l3x, l3y, l3z, l3g, l3s, l3t,
                 c4, b4, y4, l4x, l4y, l4z, l4g, l4s,
                 u1, t1, e1, field, u0, t0, double, *, gx, gy):
    level2 = (l2x, l2y, l2z, l2g, l2s, l2t)
    level3 = (l3x, l3y, l3z, l3g, l3s, l3t)
    level4 = (l4x, l4y, l4z, l4g, l4s, None)
    half = gathered.shape[1] // 2
    r2 = gathered.shape[2]
    per = 2 * half
    m2, m3, m4 = c2.shape[0] - 2, c3.shape[0] - 2, c4.shape[0] - 2
    j2, j3, j4 = c2.shape[1], c3.shape[1], c4.shape[1]
    rows2 = 8 * j2
    depth2 = LANES // 2
    depth3, depth4 = depth2 // 2, depth2 // 4
    lane = iota((8, LANES), 1)

    def unpack(i):
        for j in range(gy):
            for k in range(half):
                for which in range(2):
                    one = gathered[i * gy + j, which * half + k]
                    two = gathered[(i + gx // 2) * gy + j, which * half + k]
                    here = pl.ds(j * r2, r2)
                    n2[which, i * per + k, here, :] = jnp.where(lane < depth2, one, roll(two, depth2, 1))
                    n2[which, i * per + half + k, here, :] = jnp.where(lane < depth2, roll(one, depth2, 1), two)

    planes(0, gx // 2, unpack)

    def spread(p):
        for j in range(j2):
            c2[1 + p, j, 0] = n2[1, p, pl.ds(j, 8, stride=j2), :]

    planes(0, m2, spread)

    def level_in(c, source, level, depth, scale, omega):
        last = c.shape[0] - 1
        lane = iota((8, LANES), 1)
        for j in range(c.shape[1]):
            c[0, j, 0] = jnp.where(lane < depth, 0.0, roll(c[last - 1, j, 0], depth, 1))
            c[last, j, 0] = jnp.where(lane >= LANES - depth, 0.0, roll(c[1, j, 0], -depth, 1))
        weigh(reader(c), source, level, 1, last, depth, True, scale, omega)
        wx = level[0]
        for j in range(c.shape[1]):
            wx[1, j, 0] = jnp.where(lane < depth, 0.0, wx[1, j, 0])
            wx[last, j, 0] = jnp.where(lane >= LANES - depth, 0.0, wx[last, j, 0])

    def smooth(first, other, level, depth, sweeps):
        for _ in range(sweeps):
            pads(first, depth)
            sweep(reader(first), other, level, 1, first.shape[0] - 1)
            first, other = other, first
        return first, other

    def down(fetch, count, rows, depth, out, value):
        def pair(m, g):
            at = g * (count // 2) + 2 * m + 1
            one, two = fetch(at), fetch(at + 1)
            return [(one[2 * j] + two[2 * j]) + (one[2 * j + 1] + two[2 * j + 1]) for j in range(rows // 2)]

        parts = [jnp.concatenate(both, 1) for m in range(count // 4) for both in zip(pair(m, 0), pair(m, 1))]
        matrix = jnp.where(regroup(depth), value, 0.0).astype(F32)
        found = dot(jnp.concatenate(parts, 0), matrix)
        at = 0
        for m in range(count // 4):
            for j in range(rows // 2):
                out[1 + m, j, 0] = found[at:at + 8]
                at += 8

    def up(coarse, fine, depth):
        count, rows = fine.shape[0] - 2, fine.shape[1]
        matrix = jnp.where(regroup(depth), 1.0, 0.0).astype(F32)
        x = jnp.concatenate([coarse[1 + m, j, 0] for m in range(count // 4) for j in range(rows // 2)], 0)
        x = lax.dot_general(x, matrix, (((1,), (1,)), ((), ())), precision=lax.Precision.HIGHEST,
                            preferred_element_type=F32)
        at = 0
        for m in range(count // 4):
            for j in range(rows // 2):
                for g in range(2):
                    value = x[at:at + 8, g * LANES:(g + 1) * LANES]
                    for k in range(2):
                        p = g * (count // 2) + 2 * m + 1 + k
                        for i in range(2):
                            fine[p, 2 * j + i, 0] = fine[p, 2 * j + i, 0] + value
                at += 8

    def rest(field, level):
        return lambda p: [value for _, value in sorted(residual(reader(field), level, p).items())]

    def whole(ref):
        return lambda p: [ref[p, j, 0] for j in range(ref.shape[1])]

    level_in(c2, lambda p, j, t: n2[0, p - 1, pl.ds(j, 8, stride=j2), :], level2, depth2, 0.25**2, RELAX_WEIGHT)
    start(a2, level2, 1, m2 + 1)
    x2, z2 = smooth(a2, y2, level2, depth2, SWEEPS - 1)
    pads(x2, depth2)
    down(whole(c2), m2, j2, depth2, c3, 0.125)
    down(rest(x2, level2), m2, j2, depth2, b3, 0.125 * 0.5 * 0.25**2)

    level_in(c3, reader(b3), level3, depth3, 0.25**3, RELAX_WEIGHT)
    start(a3, level3, 1, m3 + 1)
    x3, z3 = smooth(a3, y3, level3, depth3, SWEEPS - 1)
    pads(x3, depth3)
    down(whole(c3), m3, j3, depth3, c4, 0.125)
    down(rest(x3, level3), m3, j3, depth3, b4, 0.125 * 0.5 * 0.25**3)

    level_in(c4, reader(b4), level4, depth4, 0.25**4, 1.0)
    theta, delta = (CHEBY_UPPER + CHEBY_LOWER) / 2.0, (CHEBY_UPPER - CHEBY_LOWER) / 2.0
    sigma = theta / delta
    rho = 1.0 / sigma
    cells = [(1 + p, j) for p in range(m4) for j in range(j4)]
    res = {at: l4g[at[0], at[1], 0] * l4s[at[0], at[1], 0] for at in cells}
    direction = {at: res[at] / theta for at in cells}
    total = {at: jnp.zeros((8, LANES), F32) for at in cells}
    for _ in range(CHEB):
        for p, j in cells:
            total[p, j] = total[p, j] + direction[p, j]
            y4[p, j, 0] = direction[p, j]
        pads(y4, depth4)
        for p in range(1, m4 + 1):
            def finish(j, t, v, near):
                res[p, j] = res[p, j] - (v - l4g[p, j, 0] * near)

            around(reader(y4), level4, p, finish)
        rho_new = 1.0 / (2.0 * sigma - rho)
        direction = {at: rho_new * rho * direction[at] + (2.0 * rho_new / delta) * res[at] for at in cells}
        rho = rho_new
    for p, j in cells:
        b4[p, j, 0] = total[p, j]

    up(b4, x3, depth3)
    x3, z3 = smooth(x3, z3, level3, depth3, SWEEPS)
    up(x3, x2, depth2)
    x2, z2 = smooth(x2, z2, level2, depth2, SWEEPS)

    level1 = (wx1, wy1, wz1, gain1, scaled1, None)
    at_x, at_y = place_ref[0], place_ref[1]
    planes1, count1, _, _, lanes1 = v1.shape
    n1, r1 = planes1 - 2 * COARSE, 8 * count1 - 2 * COARSE
    sub = iota((8, LANES), 0)
    reach = SWEEPS + 2
    first, last = -((reach + 1) // 2), (n1 + reach + 1) // 2
    pad = rows2 + 8
    e1[0, :8] = jnp.zeros((8, LANES), F32)
    e1[0, pad:] = jnp.zeros((8, LANES), F32)
    window = []
    for t in range(first, last):
        x = at_x * per + t
        inside = (x >= 0) & (x < gx * per)
        x = jnp.clip(x, 0, gx * per - 1)
        block = x // m2
        slot = t - first
        for j in range(j2):
            value = x2[1 + x - block * m2, j, 0]
            value = jnp.where(block == 0, value, roll(value, depth2, 1))
            e1[0, pl.ds(8 + j, 8, stride=j2), :] = jnp.where(inside, value, 0.0)
        base = pl.multiple_of(at_y * r2, 8)
        above, here, after = (e1[0, pl.ds(base + 8 * k, 8), :] for k in range(3))
        t1[slot, 0, 0] = here
        t1[slot, 1, 0] = jnp.where(sub < 4, after, above)
    wide = jnp.concatenate([t1[slot, k, 0] for slot in range(last - first) for k in range(2)], 0)
    matrix = jnp.where(iota((LANES, lanes1), 0) == iota((LANES, lanes1), 1) // 2, 1.0, 0.0).astype(F32)
    double[0, :wide.shape[0]] = dot(wide, matrix)
    for t in range(first, last):
        part = [double[0, pl.ds(16 * (t - first) + j, 8, stride=2), :] for j in range(2)]
        for k in range(2):
            p = COARSE + 2 * t + k
            for j in range(count1):
                u1[p, j, 0] = v1[p, j, 0] + part[j // 2]
    sweep(reader(u1), t1, level1, COARSE - 4, COARSE + n1 + 4)
    sweep(reader(t1), u1, level1, COARSE - 3, COARSE + n1 + 3)
    sweep(reader(u1), t1, level1, COARSE - 2, COARSE + n1 + 2)

    level0 = (wx0, wy0, wz0, gain0, scaled0, None)
    nx, ny, nz = v0.shape
    pieces = nz // LANES
    rows0 = ny + 2 * FINE
    count0 = rows0 // 8

    wide = []
    for k in range(n1 + 4):
        for j in range(count1):
            e1[k, pl.ds(j, 8, stride=count1), :] = t1[COARSE - 2 + k, j, 0]
        wide.append(e1[k, :r1])
        wide.append(jnp.where(sub < 2, e1[k, r1:r1 + 8], roll(e1[k, r1 + 8:r1 + 16], 4, 0)))
    matrix = jnp.where(iota((lanes1, nz), 0) == iota((lanes1, nz), 1) // 2, 1.0, 0.0).astype(F32)
    wide = dot(jnp.concatenate(wide, 0), matrix)
    base = SOURCE + COARSE
    beyond = 2 * n1 + 2 * SOURCE + 2 * COARSE
    for k in range(n1 + 4):
        at = k * (r1 + 8)
        for t in range(pieces):
            lanes = slice(t * LANES, (t + 1) * LANES)
            for i in range(2):
                double[t, pl.ds(i, r1, stride=2), :] = wide[at:at + r1, lanes]
                double[t, pl.ds(ny + i, 4, stride=2), :] = wide[at + r1:at + r1 + 4, lanes]
            value = double[t, :rows0]
            for i in range(2):
                p = 2 * k + i
                q = p - FINE
                if p < FINE - POST or q >= nx + POST:
                    continue
                if 0 <= q < nx:
                    own = v0[q, :, lanes]
                else:
                    message, slot = (low, p - (FINE - POST)) if q < 0 else (high, q - nx)
                    own = jnp.concatenate([message[base + 4 * slot + 2 * h + t] for h in range(2)], 0)
                side = pl.ds(t * FINE, FINE)
                at_side = beyond + p - (FINE - POST)
                side = jnp.concatenate((right[at_side, side, :], left[at_side, side, :]), 0)
                field[p, t, :ny] = own + value[:ny]
                field[p, t, ny:] = side + value[ny:]

    def arrange(p):
        for j in range(count0):
            for t in range(pieces):
                u0[p, j, t] = field[p, t, pl.ds(j, 8, stride=count0), :]

    planes(FINE - POST, FINE + nx + POST, arrange)
    sweep(reader(u0), t0, level0, FINE - 2, FINE + nx + 2)
    sweep(reader(t0), u0, level0, FINE - 1, FINE + nx + 1)
    sweep(reader(u0), t0, level0, FINE, FINE + nx)

    def put(k):
        for t in range(pieces):
            for j in range(count0):
                field[k, t, pl.ds(j, 8, stride=count0), :] = t0[FINE + k, j, t]
            out[k, :, t * LANES:(t + 1) * LANES] = field[k, t, :ny]

    planes(0, nx, put)


def call(kernel, outs, scratch, *args, scalars=0):
    specs = [pl.BlockSpec(memory_space=pltpu.SMEM if k < scalars else pltpu.VMEM) for k in range(len(args))]
    return pl.pallas_call(
        kernel,
        out_shape=outs,
        in_specs=specs,
        out_specs=[pl.BlockSpec(memory_space=pltpu.VMEM) for _ in outs],
        scratch_shapes=scratch,
        compiler_params=pltpu.CompilerParams(vmem_limit_bytes=VMEM_LIMIT),
    )(*args)


def shape(*dims):
    return jax.ShapeDtypeStruct(dims, F32)


def exchange(up, down, axis):
    count = lax.axis_size(axis)
    forward = [(i, i + 1) for i in range(count - 1)]
    backward = [(target, source) for source, target in forward]
    return lax.ppermute(up, axis, forward), lax.ppermute(down, axis, backward)


def body(guess, right_side, coefficient):
    gx, gy = lax.axis_size("gx"), lax.axis_size("gy")
    nx, ny, nz = guess.shape
    fields = ((guess, FINE), (right_side, FINE - 1), (coefficient, FINE))
    low, high = exchange(
        jnp.concatenate([f[nx - k:] for f, k in fields], 0), jnp.concatenate([f[:k] for f, k in fields], 0), "gx"
    )

    def rows(cut):
        parts, at = [], 0
        for f, k in fields:
            parts += [cut(low[at:at + k]), cut(f), cut(high[at:at + k])]
            at += k
        return jnp.concatenate(parts, 0)

    left, right = exchange(rows(lambda f: f[:, ny - FINE:]), rows(lambda f: f[:, :FINE]), "gy")

    planes0, rows0, pieces = nx + 2 * FINE, ny + 2 * FINE, nz // LANES
    block0 = (planes0, rows0 // 8, pieces, 8, LANES)
    plain0 = (planes0, pieces, rows0, LANES)
    n1, r1, z1 = nx // 2, ny // 2, nz // 2
    message = (SOURCE + COARSE + 4 * POST, r1, z1)
    v0, *level0, up, down, b1, c1 = call(
        fine_pre_kernel,
        (shape(nx, ny, nz),) + (shape(*block0),) * 5 + (shape(*message),) * 2 + (shape(n1, r1, z1),) * 2,
        [vmem(*plain0)] * 3 + [vmem(*block0)] * 3 + [vmem(n1 * rows0, LANES)] * pieces,
        guess, right_side, coefficient, low, high, left, right,
    )
    low, high = exchange(up, down, "gx")
    count = 3 * n1 + 2 * SOURCE + 2 * COARSE + 2 * POST + n1
    up, down = call(rows_kernel, (shape(count, COARSE, z1),) * 2, (), b1, c1, v0, low, high)
    left, right = exchange(up, down, "gy")

    planes1, rows1 = n1 + 2 * COARSE, r1 + 2 * COARSE
    block1 = (planes1, rows1 // 8, 1, 8, z1)
    plain1 = (planes1, rows1, z1)
    n2, r2 = n1 // 2, r1 // 2
    v1, *level1, send = call(
        coarse_pre_kernel,
        (shape(*block1),) * 6 + (shape(gx * gy, n2, r2, LANES),),
        [vmem(*plain1)] * 2 + [vmem(*block1)] * 2 + [vmem(n2 // 2 * r2, LANES)] * 2,
        b1, c1, low, high, left, right,
    )
    gathered = lax.all_to_all(send, ("gx", "gy"), 0, 0)
    place_at = jnp.stack((lax.axis_index("gx"), lax.axis_index("gy"))).astype(jnp.int32)

    m2, rows2 = gx * n2 // 2, gy * r2
    m3, m4 = m2 // 4, m2 // 16
    block2, block3, block4 = ((m + 2, rows2 // part, 1, 8, LANES) for m, part in ((m2, 8), (m3, 16), (m4, 32)))
    scratch = (
        [vmem(*block2)] * 3 + [vmem(2, m2, rows2, LANES)] + [vmem(*block2)] * 6
        + [vmem(*block3)] * 10 + [vmem(*block4)] * 8
        + [vmem(*block1)] * 2 + [vmem(planes1, max(rows2 + 16, rows1), z1)]
        + [vmem(*plain0)] + [vmem(*block0)] * 2 + [vmem(pieces, 256, LANES)]
    )
    (out,) = call(
        partial(solve_kernel, gx=gx, gy=gy), (shape(nx, ny, nz),), scratch,
        place_at, gathered, v1, *level1, v0, *level0, low, high, left, right, scalars=1,
    )
    return out


def solution(mesh):
    return jax.shard_map(
        body,
        mesh=mesh,
        in_specs=(P("gx", "gy", None), P("gx", "gy", None), P("gx", "gy", None)),
        out_specs=P("gx", "gy", None),
        check_vma=False,
    )
```

time: 143 us -> 104 us (0.73)
  Pallas kernels: 60.5 us -> 21.7 us
    pallas_call x4, Pallas kernels: 60.5 us -> 21.7 us  [call(): pl.pallas_call(kernel, out_shape=outs, in_specs=specs, out_specs=[pl.Bloc...]
  transfers between devices with their start and end apart: 9 -> 9, of which waited for: 7 -> 7; matrix products, arithmetic and copies ran while one was open for 1% -> 2% of each run, Pallas kernels for 0% -> 0%
where the time goes in v2:
time: 104 us
  waiting for transfers between devices  41.9 us (40%)
  starting transfers between devices  31 us (30%)
  Pallas kernels  21.7 us (21%)
  local copies, waits for them, and re-layouts  8.4 us (8%)
    ppermute x8, waiting for transfers between devices, exchange(): return (lax.ppermute(up, axis, forward), lax.ppermute(down, axis, backward))  27 us
    ppermute x8, starting transfers between devices, exchange(): return (lax.ppermute(up, axis, forward), lax.ppermute(down, axis, backward))  22.3 us
    pallas_call x4, Pallas kernels, call(): pl.pallas_call(kernel, out_shape=outs, in_specs=specs, out_specs=[pl.Bloc...  21.7 us
    all_to_all x1, waiting for transfers between devices, body(): gathered = lax.all_to_all(send, ('gx', 'gy'), 0, 0)  14.9 us
    all_to_all x1, starting transfers between devices, body(): gathered = lax.all_to_all(send, ('gx', 'gy'), 0, 0)  8.76 us
    unnamed x26, local copies, waits for them, and re-layouts  6.29 us
    slice x2, local copies, waits for them, and re-layouts, body(): f[:k]  2.09 us
  transfers between devices with their start and end apart: 9, of which 7 were waited for; matrix products, arithmetic and copies ran while one was open for 2% of the time, Pallas kernels for 0%

profile of v2, /device:TPU:0, one launch (start us, length us, event | category | flops | bytes accessed | tf_op | source)
XLA Modules:
  0.0 103.9 jit_solution(16537458457911900072)
XLA Ops:
  0.0 1.0 fusion.1
  1.0 1.1 %fusion = (f32[4,32,256]{2,1,0:T(8,128)S(1)}, f32[4,32,256]{2,1,0:T(8,128)S(1)}, f32[4,32,256]{2,1,0:T(8,128)S(1)}, f32[4,32,256]{2,1,0:T(8,128)S(1)}) fusion(f32[16,32,256]{2,1,0:T(8,128)} %guess.1, f32[16,32,256]{2,1,0:T(8,128)} %coef.1), kind=kLoop, calls=%fused_computation.21 | loop fusion | bytes 1048576 | tf_op jit(solution)/shard_map/slice | solution.py:645
  2.1 4.9 %collective-permute-start = (f32[11,32,256]{2,1,0:T(8,128)S(1)}, f32[11,32,256]{2,1,0:T(8,128)S(1)}, u32[]{:S(2)}, u32[]{:S(2)}) collective-permute-start(f32[11,32,256]{2,1,0:T(8,128)S(1)} %pad_maximum_fusion), channel_id=1, source_target_pairs={{0,4},{4,8},{8,12},{12,16},{16,20},{20,24},{24,28},{1,5},{5,9},{9,... | collective-permute-start | bytes 1081352 | tf_op jit(solution)/shard_map/ppermute | solution.py:637
  7.0 1.3 %collective-permute-start.1 = (f32[11,32,256]{2,1,0:T(8,128)S(1)}, f32[11,32,256]{2,1,0:T(8,128)S(1)}, u32[]{:S(2)}, u32[]{:S(2)}) collective-permute-start(f32[11,32,256]{2,1,0:T(8,128)S(1)} %pad_maximum_fusion.1), channel_id=1, source_target_pairs={{4,0},{8,4},{12,8},{16,12},{20,16},{24,20},{28,24},{5,1},{9,5},{13... | collective-permute-start | bytes 1081352 | tf_op jit(solution)/shard_map/ppermute | solution.py:637
  8.3 14.0 %collective-permute-done.low = f32[11,32,256]{2,1,0:T(8,128)S(1)} collective-permute-done((f32[11,32,256]{2,1,0:T(8,128)S(1)}, f32[11,32,256]{2,1,0:T(8,128)S(1)}, u32[]{:S(2)}, u32[]{:S(2)}) %collective-permute-start) | collective-permute-done | bytes 360480 | tf_op jit(solution)/shard_map/ppermute | solution.py:637
  22.4 1.1 %slice_dynamic-update-slice_fusion.2 = (f32[70,4,256]{2,1,0:T(4,128)S(1)}, f32[70,4,256]{2,1,0:T(4,128)S(1)}) fusion(f32[70,4,256]{2,1,0:T(4,128)S(1)} %get-tuple-element.65, f32[16,32,256]{2,1,0:T(8,128)} %guess.1, f32[70,4,256]{2,1,0:T(4,128)S(1)} %get-tuple-element.66), kind=kLoop, calls=%fused_computation.4 | loop fusion | bytes 262144
  23.5 0.0 collective-permute-done.1.high
  23.6 1.1 %slice_dynamic-update-slice_fusion.1 = (f32[70,4,256]{2,1,0:T(4,128)S(1)}, f32[70,4,256]{2,1,0:T(4,128)S(1)}) fusion(f32[70,4,256]{2,1,0:T(4,128)S(1)} %get-tuple-element.61, f32[16,32,256]{2,1,0:T(8,128)} %source.1, f32[70,4,256]{2,1,0:T(4,128)S(1)} %get-tuple-element.62), kind=kLoop, calls=%fused_computation.3 | loop fusion | bytes 262144
  24.7 1.0 slice_dynamic-update-slice_fusion
  25.8 1.3 %collective-permute-start.2 = (f32[70,4,256]{2,1,0:T(4,128)S(1)}, f32[70,4,256]{2,1,0:T(4,128)S(1)}, u32[]{:S(2)}, u32[]{:S(2)}) collective-permute-start(f32[70,4,256]{2,1,0:T(4,128)S(1)} %get-tuple-element.56), channel_id=1, source_target_pairs={{0,1},{1,2},{2,3},{4,5},{5,6},{6,7},{8,9},{9,10},{10,11},{12,13},{... | collective-permute-start | bytes 860168 | tf_op jit(solution)/shard_map/ppermute | solution.py:637
  27.1 1.3 %collective-permute-start.3 = (f32[70,4,256]{2,1,0:T(4,128)S(1)}, f32[70,4,256]{2,1,0:T(4,128)S(1)}, u32[]{:S(2)}, u32[]{:S(2)}) collective-permute-start(f32[70,4,256]{2,1,0:T(4,128)S(1)} %get-tuple-element.55), channel_id=1, source_target_pairs={{1,0},{2,1},{3,2},{5,4},{6,5},{7,6},{9,8},{10,9},{11,10},{13,12},{... | collective-permute-start | bytes 860168 | tf_op jit(solution)/shard_map/ppermute | solution.py:637
  28.4 0.0 collective-permute-done.2.left
  28.4 3.9 %collective-permute-done.3.right = f32[70,4,256]{2,1,0:T(4,128)S(1)} collective-permute-done((f32[70,4,256]{2,1,0:T(4,128)S(1)}, f32[70,4,256]{2,1,0:T(4,128)S(1)}, u32[]{:S(2)}, u32[]{:S(2)}) %collective-permute-start.3) | collective-permute-done | bytes 286752 | tf_op jit(solution)/shard_map/ppermute | solution.py:637
  32.3 0.7 copy-done.8
  33.0 5.7 %shard_map.37 = (f32[16,32,256]{2,1,0:T(8,128)}, f32[24,5,2,8,128]{4,3,2,1,0:T(8,128)}, f32[24,5,2,8,128]{4,3,2,1,0:T(8,128)}, f32[24,5,2,8,128]{4,3,2,1,0:T(8,1...) custom-call(f32[16,32,256]{2,1,0:T(8,128)} %guess.1, ...), custom_call_target="tpu_custom_call" | custom-call | tf_op jit(solution)/shard_map/pallas_call | solution.py:619
  38.7 4.4 %collective-permute-start.4 = (f32[27,16,128]{2,1,0:T(8,128)}, f32[27,16,128]{2,1,0:T(8,128)S(1)}, u32[]{:S(2)}, u32[]{:S(2)}) collective-permute-start(f32[27,16,128]{2,1,0:T(8,128)} %get-tuple-element.26), channel_id=1, source_target_pairs={{0,4},{4,8},{8,12},{12,16},{16,20},{20,24},{24,28},{1,5},{5,9},{9,... | collective-permute-start | bytes 663560 | tf_op jit(solution)/shard_map/ppermute | solution.py:637
  43.1 1.3 %collective-permute-start.5 = (f32[27,16,128]{2,1,0:T(8,128)}, f32[27,16,128]{2,1,0:T(8,128)S(1)}, u32[]{:S(2)}, u32[]{:S(2)}) collective-permute-start(f32[27,16,128]{2,1,0:T(8,128)} %get-tuple-element.27), channel_id=1, source_target_pairs={{4,0},{8,4},{12,8},{16,12},{20,16},{24,20},{28,24},{5,1},{9,5},{13... | collective-permute-start | bytes 663560 | tf_op jit(solution)/shard_map/ppermute | solution.py:637
  44.4 2.4 %collective-permute-done.4.low = f32[27,16,128]{2,1,0:T(8,128)S(1)} collective-permute-done((f32[27,16,128]{2,1,0:T(8,128)}, f32[27,16,128]{2,1,0:T(8,128)S(1)}, u32[]{:S(2)}, u32[]{:S(2)}) %collective-permute-start.4) | collective-permute-done | bytes 221216 | tf_op jit(solution)/shard_map/ppermute | solution.py:637
  46.8 4.3 %collective-permute-done.5.high = f32[27,16,128]{2,1,0:T(8,128)S(1)} collective-permute-done((f32[27,16,128]{2,1,0:T(8,128)}, f32[27,16,128]{2,1,0:T(8,128)S(1)}, u32[]{:S(2)}, u32[]{:S(2)}) %collective-permute-start.5) | collective-permute-done | bytes 221216 | tf_op jit(solution)/shard_map/ppermute | solution.py:637
  51.1 0.7 copy-done.2
  51.8 2.1 %shard_map.38 = (f32[68,8,128]{2,1,0:T(8,128)}, f32[68,8,128]{2,1,0:T(8,128)}) custom-call(f32[8,16,128]{2,1,0:T(8,128)} %get-tuple-element.24.b1, f32[8,16,128]{2,1,0:T(8,128)} %get-tuple-element.25.c1, f32[16,32,256]{2,1,0:T(8,128)} %get-tuple-element.28.v.v0, f32[27,16,128]{2,1,0:T(8,128)} %copy-done.1, f32[27,16,128]{2,1,0:T(8,128)} %copy-done.2), custom_call_target="tpu_custom_call" | custom-call | tf_op jit(solution)/shard_map/pallas_call | solution.py:619
  54.0 6.5 %collective-permute-start.6 = (f32[68,8,128]{2,1,0:T(8,128)}, f32[68,8,128]{2,1,0:T(8,128)S(1)}, u32[]{:S(2)}, u32[]{:S(2)}) collective-permute-start(f32[68,8,128]{2,1,0:T(8,128)} %get-tuple-element.29), channel_id=1, source_target_pairs={{0,1},{1,2},{2,3},{4,5},{5,6},{6,7},{8,9},{9,10},{10,11},{12,13},{... | collective-permute-start | bytes 835592 | tf_op jit(solution)/shard_map/ppermute | solution.py:637
  60.5 1.3 %collective-permute-start.7 = (f32[68,8,128]{2,1,0:T(8,128)}, f32[68,8,128]{2,1,0:T(8,128)S(1)}, u32[]{:S(2)}, u32[]{:S(2)}) collective-permute-start(f32[68,8,128]{2,1,0:T(8,128)} %get-tuple-element.30), channel_id=1, source_target_pairs={{1,0},{2,1},{3,2},{5,4},{6,5},{7,6},{9,8},{10,9},{11,10},{13,12},{... | collective-permute-start | bytes 835592 | tf_op jit(solution)/shard_map/ppermute | solution.py:637
  61.8 0.1 collective-permute-done.6.left
  61.9 2.3 %collective-permute-done.7.right = f32[68,8,128]{2,1,0:T(8,128)S(1)} collective-permute-done((f32[68,8,128]{2,1,0:T(8,128)}, f32[68,8,128]{2,1,0:T(8,128)S(1)}, u32[]{:S(2)}, u32[]{:S(2)}) %collective-permute-start.7) | collective-permute-done | bytes 278560 | tf_op jit(solution)/shard_map/ppermute | solution.py:637
  64.2 0.7 copy-done.4
  64.9 3.2 %shard_map.39 = (f32[24,4,1,8,128]{4,3,2,1,0:T(8,128)}, f32[24,4,1,8,128]{4,3,2,1,0:T(8,128)}, f32[24,4,1,8,128]{4,3,2,1,0:T(8,128)}, f32[24,4,1,8,128]{4,3,2,1,...) custom-call(f32[8,16,128]{2,1,0:T(8,128)} %get-tuple-element.24.b1, ...), custom_call_target="tpu_custom_call" | custom-call | tf_op jit(solution)/shard_map/pallas_call | solution.py:619
  68.1 8.8 %all-to-all-start = ((f32[32,4,8,128]{3,2,1,0:T(8,128)}), f32[32,4,8,128]{3,2,1,0:T(8,128)S(1)}, u32[]{:S(2)}, u32[]{:S(2)}) async-start(f32[32,4,8,128]{3,2,1,0:T(8,128)} %get-tuple-element.31), calls=%async_computation | async-start | bytes 1048576 | tf_op jit(solution)/shard_map/all_to_all | solution.py:683
  76.9 0.7 pad_add_fusion.place_ref
  77.6 14.9 %all-to-all-done.gathered = f32[32,4,8,128]{3,2,1,0:T(8,128)S(1)} async-done(((f32[32,4,8,128]{3,2,1,0:T(8,128)}), f32[32,4,8,128]{3,2,1,0:T(8,128)S(1)}, u32[]{:S(2)}, u32[]{:S(2)}) %all-to-all-start) | async-done | bytes 524320 | tf_op jit(solution)/shard_map/all_to_all | solution.py:683
  92.5 0.8 copy-done
  93.3 10.7 %shard_map.40 = f32[16,32,256]{2,1,0:T(8,128)} custom-call(s32[2]{0:T(128)} %pad_add_fusion.place_ref, f32[32,4,8,128]{3,2,1,0:T(8,128)} %copy-done, f32[24,4,1,8,128]{4,3,2,1,0:T(8,128)} %get-tuple-element.32.v1, f32[24,4,1,8,128]{4,3,2,1,0:T(8,128)} %get-tuple-element.33.wx1, f32[24,4,1,8,128]{4,3,2,1,0:T(8,128)} %get-tuple-element.34.wy1, ...), custom_call_target="tpu_custom_call" | custom-call | tf_op jit(solution)/shard_map/pallas_call | solution.py:619
  (22 shorter events, 0.2 us)
Async XLA Ops:
  2.1 20.2 %collective-permute-start = (f32[11,32,256]{2,1,0:T(8,128)S(1)}, f32[11,32,256]{2,1,0:T(8,128)S(1)}, u32[]{:S(2)}, u32[]{:S(2)}) collective-permute-start(f32[11,32,256]{2,1,0:T(8,128)S(1)} %pad_maximum_fusion), channel_id=1, source_target_pairs={{0,4},{4,8},{8,12},{12,16},{16,20},{20,24},{24,28},{1,5},{5,9},{9,... | collective-permute-start | bytes 1081352 | tf_op jit(solution)/shard_map/ppermute | solution.py:637
  7.0 16.5 %collective-permute-start.1 = (f32[11,32,256]{2,1,0:T(8,128)S(1)}, f32[11,32,256]{2,1,0:T(8,128)S(1)}, u32[]{:S(2)}, u32[]{:S(2)}) collective-permute-start(f32[11,32,256]{2,1,0:T(8,128)S(1)} %pad_maximum_fusion.1), channel_id=1, source_target_pairs={{4,0},{8,4},{12,8},{16,12},{20,16},{24,20},{28,24},{5,1},{9,5},{13... | collective-permute-start | bytes 1081352 | tf_op jit(solution)/shard_map/ppermute | solution.py:637
  22.4 2.3 %copy-start.5 = (f32[11,32,256]{2,1,0:T(8,128)}, f32[11,32,256]{2,1,0:T(8,128)S(1)}, u32[]{:S(2)}) copy-start(f32[11,32,256]{2,1,0:T(8,128)S(1)} %collective-permute-done.low) | copy-start | bytes 1081348
  23.5 2.2 %copy-start.6 = (f32[11,32,256]{2,1,0:T(8,128)}, f32[11,32,256]{2,1,0:T(8,128)S(1)}, u32[]{:S(2)}) copy-start(f32[11,32,256]{2,1,0:T(8,128)S(1)} %collective-permute-done.1.high) | copy-start | bytes 1081348
  25.8 2.6 %collective-permute-start.2 = (f32[70,4,256]{2,1,0:T(4,128)S(1)}, f32[70,4,256]{2,1,0:T(4,128)S(1)}, u32[]{:S(2)}, u32[]{:S(2)}) collective-permute-start(f32[70,4,256]{2,1,0:T(4,128)S(1)} %get-tuple-element.56), channel_id=1, source_target_pairs={{0,1},{1,2},{2,3},{4,5},{5,6},{6,7},{8,9},{9,10},{10,11},{12,13},{... | collective-permute-start | bytes 860168 | tf_op jit(solution)/shard_map/ppermute | solution.py:637
  27.1 5.2 %collective-permute-start.3 = (f32[70,4,256]{2,1,0:T(4,128)S(1)}, f32[70,4,256]{2,1,0:T(4,128)S(1)}, u32[]{:S(2)}, u32[]{:S(2)}) collective-permute-start(f32[70,4,256]{2,1,0:T(4,128)S(1)} %get-tuple-element.55), channel_id=1, source_target_pairs={{1,0},{2,1},{3,2},{5,4},{6,5},{7,6},{9,8},{10,9},{11,10},{13,12},{... | collective-permute-start | bytes 860168 | tf_op jit(solution)/shard_map/ppermute | solution.py:637
  28.4 3.9 %copy-start.7 = (f32[70,4,256]{2,1,0:T(4,128)}, f32[70,4,256]{2,1,0:T(4,128)S(1)}, u32[]{:S(2)}) copy-start(f32[70,4,256]{2,1,0:T(4,128)S(1)} %collective-permute-done.2.left) | copy-start | bytes 860164
  32.3 0.7 copy-start.8
  38.7 8.1 %collective-permute-start.4 = (f32[27,16,128]{2,1,0:T(8,128)}, f32[27,16,128]{2,1,0:T(8,128)S(1)}, u32[]{:S(2)}, u32[]{:S(2)}) collective-permute-start(f32[27,16,128]{2,1,0:T(8,128)} %get-tuple-element.26), channel_id=1, source_target_pairs={{0,4},{4,8},{8,12},{12,16},{16,20},{20,24},{24,28},{1,5},{5,9},{9,... | collective-permute-start | bytes 663560 | tf_op jit(solution)/shard_map/ppermute | solution.py:637
  43.1 8.0 %collective-permute-start.5 = (f32[27,16,128]{2,1,0:T(8,128)}, f32[27,16,128]{2,1,0:T(8,128)S(1)}, u32[]{:S(2)}, u32[]{:S(2)}) collective-permute-start(f32[27,16,128]{2,1,0:T(8,128)} %get-tuple-element.27), channel_id=1, source_target_pairs={{4,0},{8,4},{12,8},{16,12},{20,16},{24,20},{28,24},{5,1},{9,5},{13... | collective-permute-start | bytes 663560 | tf_op jit(solution)/shard_map/ppermute | solution.py:637
  46.8 4.3 %copy-start.1 = (f32[27,16,128]{2,1,0:T(8,128)}, f32[27,16,128]{2,1,0:T(8,128)S(1)}, u32[]{:S(2)}) copy-start(f32[27,16,128]{2,1,0:T(8,128)S(1)} %collective-permute-done.4.low) | copy-start | bytes 663556
  51.1 0.7 copy-start.2
  54.0 7.9 %collective-permute-start.6 = (f32[68,8,128]{2,1,0:T(8,128)}, f32[68,8,128]{2,1,0:T(8,128)S(1)}, u32[]{:S(2)}, u32[]{:S(2)}) collective-permute-start(f32[68,8,128]{2,1,0:T(8,128)} %get-tuple-element.29), channel_id=1, source_target_pairs={{0,1},{1,2},{2,3},{4,5},{5,6},{6,7},{8,9},{9,10},{10,11},{12,13},{... | collective-permute-start | bytes 835592 | tf_op jit(solution)/shard_map/ppermute | solution.py:637
  60.5 3.7 %collective-permute-start.7 = (f32[68,8,128]{2,1,0:T(8,128)}, f32[68,8,128]{2,1,0:T(8,128)S(1)}, u32[]{:S(2)}, u32[]{:S(2)}) collective-permute-start(f32[68,8,128]{2,1,0:T(8,128)} %get-tuple-element.30), channel_id=1, source_target_pairs={{1,0},{2,1},{3,2},{5,4},{6,5},{7,6},{9,8},{10,9},{11,10},{13,12},{... | collective-permute-start | bytes 835592 | tf_op jit(solution)/shard_map/ppermute | solution.py:637
  61.9 2.3 %copy-start.3 = (f32[68,8,128]{2,1,0:T(8,128)}, f32[68,8,128]{2,1,0:T(8,128)S(1)}, u32[]{:S(2)}) copy-start(f32[68,8,128]{2,1,0:T(8,128)S(1)} %collective-permute-done.6.left) | copy-start | bytes 835588
  64.2 0.7 copy-start.4
  68.1 24.3 %all-to-all-start = ((f32[32,4,8,128]{3,2,1,0:T(8,128)}), f32[32,4,8,128]{3,2,1,0:T(8,128)S(1)}, u32[]{:S(2)}, u32[]{:S(2)}) async-start(f32[32,4,8,128]{3,2,1,0:T(8,128)} %get-tuple-element.31), calls=%async_computation | async-start | bytes 1048576 | tf_op jit(solution)/shard_map/all_to_all | solution.py:683
  92.5 0.8 copy-start

commit v3 on v2

--- a/solution.py
+++ b/solution.py
@@ -1,3 +1,4 @@
+import math
 from functools import partial
 
 import jax
@@ -22,7 +23,7 @@
 SOURCE = COARSE - 1
 POST = SWEEPS
 BLOCK = 24
-VMEM_LIMIT = 56 * 1024 * 1024
+SPARE = 4 * 1024 * 1024
 
 
 def dot(a, b):
@@ -39,6 +40,27 @@
 
 def roll(x, by, axis):
     return pltpu.roll(x, by % x.shape[axis], axis)
+
+
+def is_even(axis):
+    return lax.axis_index(axis) % 2 == 0
+
+
+class Sides:
+    def __init__(self, axis, first, second):
+        self.even, self.first, self.second = is_even(axis), first, second
+
+    def low(self, *at):
+        return jnp.where(self.even, self.second[at], self.first[at])
+
+    def high(self, *at):
+        return jnp.where(self.even, self.first[at], self.second[at])
+
+
+def address(axis, first, second, write):
+    even = is_even(axis)
+    pl.when(even)(lambda: write(first, second))
+    pl.when(jnp.logical_not(even))(lambda: write(second, first))
 
 
 def planes(first, last, step):
@@ -160,14 +182,78 @@
     return jnp.where(iota((lanes, width), 0) // 2 + offset == iota((lanes, width), 1), value, 0.0).astype(F32)
 
 
+def pack_lanes(lanes, value):
+    return jnp.concatenate((halve_lanes(lanes, LANES, value), halve_lanes(lanes, LANES, value, lanes // 2)), 0)
+
+
 def even_odd(ref, count):
     return ref[pl.ds(0, count, stride=2), :] + ref[pl.ds(1, count, stride=2), :]
 
 
-def fine_pre_kernel(guess, source, coef, low, high, left, right,
-                    out, wx, wy, wz, gain, scaled, up, down, b1, c1,
+def edge_kernel(guess0, guess1, source0, source1, coef0, coef1, first, second):
+    def write(up, down):
+        at = 0
+        for lower, upper, width in ((guess0, guess1, FINE), (source0, source1, FINE - 1), (coef0, coef1, FINE)):
+            up[at:at + width] = upper[FINE - width:]
+            down[at:at + width] = lower[:width]
+            at += width
+
+    address("gx", first, second, write)
+
+
+def own_kernel(guess, source, coef, up, down, c1, send, *pairs):
+    nx, ny, nz = guess.shape
+    pieces = nz // LANES
+    n1, r1 = nx // 2, ny // 2
+    for which, field in enumerate((guess, source, coef)):
+        def edges(k):
+            up[which * nx + k] = field[k, ny - FINE:, :]
+            down[which * nx + k] = field[k, :FINE, :]
+
+        planes(0, nx, edges)
+    for q in range(n1):
+        for t in range(pieces):
+            lanes = slice(t * LANES, (t + 1) * LANES)
+            pairs[t][q * ny:(q + 1) * ny, :] = coef[2 * q, :, lanes] + coef[2 * q + 1, :, lanes]
+    wide = jnp.concatenate([even_odd(pairs[t], n1 * r1) for t in range(pieces)], 1)
+    c1[...] = dot(wide, halve_lanes(nz, nz // 2, 0.125)).reshape(n1, r1, nz // 2)
+
+    n2, r2 = n1 // 2, r1 // 2
+    for q in range(n2):
+        pairs[0][q * r1:(q + 1) * r1, :] = c1[2 * q] + c1[2 * q + 1]
+    narrow = even_odd(pairs[0], n2 * r2)
+    wide = jnp.concatenate((narrow[:n2 * r2 // 2], narrow[n2 * r2 // 2:]), 1)
+    c2 = dot(wide, pack_lanes(nz // 2, 0.125)).reshape(n2 // 2, r2, LANES)
+    for d in range(send.shape[0]):
+        send[d] = c2
+
+
+def corner_kernel(own_up, own_down, one, two, first, second):
+    nx = own_up.shape[0] // 3
+    sides = Sides("gx", one, two)
+    ny = one.shape[1]
+
+    def write(up, down):
+        at = base = 0
+        for which, width in enumerate((FINE, FINE - 1, FINE)):
+            for k in range(width):
+                for message, slot in ((sides.low, at + k), (sides.high, at + width + nx + k)):
+                    up[slot] = message(base + k, pl.ds(ny - FINE, FINE))
+                    down[slot] = message(base + k, pl.ds(0, FINE))
+            for k in range(nx):
+                up[at + width + k] = own_up[which * nx + k]
+                down[at + width + k] = own_down[which * nx + k]
+            at += nx + 2 * width
+            base += width
+
+    address("gy", first, second, write)
+
+
+def fine_pre_kernel(guess, source, coef, c1, one, two, three, four, done,
+                    out, wx, wy, wz, gain, scaled, first, second, b1,
                     field, force, c, v, w, total, *pairs):
     nx, ny, nz = guess.shape
+    across, beside = Sides("gx", one, two), Sides("gy", three, four)
     pieces = nz // LANES
     rows = ny + 2 * FINE
     count = rows // 8
@@ -180,7 +266,7 @@
         message = sum(base)
 
         def rest(k):
-            side = jnp.concatenate((right[offset + k], left[offset + k]), 0)
+            side = jnp.concatenate((beside.high(offset + k), beside.low(offset + k)), 0)
             for t in range(pieces):
                 target[at + k, t, ny:] = side[:, t * LANES:(t + 1) * LANES]
 
@@ -193,9 +279,9 @@
         planes(0, nx, main)
         for k in range(width):
             for t in range(pieces):
-                lanes = slice(t * LANES, (t + 1) * LANES)
-                target[at + k, t, :ny] = low[message + k, :, lanes]
-                target[FINE + nx + k, t, :ny] = high[message + k, :, lanes]
+                place = (message + k, slice(None), slice(t * LANES, (t + 1) * LANES))
+                target[at + k, t, :ny] = across.low(*place)
+                target[FINE + nx + k, t, :ny] = across.high(*place)
 
     def spaced(ref):
         return lambda p, j, t: ref[p, t, pl.ds(j, 8, stride=count), :]
@@ -245,71 +331,58 @@
 
     planes(0, n1, halve)
     b1[...] = coarsen(0.125 * 0.5)
-    for q in range(n1):
-        for t in range(pieces):
-            lanes = slice(t * LANES, (t + 1) * LANES)
-            pairs[t][q * rows:q * rows + ny, :] = coef[2 * q, :, lanes] + coef[2 * q + 1, :, lanes]
-    c1[...] = coarsen(0.125)
-
-    up[:SOURCE] = b1[n1 - SOURCE:]
-    down[:SOURCE] = b1[:SOURCE]
-    up[SOURCE:SOURCE + COARSE] = c1[n1 - COARSE:]
-    down[SOURCE:SOURCE + COARSE] = c1[:COARSE]
-    at = SOURCE + COARSE
-    for k in range(POST):
-        for i in range(2):
-            for j in range(2):
-                here, lanes = pl.ds(i * r1, r1), pl.ds(j * (nz // 2), nz // 2)
-                up[at] = out[nx - POST + k, here, lanes]
-                down[at] = out[k, here, lanes]
-                at += 1
-
-
-def rows_kernel(b1, c1, v, low, high, up, down):
+
+    def write(up, down):
+        up[:SOURCE] = b1[n1 - SOURCE:]
+        down[:SOURCE] = b1[:SOURCE]
+        up[SOURCE:SOURCE + COARSE] = c1[n1 - COARSE:]
+        down[SOURCE:SOURCE + COARSE] = c1[:COARSE]
+        at = SOURCE + COARSE
+        for k in range(POST):
+            for i in range(2):
+                for j in range(2):
+                    here, lanes = pl.ds(i * r1, r1), pl.ds(j * (nz // 2), nz // 2)
+                    up[at] = out[nx - POST + k, here, lanes]
+                    down[at] = out[k, here, lanes]
+                    at += 1
+
+    address("gx", first, second, write)
+
+
+def rows_kernel(b1, c1, v, one, two, first, second):
     n1, r1, half = b1.shape
     nx, ny = 2 * n1, 2 * r1
-
-    def edge(take, at):
-        up[at] = take(r1 - COARSE, COARSE)
-        down[at] = take(0, COARSE)
-
-    at = 0
-    for k in range(SOURCE):
-        edge(lambda s, n: low[k, pl.ds(s, n), :], at)
-        edge(lambda s, n: high[k, pl.ds(s, n), :], at + SOURCE + n1)
-        at += 1
-    for k in range(n1):
-        edge(lambda s, n: b1[k, pl.ds(s, n), :], at)
-        at += 1
-    at += SOURCE
-    for k in range(COARSE):
-        edge(lambda s, n: low[SOURCE + k, pl.ds(s, n), :], at)
-        edge(lambda s, n: high[SOURCE + k, pl.ds(s, n), :], at + COARSE + n1)
-        at += 1
-    for k in range(n1):
-        edge(lambda s, n: c1[k, pl.ds(s, n), :], at)
-        at += 1
-    at += COARSE
-    base = SOURCE + COARSE
-    for k in range(POST):
-        for j in range(2):
-            rows = pl.ds(j * FINE, FINE)
-            up[at, rows, :] = low[base + 4 * k + 2 + j, r1 - FINE:, :]
-            down[at, rows, :] = low[base + 4 * k + j, :FINE, :]
-            up[at + POST + nx, rows, :] = high[base + 4 * k + 2 + j, r1 - FINE:, :]
-            down[at + POST + nx, rows, :] = high[base + 4 * k + j, :FINE, :]
-        at += 1
-
-    def own(k):
+    sides = Sides("gx", one, two)
+
+    def write(up, down):
+        def edge(take, at):
+            up[at] = take(pl.ds(r1 - COARSE, COARSE))
+            down[at] = take(pl.ds(0, COARSE))
+
+        at = base = 0
+        for own, width in ((b1, SOURCE), (c1, COARSE)):
+            for k in range(width):
+                edge(lambda rows: sides.low(base + k, rows), at + k)
+                edge(lambda rows: sides.high(base + k, rows), at + width + n1 + k)
+            for k in range(n1):
+                edge(lambda rows: own[k, rows, :], at + width + k)
+            at += n1 + 2 * width
+            base += width
         for j in range(2):
             rows, lanes = pl.ds(j * FINE, FINE), pl.ds(j * half, half)
-            up[at + k, rows, :] = v[k, ny - FINE:, lanes]
-            down[at + k, rows, :] = v[k, :FINE, lanes]
-
-    planes(0, nx, own)
-
-
-def coarse_pre_kernel(b1, c1, low, high, left, right,
+            last, start = pl.ds(r1 - FINE, FINE), pl.ds(0, FINE)
+            for k in range(POST):
+                for message, slot in ((sides.low, at + k), (sides.high, at + POST + nx + k)):
+                    up[slot, rows, :] = message(base + 4 * k + 2 + j, last)
+                    down[slot, rows, :] = message(base + 4 * k + j, start)
+            for k in range(nx):
+                up[at + POST + k, rows, :] = v[k, ny - FINE:, lanes]
+                down[at + POST + k, rows, :] = v[k, :FINE, lanes]
+
+    address("gy", first, second, write)
+
+
+def coarse_pre_kernel(b1, c1, one, two, three, four,
                       v, wx, wy, wz, gain, scaled, send, field, c, w, total, upper, lower):
     n1, r1, lanes = b1.shape
     rows = r1 + 2 * COARSE
@@ -317,17 +390,18 @@
     planes1 = n1 + 2 * COARSE
     scale = 0.25
     level = (wx, wy, wz, gain, scaled, total)
+    across, beside = Sides("gx", one, two), Sides("gy", three, four)
 
     def fill(target, own, base, offset, width):
         at = COARSE - width
         for k in range(n1 + 2 * width):
-            target[at + k, r1:r1 + COARSE] = right[offset + k]
-            target[at + k, r1 + COARSE:] = left[offset + k]
+            target[at + k, r1:r1 + COARSE] = beside.high(offset + k)
+            target[at + k, r1 + COARSE:] = beside.low(offset + k)
         for k in range(n1):
             target[COARSE + k, :r1] = own[k]
         for k in range(width):
-            target[at + k, :r1] = low[base + k]
-            target[COARSE + n1 + k, :r1] = high[base + k]
+            target[at + k, :r1] = across.low(base + k)
+            target[COARSE + n1 + k, :r1] = across.high(base + k)
 
     def spaced(ref):
         return lambda p, j, t: ref[p, pl.ds(j, 8, stride=count), :]
@@ -345,25 +419,16 @@
     n2, r2 = n1 // 2, r1 // 2
     half = n2 // 2
 
-    def coarsen(value):
-        matrix = jnp.concatenate((halve_lanes(lanes, LANES, value), halve_lanes(lanes, LANES, value, lanes // 2)), 0)
-        return dot(jnp.concatenate((lower[...], upper[...]), 1), matrix).reshape(half, r2, LANES)
-
     for q in range(n2):
         one, two = (residual(reader(v), level, COARSE + 2 * q + k) for k in range(2))
         target = lower if q < half else upper
         for j in range(count // 2):
             value = (one[2 * j, 0] + two[2 * j, 0]) + (one[2 * j + 1, 0] + two[2 * j + 1, 0])
             target[pl.ds(q % half * r2 + j, r1 // count, stride=count // 2), :] = value[:r1 // count]
-    b2 = coarsen(0.125 * 0.5 * scale)
-    for q in range(n2):
-        target = lower if q < half else upper
-        field[q, :r1] = c1[2 * q] + c1[2 * q + 1]
-        target[q % half * r2:(q % half + 1) * r2, :] = even_odd(field.at[q], r2)
-    c2 = coarsen(0.125)
+    wide = jnp.concatenate((lower[...], upper[...]), 1)
+    b2 = dot(wide, pack_lanes(lanes, 0.125 * 0.5 * scale)).reshape(half, r2, LANES)
     for d in range(send.shape[0]):
-        send[d, :half] = b2
-        send[d, half:] = c2
+        send[d] = b2
 
 
 def pads(ref, depth):
@@ -380,8 +445,8 @@
     return (2 * block + group) * (depth // 2) + z // 2 == target
 
 
-def solve_kernel(place_ref, gathered, v1, wx1, wy1, wz1, gain1, scaled1, v0, wx0, wy0, wz0, gain0, scaled0,
-                 low, high, left, right, out,
+def solve_kernel(gathered_b, gathered_c, v1, wx1, wy1, wz1, gain1, scaled1, v0, wx0, wy0, wz0, gain0, scaled0,
+                 one, two, three, four, out,
                  c2, a2, y2, n2, l2x, l2y, l2z, l2g, l2s, l2t,
                  c3, b3, a3, y3, l3x, l3y, l3z, l3g, l3s, l3t,
                  c4, b4, y4, l4x, l4y, l4z, l4g, l4s,
@@ -389,8 +454,8 @@
     level2 = (l2x, l2y, l2z, l2g, l2s, l2t)
     level3 = (l3x, l3y, l3z, l3g, l3s, l3t)
     level4 = (l4x, l4y, l4z, l4g, l4s, None)
-    half = gathered.shape[1] // 2
-    r2 = gathered.shape[2]
+    across, beside = Sides("gx", one, two), Sides("gy", three, four)
+    half, r2 = gathered_b.shape[1:3]
     per = 2 * half
     m2, m3, m4 = c2.shape[0] - 2, c3.shape[0] - 2, c4.shape[0] - 2
     j2, j3, j4 = c2.shape[1], c3.shape[1], c4.shape[1]
@@ -402,12 +467,12 @@
     def unpack(i):
         for j in range(gy):
             for k in range(half):
-                for which in range(2):
-                    one = gathered[i * gy + j, which * half + k]
-                    two = gathered[(i + gx // 2) * gy + j, which * half + k]
+                for which, gathered in enumerate((gathered_b, gathered_c)):
+                    near = gathered[i * gy + j, k]
+                    far = gathered[(i + gx // 2) * gy + j, k]
                     here = pl.ds(j * r2, r2)
-                    n2[which, i * per + k, here, :] = jnp.where(lane < depth2, one, roll(two, depth2, 1))
-                    n2[which, i * per + half + k, here, :] = jnp.where(lane < depth2, roll(one, depth2, 1), two)
+                    n2[which, i * per + k, here, :] = jnp.where(lane < depth2, near, roll(far, depth2, 1))
+                    n2[which, i * per + half + k, here, :] = jnp.where(lane < depth2, roll(near, depth2, 1), far)
 
     planes(0, gx // 2, unpack)
 
@@ -518,7 +583,7 @@
     x2, z2 = smooth(x2, z2, level2, depth2, SWEEPS)
 
     level1 = (wx1, wy1, wz1, gain1, scaled1, None)
-    at_x, at_y = place_ref[0], place_ref[1]
+    at_x, at_y = lax.axis_index("gx"), lax.axis_index("gy")
     planes1, count1, _, _, lanes1 = v1.shape
     n1, r1 = planes1 - 2 * COARSE, 8 * count1 - 2 * COARSE
     sub = iota((8, LANES), 0)
@@ -587,11 +652,11 @@
                 if 0 <= q < nx:
                     own = v0[q, :, lanes]
                 else:
-                    message, slot = (low, p - (FINE - POST)) if q < 0 else (high, q - nx)
-                    own = jnp.concatenate([message[base + 4 * slot + 2 * h + t] for h in range(2)], 0)
+                    message, slot = (across.low, p - (FINE - POST)) if q < 0 else (across.high, q - nx)
+                    own = jnp.concatenate([message(base + 4 * slot + 2 * h + t) for h in range(2)], 0)
                 side = pl.ds(t * FINE, FINE)
                 at_side = beyond + p - (FINE - POST)
-                side = jnp.concatenate((right[at_side, side, :], left[at_side, side, :]), 0)
+                side = jnp.concatenate((beside.high(at_side, side), beside.low(at_side, side)), 0)
                 field[p, t, :ny] = own + value[:ny]
                 field[p, t, ny:] = side + value[ny:]
 
@@ -614,74 +679,85 @@
     planes(0, nx, put)
 
 
-def call(kernel, outs, scratch, *args, scalars=0):
-    specs = [pl.BlockSpec(memory_space=pltpu.SMEM if k < scalars else pltpu.VMEM) for k in range(len(args))]
+def limit(scratch, more):
+    need = sum(4 * math.prod(x.inner_aval.shape) for x in scratch)
+    return pltpu.CompilerParams(vmem_limit_bytes=SPARE + need + 2 * more)
+
+
+def call(kernel, outs, scratch, *args, specs=None):
+    if specs is None:
+        specs = [None] * len(args)
+    args = [x if spec and spec.memory_space == pl.ANY else pltpu.with_memory_space_constraint(x, pltpu.HBM if spec else pltpu.VMEM) for x, spec in zip(args, specs)]
+    size = sum(4 * math.prod(x.shape) for x, spec in zip(args, specs) if spec)
+    whole = pl.BlockSpec(memory_space=pltpu.VMEM)
     return pl.pallas_call(
         kernel,
+        grid=(1,) if any(spec and spec.block_shape for spec in specs) else (),
         out_shape=outs,
-        in_specs=specs,
-        out_specs=[pl.BlockSpec(memory_space=pltpu.VMEM) for _ in outs],
+        in_specs=[spec or whole for spec in specs],
+        out_specs=[whole for _ in outs],
         scratch_shapes=scratch,
-        compiler_params=pltpu.CompilerParams(vmem_limit_bytes=VMEM_LIMIT),
+        compiler_params=limit(scratch, size),
     )(*args)
 
 
 def shape(*dims):
-    return jax.ShapeDtypeStruct(dims, F32)
-
-
-def exchange(up, down, axis):
+    return pltpu.VMEM(dims, F32)
+
+
+def swap(first, second, axis):
     count = lax.axis_size(axis)
-    forward = [(i, i + 1) for i in range(count - 1)]
-    backward = [(target, source) for source, target in forward]
-    return lax.ppermute(up, axis, forward), lax.ppermute(down, axis, backward)
+    even = [(i, i ^ 1) for i in range(count) if i ^ 1 < count]
+    odd = [(i, ((i + 1) ^ 1) - 1) for i in range(count) if 0 <= ((i + 1) ^ 1) - 1 < count]
+    return lax.ppermute(first, axis, even), lax.ppermute(second, axis, odd)
 
 
 def body(guess, right_side, coefficient):
     gx, gy = lax.axis_size("gx"), lax.axis_size("gy")
     nx, ny, nz = guess.shape
-    fields = ((guess, FINE), (right_side, FINE - 1), (coefficient, FINE))
-    low, high = exchange(
-        jnp.concatenate([f[nx - k:] for f, k in fields], 0), jnp.concatenate([f[:k] for f, k in fields], 0), "gx"
+    n1, r1, z1 = nx // 2, ny // 2, nz // 2
+    n2, r2 = n1 // 2, r1 // 2
+    planes0, rows0, pieces = nx + 2 * FINE, ny + 2 * FINE, nz // LANES
+    whole = pl.BlockSpec(memory_space=pltpu.VMEM)
+    fields = (guess, right_side, coefficient)
+
+    ends = [pl.BlockSpec((FINE, ny, nz), lambda i, at=at: (at, 0, 0)) for at in (0, nx // FINE - 1)]
+    across = swap(*call(
+        edge_kernel, (shape(3 * FINE - 1, ny, nz),) * 2, (), *(f for f in fields for _ in range(2)), specs=ends * 3
+    ), "gx")
+    own_up, own_down, c1, send = call(
+        own_kernel,
+        (shape(3 * nx, FINE, nz),) * 2 + (shape(n1, r1, z1), shape(gx * gy, n2 // 2, r2, LANES)),
+        [vmem(n1 * ny, LANES)] * pieces,
+        *fields, specs=[whole] * 3,
     )
-
-    def rows(cut):
-        parts, at = [], 0
-        for f, k in fields:
-            parts += [cut(low[at:at + k]), cut(f), cut(high[at:at + k])]
-            at += k
-        return jnp.concatenate(parts, 0)
-
-    left, right = exchange(rows(lambda f: f[:, ny - FINE:]), rows(lambda f: f[:, :FINE]), "gy")
-
-    planes0, rows0, pieces = nx + 2 * FINE, ny + 2 * FINE, nz // LANES
+    gathered_c = lax.all_to_all(send, ("gx", "gy"), 0, 0)
+    corners = 3 * nx + 2 * (3 * FINE - 1)
+    beside = swap(*call(corner_kernel, (shape(corners, FINE, nz),) * 2, (), own_up, own_down, *across), "gy")
+
     block0 = (planes0, rows0 // 8, pieces, 8, LANES)
     plain0 = (planes0, pieces, rows0, LANES)
-    n1, r1, z1 = nx // 2, ny // 2, nz // 2
     message = (SOURCE + COARSE + 4 * POST, r1, z1)
-    v0, *level0, up, down, b1, c1 = call(
+    v0, *level0, first, second, b1 = call(
         fine_pre_kernel,
-        (shape(nx, ny, nz),) + (shape(*block0),) * 5 + (shape(*message),) * 2 + (shape(n1, r1, z1),) * 2,
+        (shape(nx, ny, nz),) + (shape(*block0),) * 5 + (shape(*message),) * 2 + (shape(n1, r1, z1),),
         [vmem(*plain0)] * 3 + [vmem(*block0)] * 3 + [vmem(n1 * rows0, LANES)] * pieces,
-        guess, right_side, coefficient, low, high, left, right,
+        *fields, c1, *across, *beside, gathered_c, specs=[whole] * 3 + [None] * 5 + [pl.BlockSpec(memory_space=pl.ANY)],
     )
-    low, high = exchange(up, down, "gx")
+    across = swap(first, second, "gx")
     count = 3 * n1 + 2 * SOURCE + 2 * COARSE + 2 * POST + n1
-    up, down = call(rows_kernel, (shape(count, COARSE, z1),) * 2, (), b1, c1, v0, low, high)
-    left, right = exchange(up, down, "gy")
+    beside = swap(*call(rows_kernel, (shape(count, COARSE, z1),) * 2, (), b1, c1, v0, *across), "gy")
 
     planes1, rows1 = n1 + 2 * COARSE, r1 + 2 * COARSE
     block1 = (planes1, rows1 // 8, 1, 8, z1)
     plain1 = (planes1, rows1, z1)
-    n2, r2 = n1 // 2, r1 // 2
     v1, *level1, send = call(
         coarse_pre_kernel,
-        (shape(*block1),) * 6 + (shape(gx * gy, n2, r2, LANES),),
+        (shape(*block1),) * 6 + (shape(gx * gy, n2 // 2, r2, LANES),),
         [vmem(*plain1)] * 2 + [vmem(*block1)] * 2 + [vmem(n2 // 2 * r2, LANES)] * 2,
-        b1, c1, low, high, left, right,
+        b1, c1, *across, *beside,
     )
-    gathered = lax.all_to_all(send, ("gx", "gy"), 0, 0)
-    place_at = jnp.stack((lax.axis_index("gx"), lax.axis_index("gy"))).astype(jnp.int32)
+    gathered_b = lax.all_to_all(send, ("gx", "gy"), 0, 0)
 
     m2, rows2 = gx * n2 // 2, gy * r2
     m3, m4 = m2 // 4, m2 // 16
@@ -692,10 +768,15 @@
         + [vmem(*block1)] * 2 + [vmem(planes1, max(rows2 + 16, rows1), z1)]
         + [vmem(*plain0)] + [vmem(*block0)] * 2 + [vmem(pieces, 256, LANES)]
     )
-    (out,) = call(
-        partial(solve_kernel, gx=gx, gy=gy), (shape(nx, ny, nz),), scratch,
-        place_at, gathered, v1, *level1, v0, *level0, low, high, left, right, scalars=1,
-    )
+    (out,) = pl.pallas_call(
+        partial(solve_kernel, gx=gx, gy=gy),
+        out_shape=(jax.ShapeDtypeStruct((nx, ny, nz), F32),),
+        in_specs=[whole] * 18,
+        out_specs=(whole,),
+        scratch_shapes=scratch,
+        compiler_params=limit(scratch, guess.size * 4),
+    )(*(pltpu.with_memory_space_constraint(x, pltpu.VMEM)
+        for x in (gathered_b, gathered_c, v1, *level1, v0, *level0, *across, *beside)))
     return out
 
 

time: 104 us -> 76.7 us (0.74)
  waiting for transfers between devices: 41.9 us -> 14.7 us
  blocking collectives: 0 us -> 25.9 us
  starting transfers between devices: 31 us -> 19.2 us
  local copies, waits for them, and re-layouts: 8.4 us -> 0 us
  Pallas kernels: 21.7 us -> 16.5 us
    all_to_all x0 -> x1, blocking collectives: none -> 25.9 us  [body(): gathered_b = lax.all_to_all(send, ('gx', 'gy'), 0, 0)]
    ppermute x8, waiting for transfers between devices: 27 us -> 11.3 us  [swap(): return (lax.ppermute(first, axis, even), lax.ppermute(second, axis, odd))]
    all_to_all x1, waiting for transfers between devices: 14.9 us -> 3.35 us  [body(): gathered_c = lax.all_to_all(send, ('gx', 'gy'), 0, 0)]
    ppermute x8, starting transfers between devices: 22.3 us -> 11.6 us  [swap(): return (lax.ppermute(first, axis, even), lax.ppermute(second, axis, odd))]
    unnamed x26 -> x0, local copies, waits for them, and re-layouts: 6.29 us -> none
    pallas_call x4 -> x7, Pallas kernels: 21.7 us -> 16.5 us  [the longest x6 9.32 us: call(): pl.pallas_call(kernel, grid=(1,) if any((spec and spec.block_shape for sp...]
    slice x2 -> x0, local copies, waits for them, and re-layouts: 2.09 us -> none  [body(): f[:k]]
    all_to_all x1, starting transfers between devices: 8.76 us -> 7.61 us  [body(): gathered_c = lax.all_to_all(send, ('gx', 'gy'), 0, 0)]
  transfers between devices with their start and end apart: 9 -> 9, of which waited for: 7 -> 4; matrix products, arithmetic and copies ran while one was open for 2% -> 0% of each run, Pallas kernels for 0% -> 3%
where the time goes in v3:
time: 76.7 us; the launch traced here: 76.4 us
  blocking collectives  25.9 us (34%)
  starting transfers between devices  19.2 us (25%)
  Pallas kernels  16.5 us (22%)
  waiting for transfers between devices  14.7 us (19%)
    all_to_all x1, blocking collectives, body(): gathered_b = lax.all_to_all(send, ('gx', 'gy'), 0, 0)  25.9 us
    ppermute x8, starting transfers between devices, swap(): return (lax.ppermute(first, axis, even), lax.ppermute(second, axis, odd))  11.6 us
    ppermute x8, waiting for transfers between devices, swap(): return (lax.ppermute(first, axis, even), lax.ppermute(second, axis, odd))  11.3 us
    pallas_call x6, Pallas kernels, call(): pl.pallas_call(kernel, grid=(1,) if any((spec and spec.block_shape for sp...  9.32 us
    all_to_all x1, starting transfers between devices, body(): gathered_c = lax.all_to_all(send, ('gx', 'gy'), 0, 0)  7.61 us
    pallas_call x1, Pallas kernels, body(): pl.pallas_call(partial(solve_kernel, gx=gx, gy=gy), out_shape=(jax.ShapeD...  7.18 us
    all_to_all x1, waiting for transfers between devices, body(): gathered_c = lax.all_to_all(send, ('gx', 'gy'), 0, 0)  3.35 us
  transfers between devices with their start and end apart: 9, of which 4 were waited for; matrix products, arithmetic and copies ran while one was open for 0% of the time, Pallas kernels for 3%

profile of v3, /device:TPU:0, one launch (start us, length us, event | category | flops | bytes accessed | tf_op | source)
XLA Modules:
  0.0 76.4 jit_solution(8406307436541411408)
XLA Ops:
  0.0 1.2 %shard_map.38 = (f32[11,32,256]{2,1,0:T(8,128)S(1)}, f32[11,32,256]{2,1,0:T(8,128)S(1)}) custom-call(f32[16,32,256]{2,1,0:T(8,128)} %guess.3, f32[16,32,256]{2,1,0:T(8,128)} %guess.3, f32[16,32,256]{2,1,0:T(8,128)} %source.3, f32[16,32,256]{2,1,0:T(8,128)} %source.3, f32[16,32,256]{2,1,0:T(8,128)} %coef.3, f32[16,32,256]{2,1,0:T(8,128)} %coef.3), custom_call_target="tpu_custom_call" | custom-call | tf_op jit(solution)/shard_map/pallas_call | solution.py:693
  1.3 3.0 %collective-permute-start = (f32[11,32,256]{2,1,0:T(8,128)S(1)}, f32[11,32,256]{2,1,0:T(8,128)S(1)}, u32[]{:S(2)}, u32[]{:S(2)}) collective-permute-start(f32[11,32,256]{2,1,0:T(8,128)S(1)} %get-tuple-element.32), channel_id=1, source_target_pairs={{0,4},{4,0},{8,12},{12,8},{16,20},{20,16},{24,28},{28,24},{1,5},{5... | collective-permute-start | bytes 1081352 | tf_op jit(solution)/shard_map/ppermute | solution.py:712
  4.3 0.7 collective-permute-start.1
  4.9 2.6 %shard_map.37 = (f32[48,4,256]{2,1,0:T(4,128)S(1)}, f32[48,4,256]{2,1,0:T(4,128)S(1)}, f32[8,16,128]{2,1,0:T(8,128)S(1)}, f32[32,2,8,128]{3,2,1,0:T(8,128)}) custom-call(f32[16,32,256]{2,1,0:T(8,128)} %guess.3, f32[16,32,256]{2,1,0:T(8,128)} %source.3, f32[16,32,256]{2,1,0:T(8,128)} %coef.3), custom_call_target="tpu_custom_call" | custom-call | tf_op jit(solution)/shard_map/pallas_call | solution.py:693
  7.5 7.6 %all-to-all-start = ((f32[32,2,8,128]{3,2,1,0:T(8,128)}), f32[32,2,8,128]{3,2,1,0:T(8,128)S(1)}, u32[]{:S(2)}, u32[]{:S(2)}) async-start(f32[32,2,8,128]{3,2,1,0:T(8,128)} %get-tuple-element.38), calls=%async_computation | async-start | bytes 524288 | tf_op jit(solution)/shard_map/all_to_all | solution.py:734
  15.1 6.4 %collective-permute-done.one = f32[11,32,256]{2,1,0:T(8,128)S(1)} collective-permute-done((f32[11,32,256]{2,1,0:T(8,128)S(1)}, f32[11,32,256]{2,1,0:T(8,128)S(1)}, u32[]{:S(2)}, u32[]{:S(2)}) %collective-permute-start) | collective-permute-done | bytes 360480 | tf_op jit(solution)/shard_map/ppermute | solution.py:712
  21.5 0.0 collective-permute-done.1.two
  21.6 0.1 collective-permute-start.2
  21.7 0.7 collective-permute-start.3
  22.4 3.4 %all-to-all-done.done.gathered_c = f32[32,2,8,128]{3,2,1,0:T(8,128)S(1)} async-done(((f32[32,2,8,128]{3,2,1,0:T(8,128)}), f32[32,2,8,128]{3,2,1,0:T(8,128)S(1)}, u32[]{:S(2)}, u32[]{:S(2)}) %all-to-all-start) | async-done | bytes 262176 | tf_op jit(solution)/shard_map/all_to_all | solution.py:734
  25.7 0.0 collective-permute-done.2.three
  25.7 0.0 collective-permute-done.3.four
  25.7 4.4 %shard_map.40 = (f32[16,32,256]{2,1,0:T(8,128)S(1)}, f32[24,5,2,8,128]{4,3,2,1,0:T(8,128)S(1)}, f32[24,5,2,8,128]{4,3,2,1,0:T(8,128)S(1)}, f32[24,5,2,8,128]{4,3...) custom-call(f32[16,32,256]{2,1,0:T(8,128)} %guess.3, ...), custom_call_target="tpu_custom_call" | custom-call | tf_op jit(solution)/shard_map/pallas_call | solution.py:693
  30.2 1.0 %collective-permute-start.4 = (f32[27,16,128]{2,1,0:T(8,128)S(1)}, f32[27,16,128]{2,1,0:T(8,128)S(1)}, u32[]{:S(2)}, u32[]{:S(2)}) collective-permute-start(f32[27,16,128]{2,1,0:T(8,128)S(1)} %get-tuple-element.40), channel_id=1, source_target_pairs={{0,4},{4,0},{8,12},{12,8},{16,20},{20,16},{24,28},{28,24},{1,5},{5... | collective-permute-start | bytes 663560 | tf_op jit(solution)/shard_map/ppermute | solution.py:712
  31.1 0.7 collective-permute-start.5
  31.8 4.4 %collective-permute-done.4.one = f32[27,16,128]{2,1,0:T(8,128)S(1)} collective-permute-done((f32[27,16,128]{2,1,0:T(8,128)S(1)}, f32[27,16,128]{2,1,0:T(8,128)S(1)}, u32[]{:S(2)}, u32[]{:S(2)}) %collective-permute-start.4) | collective-permute-done | bytes 221216 | tf_op jit(solution)/shard_map/ppermute | solution.py:712
  36.2 0.0 collective-permute-done.5.two
  36.2 0.1 shard_map.41
  36.2 4.9 %collective-permute-start.6 = (f32[68,8,128]{2,1,0:T(8,128)S(1)}, f32[68,8,128]{2,1,0:T(8,128)S(1)}, u32[]{:S(2)}, u32[]{:S(2)}) collective-permute-start(f32[68,8,128]{2,1,0:T(8,128)S(1)} %get-tuple-element.43), channel_id=1, source_target_pairs={{0,1},{1,0},{2,3},{3,2},{4,5},{5,4},{6,7},{7,6},{8,9},{9,8},{10,11... | collective-permute-start | bytes 835592 | tf_op jit(solution)/shard_map/ppermute | solution.py:712
  41.1 0.7 collective-permute-start.7
  41.8 0.5 collective-permute-done.6.three
  42.3 0.0 collective-permute-done.7.four
  42.3 1.0 %shard_map.42 = (f32[24,4,1,8,128]{4,3,2,1,0:T(8,128)S(1)}, f32[24,4,1,8,128]{4,3,2,1,0:T(8,128)S(1)}, f32[24,4,1,8,128]{4,3,2,1,0:T(8,128)S(1)}, f32[24,4,1,8,1...) custom-call(f32[8,16,128]{2,1,0:T(8,128)S(1)} %get-tuple-element.39., ...), custom_call_target="tpu_custom_call" | custom-call | tf_op jit(solution)/shard_map/pallas_call | solution.py:693
  43.3 25.9 %all_to_all.10.gathered_b = f32[32,2,8,128]{3,2,1,0:T(8,128)S(1)} all-to-all(f32[32,2,8,128]{3,2,1,0:T(8,128)S(1)} %get-tuple-element.45), channel_id=1, replica_groups=mesh['gx'=8,'gy'=4] {'gx','gy'}, dimensions={0} | all-to-all | bytes 524288 | tf_op jit(solution)/shard_map/all_to_all | solution.py:760
  69.2 7.2 %shard_map.43 = f32[16,32,256]{2,1,0:T(8,128)} custom-call(f32[32,2,8,128]{3,2,1,0:T(8,128)S(1)} %all_to_all.10.gathered_b, f32[32,2,8,128]{3,2,1,0:T(8,128)S(1)} %all-to-all-done.done.gathered_c, f32[24,4,1,8,128]{4,3,2,1,0:T(8,128)S(1)} %get-tuple-element.46.v1, f32[24,4,1,8,128]{4,3,2,1,0:T(8,128)S(1)} %get-tuple-element.47.wx1, ...), custom_call_target="tpu_custom_call" | custom-call | tf_op jit(solution)/shard_map/pallas_call | solution.py:771
  (1 shorter events, 0.0 us)
Async XLA Ops:
  1.3 20.3 %collective-permute-start = (f32[11,32,256]{2,1,0:T(8,128)S(1)}, f32[11,32,256]{2,1,0:T(8,128)S(1)}, u32[]{:S(2)}, u32[]{:S(2)}) collective-permute-start(f32[11,32,256]{2,1,0:T(8,128)S(1)} %get-tuple-element.32), channel_id=1, source_target_pairs={{0,4},{4,0},{8,12},{12,8},{16,20},{20,16},{24,28},{28,24},{1,5},{5... | collective-permute-start | bytes 1081352 | tf_op jit(solution)/shard_map/ppermute | solution.py:712
  4.3 17.3 %collective-permute-start.1 = (f32[11,32,256]{2,1,0:T(8,128)S(1)}, f32[11,32,256]{2,1,0:T(8,128)S(1)}, u32[]{:S(2)}, u32[]{:S(2)}) collective-permute-start(f32[11,32,256]{2,1,0:T(8,128)S(1)} %get-tuple-element.33), channel_id=1, source_target_pairs={{4,8},{8,4},{12,16},{16,12},{20,24},{24,20},{5,9},{9,5},{13,17},{1... | collective-permute-start | bytes 1081352 | tf_op jit(solution)/shard_map/ppermute | solution.py:712
  7.5 18.2 %all-to-all-start = ((f32[32,2,8,128]{3,2,1,0:T(8,128)}), f32[32,2,8,128]{3,2,1,0:T(8,128)S(1)}, u32[]{:S(2)}, u32[]{:S(2)}) async-start(f32[32,2,8,128]{3,2,1,0:T(8,128)} %get-tuple-element.38), calls=%async_computation | async-start | bytes 524288 | tf_op jit(solution)/shard_map/all_to_all | solution.py:734
  21.6 4.1 %collective-permute-start.2 = (f32[70,4,256]{2,1,0:T(4,128)S(1)}, f32[70,4,256]{2,1,0:T(4,128)S(1)}, u32[]{:S(2)}, u32[]{:S(2)}) collective-permute-start(f32[70,4,256]{2,1,0:T(4,128)S(1)} %get-tuple-element.36), channel_id=1, source_target_pairs={{0,1},{1,0},{2,3},{3,2},{4,5},{5,4},{6,7},{7,6},{8,9},{9,8},{10,11... | collective-permute-start | bytes 860168 | tf_op jit(solution)/shard_map/ppermute | solution.py:712
  21.7 4.0 %collective-permute-start.3 = (f32[70,4,256]{2,1,0:T(4,128)S(1)}, f32[70,4,256]{2,1,0:T(4,128)S(1)}, u32[]{:S(2)}, u32[]{:S(2)}) collective-permute-start(f32[70,4,256]{2,1,0:T(4,128)S(1)} %get-tuple-element.37), channel_id=1, source_target_pairs={{1,2},{2,1},{5,6},{6,5},{9,10},{10,9},{13,14},{14,13},{17,18},{18,... | collective-permute-start | bytes 860168 | tf_op jit(solution)/shard_map/ppermute | solution.py:712
  30.2 6.0 %collective-permute-start.4 = (f32[27,16,128]{2,1,0:T(8,128)S(1)}, f32[27,16,128]{2,1,0:T(8,128)S(1)}, u32[]{:S(2)}, u32[]{:S(2)}) collective-permute-start(f32[27,16,128]{2,1,0:T(8,128)S(1)} %get-tuple-element.40), channel_id=1, source_target_pairs={{0,4},{4,0},{8,12},{12,8},{16,20},{20,16},{24,28},{28,24},{1,5},{5... | collective-permute-start | bytes 663560 | tf_op jit(solution)/shard_map/ppermute | solution.py:712
  31.1 5.0 %collective-permute-start.5 = (f32[27,16,128]{2,1,0:T(8,128)S(1)}, f32[27,16,128]{2,1,0:T(8,128)S(1)}, u32[]{:S(2)}, u32[]{:S(2)}) collective-permute-start(f32[27,16,128]{2,1,0:T(8,128)S(1)} %get-tuple-element.41), channel_id=1, source_target_pairs={{4,8},{8,4},{12,16},{16,12},{20,24},{24,20},{5,9},{9,5},{13,17},{1... | collective-permute-start | bytes 663560 | tf_op jit(solution)/shard_map/ppermute | solution.py:712
  36.2 6.1 %collective-permute-start.6 = (f32[68,8,128]{2,1,0:T(8,128)S(1)}, f32[68,8,128]{2,1,0:T(8,128)S(1)}, u32[]{:S(2)}, u32[]{:S(2)}) collective-permute-start(f32[68,8,128]{2,1,0:T(8,128)S(1)} %get-tuple-element.43), channel_id=1, source_target_pairs={{0,1},{1,0},{2,3},{3,2},{4,5},{5,4},{6,7},{7,6},{8,9},{9,8},{10,11... | collective-permute-start | bytes 835592 | tf_op jit(solution)/shard_map/ppermute | solution.py:712
  41.1 1.2 %collective-permute-start.7 = (f32[68,8,128]{2,1,0:T(8,128)S(1)}, f32[68,8,128]{2,1,0:T(8,128)S(1)}, u32[]{:S(2)}, u32[]{:S(2)}) collective-permute-start(f32[68,8,128]{2,1,0:T(8,128)S(1)} %get-tuple-element.44), channel_id=1, source_target_pairs={{1,2},{2,1},{5,6},{6,5},{9,10},{10,9},{13,14},{14,13},{17,18},{18,... | collective-permute-start | bytes 835592 | tf_op jit(solution)/shard_map/ppermute | solution.py:712

commit v4 on v3

--- a/solution.py
+++ b/solution.py
@@ -6,7 +6,7 @@
 from jax import lax
 from jax.experimental import pallas as pl
 from jax.experimental.pallas import tpu as pltpu
-from jax.sharding import PartitionSpec as P
+from jax.sharding import Mesh, PartitionSpec as P
 
 LEVELS = 4
 SWEEPS = 3
@@ -19,9 +19,11 @@
 F32 = jnp.float32
 LANES = 128
 FINE = SWEEPS + 1
+WIDTHS = (FINE - 1, FINE - 1, FINE)
 COARSE = 8
 SOURCE = COARSE - 1
 POST = SWEEPS
+SENT = POST - 1
 BLOCK = 24
 SPARE = 4 * 1024 * 1024
 
@@ -40,6 +42,9 @@
 
 def roll(x, by, axis):
     return pltpu.roll(x, by % x.shape[axis], axis)
+
+
+GX, GY = "gx", ("gy_far", "gy_near")
 
 
 def is_even(axis):
@@ -193,12 +198,16 @@
 def edge_kernel(guess0, guess1, source0, source1, coef0, coef1, first, second):
     def write(up, down):
         at = 0
-        for lower, upper, width in ((guess0, guess1, FINE), (source0, source1, FINE - 1), (coef0, coef1, FINE)):
+        for lower, upper, width in zip((guess0, source0, coef0), (guess1, source1, coef1), WIDTHS):
             up[at:at + width] = upper[FINE - width:]
             down[at:at + width] = lower[:width]
             at += width
-
-    address("gx", first, second, write)
+        far = WIDTHS[0]
+        up[far] = source1[1] + 0.5 * (coef1[1] + coef1[0]) * guess1[0]
+        far += WIDTHS[1] - 1
+        down[far] = source0[FINE - 2] + 0.5 * (coef0[FINE - 2] + coef0[FINE - 1]) * guess0[FINE - 1]
+
+    address(GX, first, second, write)
 
 
 def own_kernel(guess, source, coef, up, down, c1, send, *pairs):
@@ -228,14 +237,21 @@
         send[d] = c2
 
 
+def keep_kernel(guess, source, coef, *rest):
+    guess_out, source_out, coef_out = rest[-3:]
+    guess_out[...] = guess[...]
+    source_out[...] = source[...]
+    coef_out[...] = coef[...]
+
+
 def corner_kernel(own_up, own_down, one, two, first, second):
     nx = own_up.shape[0] // 3
-    sides = Sides("gx", one, two)
+    sides = Sides(GX, one, two)
     ny = one.shape[1]
 
     def write(up, down):
         at = base = 0
-        for which, width in enumerate((FINE, FINE - 1, FINE)):
+        for which, width in enumerate(WIDTHS):
             for k in range(width):
                 for message, slot in ((sides.low, at + k), (sides.high, at + width + nx + k)):
                     up[slot] = message(base + k, pl.ds(ny - FINE, FINE))
@@ -246,24 +262,25 @@
             at += nx + 2 * width
             base += width
 
-    address("gy", first, second, write)
-
-
-def fine_pre_kernel(guess, source, coef, c1, one, two, three, four, done,
+    address(GY, first, second, write)
+
+
+def fine_pre_kernel(guess, source, coef, c1, one, two, three, four,
                     out, wx, wy, wz, gain, scaled, first, second, b1,
                     field, force, c, v, w, total, *pairs):
     nx, ny, nz = guess.shape
-    across, beside = Sides("gx", one, two), Sides("gy", three, four)
+    across, beside = Sides(GX, one, two), Sides(GY, three, four)
     pieces = nz // LANES
     rows = ny + 2 * FINE
     count = rows // 8
     planes0 = nx + 2 * FINE
     level = (wx, wy, wz, gain, scaled, total)
 
-    def fill(target, own, base, width):
+    def fill(target, own, which):
+        width = WIDTHS[which]
         at = FINE - width
-        offset = sum(nx + 2 * k for k in base)
-        message = sum(base)
+        offset = sum(nx + 2 * k for k in WIDTHS[:which])
+        message = sum(WIDTHS[:which])
 
         def rest(k):
             side = jnp.concatenate((beside.high(offset + k), beside.low(offset + k)), 0)
@@ -286,9 +303,9 @@
     def spaced(ref):
         return lambda p, j, t: ref[p, t, pl.ds(j, 8, stride=count), :]
 
-    fill(field, guess, (), FINE)
-    fill(force, source, (FINE,), FINE - 1)
-    fill(c, coef, (FINE, FINE - 1), FINE)
+    fill(field, guess, 0)
+    fill(force, source, 1)
+    fill(c, coef, 2)
     def arrange(p):
         for j in range(count):
             for t in range(pieces):
@@ -302,7 +319,12 @@
             for t in range(pieces):
                 v[p, j, t] = spaced(field)(p, j, t)
 
-    planes(0, planes0, arrange_field)
+    planes(1, planes0 - 1, arrange_field)
+    for p, face in ((0, 1), (planes0 - 1, planes0 - 1)):
+        for j in range(count):
+            for t in range(pieces):
+                v[p, j, t] = jnp.zeros((8, LANES), F32)
+                wx[face, j, t] = jnp.zeros((8, LANES), F32)
     sweep(reader(v), w, level, 1, planes0 - 1)
     sweep(reader(w), v, level, 2, planes0 - 2)
     sweep(reader(v), w, level, 3, planes0 - 3)
@@ -310,10 +332,10 @@
     def put(k):
         for t in range(pieces):
             for j in range(count):
-                field[k, t, pl.ds(j, 8, stride=count), :] = w[FINE + k, j, t]
+                field[k, t, pl.ds(j, 8, stride=count), :] = w[FINE - 1 + k, j, t]
             out[k, :, t * LANES:(t + 1) * LANES] = field[k, t, :ny]
 
-    planes(0, nx, put)
+    planes(0, nx + 2, put)
 
     n1, r1 = nx // 2, ny // 2
 
@@ -338,21 +360,21 @@
         up[SOURCE:SOURCE + COARSE] = c1[n1 - COARSE:]
         down[SOURCE:SOURCE + COARSE] = c1[:COARSE]
         at = SOURCE + COARSE
-        for k in range(POST):
+        for k in range(SENT):
             for i in range(2):
                 for j in range(2):
                     here, lanes = pl.ds(i * r1, r1), pl.ds(j * (nz // 2), nz // 2)
-                    up[at] = out[nx - POST + k, here, lanes]
-                    down[at] = out[k, here, lanes]
+                    up[at] = out[nx - POST + 1 + k, here, lanes]
+                    down[at] = out[2 + k, here, lanes]
                     at += 1
 
-    address("gx", first, second, write)
+    address(GX, first, second, write)
 
 
 def rows_kernel(b1, c1, v, one, two, first, second):
     n1, r1, half = b1.shape
     nx, ny = 2 * n1, 2 * r1
-    sides = Sides("gx", one, two)
+    sides = Sides(GX, one, two)
 
     def write(up, down):
         def edge(take, at):
@@ -371,15 +393,15 @@
         for j in range(2):
             rows, lanes = pl.ds(j * FINE, FINE), pl.ds(j * half, half)
             last, start = pl.ds(r1 - FINE, FINE), pl.ds(0, FINE)
-            for k in range(POST):
-                for message, slot in ((sides.low, at + k), (sides.high, at + POST + nx + k)):
+            for k in range(SENT):
+                for message, slot in ((sides.low, at + k), (sides.high, at + SENT + nx + 2 + k)):
                     up[slot, rows, :] = message(base + 4 * k + 2 + j, last)
                     down[slot, rows, :] = message(base + 4 * k + j, start)
-            for k in range(nx):
-                up[at + POST + k, rows, :] = v[k, ny - FINE:, lanes]
-                down[at + POST + k, rows, :] = v[k, :FINE, lanes]
-
-    address("gy", first, second, write)
+            for k in range(nx + 2):
+                up[at + SENT + k, rows, :] = v[k, ny - FINE:, lanes]
+                down[at + SENT + k, rows, :] = v[k, :FINE, lanes]
+
+    address(GY, first, second, write)
 
 
 def coarse_pre_kernel(b1, c1, one, two, three, four,
@@ -390,7 +412,7 @@
     planes1 = n1 + 2 * COARSE
     scale = 0.25
     level = (wx, wy, wz, gain, scaled, total)
-    across, beside = Sides("gx", one, two), Sides("gy", three, four)
+    across, beside = Sides(GX, one, two), Sides(GY, three, four)
 
     def fill(target, own, base, offset, width):
         at = COARSE - width
@@ -445,7 +467,7 @@
     return (2 * block + group) * (depth // 2) + z // 2 == target
 
 
-def solve_kernel(gathered_b, gathered_c, v1, wx1, wy1, wz1, gain1, scaled1, v0, wx0, wy0, wz0, gain0, scaled0,
+def solve_kernel(mine_b, other_b, mine_c, other_c, v1, wx1, wy1, wz1, gain1, scaled1, v0, wx0, wy0, wz0, gain0, scaled0,
                  one, two, three, four, out,
                  c2, a2, y2, n2, l2x, l2y, l2z, l2g, l2s, l2t,
                  c3, b3, a3, y3, l3x, l3y, l3z, l3g, l3s, l3t,
@@ -454,8 +476,8 @@
     level2 = (l2x, l2y, l2z, l2g, l2s, l2t)
     level3 = (l3x, l3y, l3z, l3g, l3s, l3t)
     level4 = (l4x, l4y, l4z, l4g, l4s, None)
-    across, beside = Sides("gx", one, two), Sides("gy", three, four)
-    half, r2 = gathered_b.shape[1:3]
+    across, beside = Sides(GX, one, two), Sides(GY, three, four)
+    half, r2 = mine_b.shape[1:3]
     per = 2 * half
     m2, m3, m4 = c2.shape[0] - 2, c3.shape[0] - 2, c4.shape[0] - 2
     j2, j3, j4 = c2.shape[1], c3.shape[1], c4.shape[1]
@@ -464,12 +486,17 @@
     depth3, depth4 = depth2 // 2, depth2 // 4
     lane = iota((8, LANES), 1)
 
+    near_one = lax.axis_index(GY[1])
+
     def unpack(i):
         for j in range(gy):
             for k in range(half):
-                for which, gathered in enumerate((gathered_b, gathered_c)):
-                    near = gathered[i * gy + j, k]
-                    far = gathered[(i + gx // 2) * gy + j, k]
+                for which, (mine, other) in enumerate(((mine_b, other_b), (mine_c, other_c))):
+                    def block(x):
+                        at = x * (gy // 2) + j // 2
+                        return jnp.where(near_one == j % 2, mine[at, k], other[at, k])
+
+                    near, far = block(i), block(i + gx // 2)
                     here = pl.ds(j * r2, r2)
                     n2[which, i * per + k, here, :] = jnp.where(lane < depth2, near, roll(far, depth2, 1))
                     n2[which, i * per + half + k, here, :] = jnp.where(lane < depth2, roll(near, depth2, 1), far)
@@ -583,7 +610,7 @@
     x2, z2 = smooth(x2, z2, level2, depth2, SWEEPS)
 
     level1 = (wx1, wy1, wz1, gain1, scaled1, None)
-    at_x, at_y = lax.axis_index("gx"), lax.axis_index("gy")
+    at_x, at_y = lax.axis_index(GX), lax.axis_index(GY)
     planes1, count1, _, _, lanes1 = v1.shape
     n1, r1 = planes1 - 2 * COARSE, 8 * count1 - 2 * COARSE
     sub = iota((8, LANES), 0)
@@ -621,7 +648,7 @@
     sweep(reader(u1), t1, level1, COARSE - 2, COARSE + n1 + 2)
 
     level0 = (wx0, wy0, wz0, gain0, scaled0, None)
-    nx, ny, nz = v0.shape
+    nx, ny, nz = out.shape
     pieces = nz // LANES
     rows0 = ny + 2 * FINE
     count0 = rows0 // 8
@@ -649,10 +676,10 @@
                 q = p - FINE
                 if p < FINE - POST or q >= nx + POST:
                     continue
-                if 0 <= q < nx:
-                    own = v0[q, :, lanes]
+                if -1 <= q <= nx:
+                    own = v0[q + 1, :, lanes]
                 else:
-                    message, slot = (across.low, p - (FINE - POST)) if q < 0 else (across.high, q - nx)
+                    message, slot = (across.low, q + POST) if q < 0 else (across.high, q - nx - 1)
                     own = jnp.concatenate([message(base + 4 * slot + 2 * h + t) for h in range(2)], 0)
                 side = pl.ds(t * FINE, FINE)
                 at_side = beyond + p - (FINE - POST)
@@ -712,8 +739,13 @@
     return lax.ppermute(first, axis, even), lax.ppermute(second, axis, odd)
 
 
+def spread(send):
+    found = lax.all_to_all(send, (GX, GY[0]), 0, 0)
+    return found, lax.ppermute(found, GY[1], [(0, 1), (1, 0)])
+
+
 def body(guess, right_side, coefficient):
-    gx, gy = lax.axis_size("gx"), lax.axis_size("gy")
+    gx, gy = lax.axis_size(GX), lax.axis_size(GY)
     nx, ny, nz = guess.shape
     n1, r1, z1 = nx // 2, ny // 2, nz // 2
     n2, r2 = n1 // 2, r1 // 2
@@ -723,41 +755,46 @@
 
     ends = [pl.BlockSpec((FINE, ny, nz), lambda i, at=at: (at, 0, 0)) for at in (0, nx // FINE - 1)]
     across = swap(*call(
-        edge_kernel, (shape(3 * FINE - 1, ny, nz),) * 2, (), *(f for f in fields for _ in range(2)), specs=ends * 3
-    ), "gx")
+        edge_kernel, (shape(sum(WIDTHS), ny, nz),) * 2, (), *(f for f in fields for _ in range(2)), specs=ends * 3
+    ), GX)
     own_up, own_down, c1, send = call(
         own_kernel,
-        (shape(3 * nx, FINE, nz),) * 2 + (shape(n1, r1, z1), shape(gx * gy, n2 // 2, r2, LANES)),
+        (shape(3 * nx, FINE, nz),) * 2 + (shape(n1, r1, z1), shape(gx * gy // 2, n2 // 2, r2, LANES)),
         [vmem(n1 * ny, LANES)] * pieces,
         *fields, specs=[whole] * 3,
     )
-    gathered_c = lax.all_to_all(send, ("gx", "gy"), 0, 0)
-    corners = 3 * nx + 2 * (3 * FINE - 1)
-    beside = swap(*call(corner_kernel, (shape(corners, FINE, nz),) * 2, (), own_up, own_down, *across), "gy")
+    gathered_c = spread(send)
+    corners = 3 * nx + 2 * sum(WIDTHS)
+    rows = call(corner_kernel, (shape(corners, FINE, nz),) * 2, (), own_up, own_down, *across)
+    beside = swap(*rows, GY)
+    fields = call(
+        keep_kernel, (shape(nx, ny, nz),) * 3, (), *fields, gathered_c[1], rows[0],
+        specs=[whole] * 3 + [pl.BlockSpec(memory_space=pl.ANY)] * 2,
+    )
 
     block0 = (planes0, rows0 // 8, pieces, 8, LANES)
     plain0 = (planes0, pieces, rows0, LANES)
-    message = (SOURCE + COARSE + 4 * POST, r1, z1)
+    message = (SOURCE + COARSE + 4 * SENT, r1, z1)
     v0, *level0, first, second, b1 = call(
         fine_pre_kernel,
-        (shape(nx, ny, nz),) + (shape(*block0),) * 5 + (shape(*message),) * 2 + (shape(n1, r1, z1),),
+        (shape(nx + 2, ny, nz),) + (shape(*block0),) * 5 + (shape(*message),) * 2 + (shape(n1, r1, z1),),
         [vmem(*plain0)] * 3 + [vmem(*block0)] * 3 + [vmem(n1 * rows0, LANES)] * pieces,
-        *fields, c1, *across, *beside, gathered_c, specs=[whole] * 3 + [None] * 5 + [pl.BlockSpec(memory_space=pl.ANY)],
+        *fields, c1, *across, *beside, specs=[None] * 8,
     )
-    across = swap(first, second, "gx")
+    across = swap(first, second, GX)
     count = 3 * n1 + 2 * SOURCE + 2 * COARSE + 2 * POST + n1
-    beside = swap(*call(rows_kernel, (shape(count, COARSE, z1),) * 2, (), b1, c1, v0, *across), "gy")
+    beside = swap(*call(rows_kernel, (shape(count, COARSE, z1),) * 2, (), b1, c1, v0, *across), GY)
 
     planes1, rows1 = n1 + 2 * COARSE, r1 + 2 * COARSE
     block1 = (planes1, rows1 // 8, 1, 8, z1)
     plain1 = (planes1, rows1, z1)
     v1, *level1, send = call(
         coarse_pre_kernel,
-        (shape(*block1),) * 6 + (shape(gx * gy, n2 // 2, r2, LANES),),
+        (shape(*block1),) * 6 + (shape(gx * gy // 2, n2 // 2, r2, LANES),),
         [vmem(*plain1)] * 2 + [vmem(*block1)] * 2 + [vmem(n2 // 2 * r2, LANES)] * 2,
         b1, c1, *across, *beside,
     )
-    gathered_b = lax.all_to_all(send, ("gx", "gy"), 0, 0)
+    gathered_b = spread(send)
 
     m2, rows2 = gx * n2 // 2, gy * r2
     m3, m4 = m2 // 4, m2 // 16
@@ -771,20 +808,22 @@
     (out,) = pl.pallas_call(
         partial(solve_kernel, gx=gx, gy=gy),
         out_shape=(jax.ShapeDtypeStruct((nx, ny, nz), F32),),
-        in_specs=[whole] * 18,
+        in_specs=[whole] * 20,
         out_specs=(whole,),
         scratch_shapes=scratch,
         compiler_params=limit(scratch, guess.size * 4),
     )(*(pltpu.with_memory_space_constraint(x, pltpu.VMEM)
-        for x in (gathered_b, gathered_c, v1, *level1, v0, *level0, *across, *beside)))
+        for x in (*gathered_b, *gathered_c, v1, *level1, v0, *level0, *across, *beside)))
     return out
 
 
 def solution(mesh):
+    gx, gy = mesh.devices.shape
+    mesh = Mesh(mesh.devices.reshape(gx, gy // 2, 2), (GX, *GY))
     return jax.shard_map(
         body,
         mesh=mesh,
-        in_specs=(P("gx", "gy", None), P("gx", "gy", None), P("gx", "gy", None)),
-        out_specs=P("gx", "gy", None),
+        in_specs=(P(GX, GY, None),) * 3,
+        out_specs=P(GX, GY, None),
         check_vma=False,
     )

time: 76.7 us -> 72.8 us (0.949)
  blocking collectives: 25.9 us -> 20.5 us
  starting transfers between devices: 19.2 us -> 21.8 us
  waiting for transfers between devices: 14.7 us -> 12.8 us
    all_to_all x1, blocking collectives: 25.9 us -> 20.5 us  [spread(): found = lax.all_to_all(send, (GX, GY[0]), 0, 0)]
    ppermute x0 -> x2, waiting for transfers between devices: none -> 2.69 us  [spread(): return (found, lax.ppermute(found, GY[1], [(0, 1), (1, 0)]))]
    ppermute x8, waiting for transfers between devices: 11.3 us -> 8.78 us  [swap(): return (lax.ppermute(first, axis, even), lax.ppermute(second, axis, odd))]
    all_to_all x1, waiting for transfers between devices: 3.35 us -> 1.37 us  [spread(): found = lax.all_to_all(send, (GX, GY[0]), 0, 0)]
    ppermute x8, starting transfers between devices: 11.6 us -> 13.2 us  [swap(): return (lax.ppermute(first, axis, even), lax.ppermute(second, axis, odd))]
    all_to_all x1, starting transfers between devices: 7.61 us -> 8.63 us  [spread(): found = lax.all_to_all(send, (GX, GY[0]), 0, 0)]
    pallas_call x6 -> x7, Pallas kernels: 9.32 us -> 9.7 us  [call(): pl.pallas_call(kernel, grid=(1,) if any((spec and spec.block_shape for sp...]
  transfers between devices with their start and end apart: 9 -> 11, of which waited for: 4 -> 6; matrix products, arithmetic and copies ran while one was open for 0% -> 0% of each run, Pallas kernels for 3% -> 6%
where the time goes in v4:
time: 72.8 us; the launch traced here: 72.4 us
  starting transfers between devices  21.8 us (30%)
  blocking collectives  20.5 us (28%)
  Pallas kernels  17.2 us (24%)
  waiting for transfers between devices  12.8 us (18%)
    all_to_all x1, blocking collectives, spread(): found = lax.all_to_all(send, (GX, GY[0]), 0, 0)  20.5 us
    ppermute x8, starting transfers between devices, swap(): return (lax.ppermute(first, axis, even), lax.ppermute(second, axis, odd))  13.2 us
    pallas_call x7, Pallas kernels, call(): pl.pallas_call(kernel, grid=(1,) if any((spec and spec.block_shape for sp...  9.7 us
    ppermute x8, waiting for transfers between devices, swap(): return (lax.ppermute(first, axis, even), lax.ppermute(second, axis, odd))  8.78 us
    all_to_all x1, starting transfers between devices, spread(): found = lax.all_to_all(send, (GX, GY[0]), 0, 0)  8.63 us
    pallas_call x1, Pallas kernels, body(): pl.pallas_call(partial(solve_kernel, gx=gx, gy=gy), out_shape=(jax.ShapeD...  7.52 us
    ppermute x2, waiting for transfers between devices, spread(): return (found, lax.ppermute(found, GY[1], [(0, 1), (1, 0)]))  2.69 us
  transfers between devices with their start and end apart: 11, of which 6 were waited for; matrix products, arithmetic and copies ran while one was open for 0% of the time, Pallas kernels for 6%

profile of v4, /device:TPU:0, one launch (start us, length us, event | category | flops | bytes accessed | tf_op | source)
XLA Modules:
  0.0 72.4 jit_solution(17785397355055876613)
XLA Ops:
  0.0 1.2 %shard_map.38 = (f32[10,32,256]{2,1,0:T(8,128)S(1)}, f32[10,32,256]{2,1,0:T(8,128)S(1)}) custom-call(f32[16,32,256]{2,1,0:T(8,128)} %guess.3, f32[16,32,256]{2,1,0:T(8,128)} %guess.3, f32[16,32,256]{2,1,0:T(8,128)} %source.3, f32[16,32,256]{2,1,0:T(8,128)} %source.3, f32[16,32,256]{2,1,0:T(8,128)} %coef.3, f32[16,32,256]{2,1,0:T(8,128)} %coef.3), custom_call_target="tpu_custom_call" | custom-call | tf_op jit(solution)/shard_map/pallas_call | solution.py:720
  1.3 3.0 %collective-permute-start.1 = (f32[10,32,256]{2,1,0:T(8,128)S(1)}, f32[10,32,256]{2,1,0:T(8,128)S(1)}, u32[]{:S(2)}, u32[]{:S(2)}) collective-permute-start(f32[10,32,256]{2,1,0:T(8,128)S(1)} %get-tuple-element.37), channel_id=1, source_target_pairs={{0,4},{4,0},{8,12},{12,8},{16,20},{20,16},{24,28},{28,24},{1,5},{5... | collective-permute-start | bytes 983048 | tf_op jit(solution)/shard_map/ppermute | solution.py:739
  4.3 0.7 collective-permute-start.2
  4.9 2.5 %shard_map.37 = (f32[48,4,256]{2,1,0:T(4,128)S(1)}, f32[48,4,256]{2,1,0:T(4,128)S(1)}, f32[8,16,128]{2,1,0:T(8,128)S(1)}, f32[16,2,8,128]{3,2,1,0:T(8,128)}) custom-call(f32[16,32,256]{2,1,0:T(8,128)} %guess.3, f32[16,32,256]{2,1,0:T(8,128)} %source.3, f32[16,32,256]{2,1,0:T(8,128)} %coef.3), custom_call_target="tpu_custom_call" | custom-call | tf_op jit(solution)/shard_map/pallas_call | solution.py:720
  7.4 8.6 %all-to-all-start = ((f32[16,2,8,128]{3,2,1,0:T(8,128)}), f32[16,2,8,128]{3,2,1,0:T(8,128)S(1)}, u32[]{:S(2)}, u32[]{:S(2)}) async-start(f32[16,2,8,128]{3,2,1,0:T(8,128)} %get-tuple-element.34), calls=%async_computation | async-start | bytes 262144 | tf_op jit(solution)/shard_map/all_to_all | solution.py:743
  16.1 2.7 %collective-permute-done.1.one = f32[10,32,256]{2,1,0:T(8,128)S(1)} collective-permute-done((f32[10,32,256]{2,1,0:T(8,128)S(1)}, f32[10,32,256]{2,1,0:T(8,128)S(1)}, u32[]{:S(2)}, u32[]{:S(2)}) %collective-permute-start.1) | collective-permute-done | bytes 327712 | tf_op jit(solution)/shard_map/ppermute | solution.py:739
  18.8 0.0 collective-permute-done.2.two
  18.9 0.7 collective-permute-start.4
  19.6 2.9 %collective-permute-start.3 = (f32[68,4,256]{2,1,0:T(4,128)S(1)}, f32[68,4,256]{2,1,0:T(4,128)S(1)}, u32[]{:S(2)}, u32[]{:S(2)}) collective-permute-start(f32[68,4,256]{2,1,0:T(4,128)S(1)} %get-tuple-element.39.rest_1_), channel_id=1, source_target_pairs={{0,1},{1,0},{2,3},{3,2},{4,5},{5,4},{6,7},{7,6},{8,9},{9,8},{10,11... | collective-permute-start | bytes 835592 | tf_op jit(solution)/shard_map/ppermute | solution.py:739
  22.5 1.4 %all-to-all-done.mine_c = f32[16,2,8,128]{3,2,1,0:T(8,128)S(1)} async-done(((f32[16,2,8,128]{3,2,1,0:T(8,128)}), f32[16,2,8,128]{3,2,1,0:T(8,128)S(1)}, u32[]{:S(2)}, u32[]{:S(2)}) %all-to-all-start) | async-done | bytes 131104 | tf_op jit(solution)/shard_map/all_to_all | solution.py:743
  23.9 0.0 collective-permute-start
  23.9 1.3 %collective-permute-done.rest_0_.other_c = f32[16,2,8,128]{3,2,1,0:T(8,128)S(1)} collective-permute-done((f32[16,2,8,128]{3,2,1,0:T(8,128)S(1)}, f32[16,2,8,128]{3,2,1,0:T(8,128)S(1)}, u32[]{:S(2)}, u32[]{:S(2)}) %collective-permute-start) | collective-permute-done | bytes 131104 | tf_op jit(solution)/shard_map/ppermute | solution.py:744
  25.2 1.5 %shard_map.40 = (f32[16,32,256]{2,1,0:T(8,128)S(1)}, f32[16,32,256]{2,1,0:T(8,128)S(1)}, f32[16,32,256]{2,1,0:T(8,128)S(1)}) custom-call(f32[16,32,256]{2,1,0:T(8,128)} %guess.3, f32[16,32,256]{2,1,0:T(8,128)} %source.3, f32[16,32,256]{2,1,0:T(8,128)} %coef.3, f32[16,2,8,128]{3,2,1,0:T(8,128)S(1)} %collective-permute-done.rest_0_.other_c, ...), custom_call_target="tpu_custom_call" | custom-call | tf_op jit(solution)/shard_map/pallas_call | solution.py:720
  26.7 0.0 collective-permute-done.4.four
  26.7 0.0 collective-permute-done.3.three
  26.7 3.4 %shard_map.41 = (f32[18,32,256]{2,1,0:T(8,128)S(1)}, f32[24,5,2,8,128]{4,3,2,1,0:T(8,128)S(1)}, f32[24,5,2,8,128]{4,3,2,1,0:T(8,128)S(1)}, f32[24,5,2,8,128]{4,3...) custom-call(f32[16,32,256]{2,1,0:T(8,128)S(1)} %get-tuple-element.40, ...), custom_call_target="tpu_custom_call" | custom-call | tf_op jit(solution)/shard_map/pallas_call | solution.py:720
  30.1 1.4 %collective-permute-start.5 = (f32[23,16,128]{2,1,0:T(8,128)S(1)}, f32[23,16,128]{2,1,0:T(8,128)S(1)}, u32[]{:S(2)}, u32[]{:S(2)}) collective-permute-start(f32[23,16,128]{2,1,0:T(8,128)S(1)} %get-tuple-element.46), channel_id=1, source_target_pairs={{0,4},{4,0},{8,12},{12,8},{16,20},{20,16},{24,28},{28,24},{1,5},{5... | collective-permute-start | bytes 565256 | tf_op jit(solution)/shard_map/ppermute | solution.py:739
  31.6 0.7 collective-permute-start.6
  32.2 5.5 %collective-permute-done.5.one = f32[23,16,128]{2,1,0:T(8,128)S(1)} collective-permute-done((f32[23,16,128]{2,1,0:T(8,128)S(1)}, f32[23,16,128]{2,1,0:T(8,128)S(1)}, u32[]{:S(2)}, u32[]{:S(2)}) %collective-permute-start.5) | collective-permute-done | bytes 188448 | tf_op jit(solution)/shard_map/ppermute | solution.py:739
  37.8 0.0 collective-permute-done.6.two
  37.8 0.1 shard_map.42
  37.8 3.2 %collective-permute-start.7 = (f32[68,8,128]{2,1,0:T(8,128)S(1)}, f32[68,8,128]{2,1,0:T(8,128)S(1)}, u32[]{:S(2)}, u32[]{:S(2)}) collective-permute-start(f32[68,8,128]{2,1,0:T(8,128)S(1)} %get-tuple-element.49), channel_id=1, source_target_pairs={{0,1},{1,0},{2,3},{3,2},{4,5},{5,4},{6,7},{7,6},{8,9},{9,8},{10,11... | collective-permute-start | bytes 835592 | tf_op jit(solution)/shard_map/ppermute | solution.py:739
  41.0 0.7 collective-permute-start.8
  41.6 0.5 collective-permute-done.7.three
  42.2 0.0 collective-permute-done.8.four
  42.2 0.9 %shard_map.43 = (f32[24,4,1,8,128]{4,3,2,1,0:T(8,128)S(1)}, f32[24,4,1,8,128]{4,3,2,1,0:T(8,128)S(1)}, f32[24,4,1,8,128]{4,3,2,1,0:T(8,128)S(1)}, f32[24,4,1,8,1...) custom-call(f32[8,16,128]{2,1,0:T(8,128)S(1)} %get-tuple-element.45., ...), custom_call_target="tpu_custom_call" | custom-call | tf_op jit(solution)/shard_map/pallas_call | solution.py:720
  43.1 20.5 %all_to_all.10.mine_b = f32[16,2,8,128]{3,2,1,0:T(8,128)S(1)} all-to-all(f32[16,2,8,128]{3,2,1,0:T(8,128)S(1)} %get-tuple-element.51), channel_id=1, replica_groups=mesh['gx'=8,'gy_far'=2,'gy_near'=2] {'gx','gy_far'}, dimensions={0} | all-to-all | bytes 262144 | tf_op jit(solution)/shard_map/all_to_all | solution.py:743
  63.6 0.0 collective-permute-start.9
  63.6 1.3 %collective-permute-done.9.other_b = f32[16,2,8,128]{3,2,1,0:T(8,128)S(1)} collective-permute-done((f32[16,2,8,128]{3,2,1,0:T(8,128)S(1)}, f32[16,2,8,128]{3,2,1,0:T(8,128)S(1)}, u32[]{:S(2)}, u32[]{:S(2)}) %collective-permute-start.9) | collective-permute-done | bytes 131104 | tf_op jit(solution)/shard_map/ppermute | solution.py:744
  64.9 7.5 %shard_map.44 = f32[16,32,256]{2,1,0:T(8,128)} custom-call(f32[16,2,8,128]{3,2,1,0:T(8,128)S(1)} %all_to_all.10.mine_b, f32[16,2,8,128]{3,2,1,0:T(8,128)S(1)} %collective-permute-done.9.other_b, f32[16,2,8,128]{3,2,1,0:T(8,128)S(1)} %all-to-all-done.mine_c, f32[16,2,8,128]{3,2,1,0:T(8,128)S(1)} %collective-permute-done.rest_0_.other_c, ...), custom_call_target="tpu_custom_call" | custom-call | tf_op jit(solution)/shard_map/pallas_call | solution.py:808
  (1 shorter events, 0.0 us)
Async XLA Ops:
  1.3 17.6 %collective-permute-start.1 = (f32[10,32,256]{2,1,0:T(8,128)S(1)}, f32[10,32,256]{2,1,0:T(8,128)S(1)}, u32[]{:S(2)}, u32[]{:S(2)}) collective-permute-start(f32[10,32,256]{2,1,0:T(8,128)S(1)} %get-tuple-element.37), channel_id=1, source_target_pairs={{0,4},{4,0},{8,12},{12,8},{16,20},{20,16},{24,28},{28,24},{1,5},{5... | collective-permute-start | bytes 983048 | tf_op jit(solution)/shard_map/ppermute | solution.py:739
  4.3 14.6 %collective-permute-start.2 = (f32[10,32,256]{2,1,0:T(8,128)S(1)}, f32[10,32,256]{2,1,0:T(8,128)S(1)}, u32[]{:S(2)}, u32[]{:S(2)}) collective-permute-start(f32[10,32,256]{2,1,0:T(8,128)S(1)} %get-tuple-element.38), channel_id=1, source_target_pairs={{4,8},{8,4},{12,16},{16,12},{20,24},{24,20},{5,9},{9,5},{13,17},{1... | collective-permute-start | bytes 983048 | tf_op jit(solution)/shard_map/ppermute | solution.py:739
  7.4 16.4 %all-to-all-start = ((f32[16,2,8,128]{3,2,1,0:T(8,128)}), f32[16,2,8,128]{3,2,1,0:T(8,128)S(1)}, u32[]{:S(2)}, u32[]{:S(2)}) async-start(f32[16,2,8,128]{3,2,1,0:T(8,128)} %get-tuple-element.34), calls=%async_computation | async-start | bytes 262144 | tf_op jit(solution)/shard_map/all_to_all | solution.py:743
  18.9 7.8 %collective-permute-start.4 = (f32[68,4,256]{2,1,0:T(4,128)S(1)}, f32[68,4,256]{2,1,0:T(4,128)S(1)}, u32[]{:S(2)}, u32[]{:S(2)}) collective-permute-start(f32[68,4,256]{2,1,0:T(4,128)S(1)} %get-tuple-element.44), channel_id=1, source_target_pairs={{1,2},{2,1},{5,6},{6,5},{9,10},{10,9},{13,14},{14,13},{17,18},{18,... | collective-permute-start | bytes 835592 | tf_op jit(solution)/shard_map/ppermute | solution.py:739
  19.6 7.1 %collective-permute-start.3 = (f32[68,4,256]{2,1,0:T(4,128)S(1)}, f32[68,4,256]{2,1,0:T(4,128)S(1)}, u32[]{:S(2)}, u32[]{:S(2)}) collective-permute-start(f32[68,4,256]{2,1,0:T(4,128)S(1)} %get-tuple-element.39.rest_1_), channel_id=1, source_target_pairs={{0,1},{1,0},{2,3},{3,2},{4,5},{5,4},{6,7},{7,6},{8,9},{9,8},{10,11... | collective-permute-start | bytes 835592 | tf_op jit(solution)/shard_map/ppermute | solution.py:739
  23.9 1.3 %collective-permute-start = (f32[16,2,8,128]{3,2,1,0:T(8,128)S(1)}, f32[16,2,8,128]{3,2,1,0:T(8,128)S(1)}, u32[]{:S(2)}, u32[]{:S(2)}) collective-permute-start(f32[16,2,8,128]{3,2,1,0:T(8,128)S(1)} %all-to-all-done.mine_c), channel_id=1, source_target_pairs={{0,1},{1,0},{2,3},{3,2},{4,5},{5,4},{6,7},{7,6},{8,9},{9,8},{10,11... | collective-permute-start | bytes 393224 | tf_op jit(solution)/shard_map/ppermute | solution.py:744
  30.1 7.6 %collective-permute-start.5 = (f32[23,16,128]{2,1,0:T(8,128)S(1)}, f32[23,16,128]{2,1,0:T(8,128)S(1)}, u32[]{:S(2)}, u32[]{:S(2)}) collective-permute-start(f32[23,16,128]{2,1,0:T(8,128)S(1)} %get-tuple-element.46), channel_id=1, source_target_pairs={{0,4},{4,0},{8,12},{12,8},{16,20},{20,16},{24,28},{28,24},{1,5},{5... | collective-permute-start | bytes 565256 | tf_op jit(solution)/shard_map/ppermute | solution.py:739
  31.6 6.2 %collective-permute-start.6 = (f32[23,16,128]{2,1,0:T(8,128)S(1)}, f32[23,16,128]{2,1,0:T(8,128)S(1)}, u32[]{:S(2)}, u32[]{:S(2)}) collective-permute-start(f32[23,16,128]{2,1,0:T(8,128)S(1)} %get-tuple-element.47), channel_id=1, source_target_pairs={{4,8},{8,4},{12,16},{16,12},{20,24},{24,20},{5,9},{9,5},{13,17},{1... | collective-permute-start | bytes 565256 | tf_op jit(solution)/shard_map/ppermute | solution.py:739
  37.8 4.3 %collective-permute-start.7 = (f32[68,8,128]{2,1,0:T(8,128)S(1)}, f32[68,8,128]{2,1,0:T(8,128)S(1)}, u32[]{:S(2)}, u32[]{:S(2)}) collective-permute-start(f32[68,8,128]{2,1,0:T(8,128)S(1)} %get-tuple-element.49), channel_id=1, source_target_pairs={{0,1},{1,0},{2,3},{3,2},{4,5},{5,4},{6,7},{7,6},{8,9},{9,8},{10,11... | collective-permute-start | bytes 835592 | tf_op jit(solution)/shard_map/ppermute | solution.py:739
  41.0 1.2 %collective-permute-start.8 = (f32[68,8,128]{2,1,0:T(8,128)S(1)}, f32[68,8,128]{2,1,0:T(8,128)S(1)}, u32[]{:S(2)}, u32[]{:S(2)}) collective-permute-start(f32[68,8,128]{2,1,0:T(8,128)S(1)} %get-tuple-element.50), channel_id=1, source_target_pairs={{1,2},{2,1},{5,6},{6,5},{9,10},{10,9},{13,14},{14,13},{17,18},{18,... | collective-permute-start | bytes 835592 | tf_op jit(solution)/shard_map/ppermute | solution.py:739
  63.6 1.3 %collective-permute-start.9 = (f32[16,2,8,128]{3,2,1,0:T(8,128)S(1)}, f32[16,2,8,128]{3,2,1,0:T(8,128)S(1)}, u32[]{:S(2)}, u32[]{:S(2)}) collective-permute-start(f32[16,2,8,128]{3,2,1,0:T(8,128)S(1)} %all_to_all.10.mine_b), channel_id=1, source_target_pairs={{0,1},{1,0},{2,3},{3,2},{4,5},{5,4},{6,7},{7,6},{8,9},{9,8},{10,11... | collective-permute-start | bytes 393224 | tf_op jit(solution)/shard_map/ppermute | solution.py:744

commit v5 on v4

--- a/solution.py
+++ b/solution.py
@@ -18,10 +18,12 @@
 
 F32 = jnp.float32
 LANES = 128
+PARTS = 2
 FINE = SWEEPS + 1
 WIDTHS = (FINE - 1, FINE - 1, FINE)
 COARSE = 8
 SOURCE = COARSE - 1
+LOCAL = FINE // 2
 POST = SWEEPS
 SENT = POST - 1
 BLOCK = 24
@@ -29,7 +31,13 @@
 
 
 def dot(a, b):
-    return jnp.dot(a, b, precision=lax.Precision.HIGHEST, preferred_element_type=F32)
+    b = b.astype(jnp.bfloat16)
+    parts = []
+    for _ in range(PARTS):
+        parts.append(a.astype(jnp.bfloat16))
+        a = a - parts[-1].astype(F32)
+    found = [jnp.dot(part, b, preferred_element_type=F32) for part in reversed(parts)]
+    return sum(found[1:], found[0])
 
 
 def iota(shape, dim):
@@ -266,7 +274,7 @@
 
 
 def fine_pre_kernel(guess, source, coef, c1, one, two, three, four,
-                    out, wx, wy, wz, gain, scaled, first, second, b1,
+                    out, wx, wy, wz, gain, scaled, first, second, b1, local,
                     field, force, c, v, w, total, *pairs):
     nx, ny, nz = guess.shape
     across, beside = Sides(GX, one, two), Sides(GY, three, four)
@@ -339,11 +347,17 @@
 
     n1, r1 = nx // 2, ny // 2
 
-    def coarsen(value):
+    def coarsen(value, number):
         wide = jnp.concatenate(
-            [jnp.concatenate([even_odd(pairs[t].at[pl.ds(q * rows, ny)], r1) for t in range(pieces)], 1) for q in range(n1)], 0
+            [jnp.concatenate([even_odd(pairs[t].at[pl.ds(q * rows, ny)], r1) for t in range(pieces)], 1) for q in range(number)], 0
         )
-        return dot(wide, halve_lanes(nz, nz // 2, value)).reshape(n1, r1, nz // 2)
+        return dot(wide, halve_lanes(nz, nz // 2, value)).reshape(number, r1, nz // 2)
+
+    for k in range(2 * LOCAL):
+        p = 2 * k if k < LOCAL else nx + 2 * k
+        for t in range(pieces):
+            pairs[t][k * rows:k * rows + ny, :] = c[p, t, :ny] + c[p + 1, t, :ny]
+    local[...] = coarsen(0.125, 2 * LOCAL)
 
     def halve(q):
         one, two = (residual(reader(w), level, FINE + 2 * q + k) for k in range(2))
@@ -352,14 +366,14 @@
                 pairs[t][pl.ds(q * rows + j, 8, stride=count), :] = one[j, t] + two[j, t]
 
     planes(0, n1, halve)
-    b1[...] = coarsen(0.125 * 0.5)
+    b1[...] = coarsen(0.125 * 0.5, n1)
 
     def write(up, down):
         up[:SOURCE] = b1[n1 - SOURCE:]
         down[:SOURCE] = b1[:SOURCE]
-        up[SOURCE:SOURCE + COARSE] = c1[n1 - COARSE:]
-        down[SOURCE:SOURCE + COARSE] = c1[:COARSE]
-        at = SOURCE + COARSE
+        at = SOURCE + COARSE - LOCAL
+        up[SOURCE:at] = c1[n1 - COARSE:n1 - LOCAL]
+        down[SOURCE:at] = c1[LOCAL:COARSE]
         for k in range(SENT):
             for i in range(2):
                 for j in range(2):
@@ -371,7 +385,7 @@
     address(GX, first, second, write)
 
 
-def rows_kernel(b1, c1, v, one, two, first, second):
+def rows_kernel(b1, c1, local, v, one, two, first, second):
     n1, r1, half = b1.shape
     nx, ny = 2 * n1, 2 * r1
     sides = Sides(GX, one, two)
@@ -382,14 +396,17 @@
             down[at] = take(pl.ds(0, COARSE))
 
         at = base = 0
-        for own, width in ((b1, SOURCE), (c1, COARSE)):
-            for k in range(width):
+        for own, width, known in ((b1, SOURCE, 0), (c1, COARSE, LOCAL)):
+            for k in range(width - known):
                 edge(lambda rows: sides.low(base + k, rows), at + k)
-                edge(lambda rows: sides.high(base + k, rows), at + width + n1 + k)
+                edge(lambda rows: sides.high(base + k, rows), at + width + n1 + known + k)
+            for k in range(known):
+                edge(lambda rows: local[k, rows, :], at + width - known + k)
+                edge(lambda rows: local[known + k, rows, :], at + width + n1 + k)
             for k in range(n1):
                 edge(lambda rows: own[k, rows, :], at + width + k)
             at += n1 + 2 * width
-            base += width
+            base += width - known
         for j in range(2):
             rows, lanes = pl.ds(j * FINE, FINE), pl.ds(j * half, half)
             last, start = pl.ds(r1 - FINE, FINE), pl.ds(0, FINE)
@@ -404,7 +421,7 @@
     address(GY, first, second, write)
 
 
-def coarse_pre_kernel(b1, c1, one, two, three, four,
+def coarse_pre_kernel(b1, c1, local, one, two, three, four, sent,
                       v, wx, wy, wz, gain, scaled, send, field, c, w, total, upper, lower):
     n1, r1, lanes = b1.shape
     rows = r1 + 2 * COARSE
@@ -414,22 +431,25 @@
     level = (wx, wy, wz, gain, scaled, total)
     across, beside = Sides(GX, one, two), Sides(GY, three, four)
 
-    def fill(target, own, base, offset, width):
+    def fill(target, own, base, offset, width, known):
         at = COARSE - width
         for k in range(n1 + 2 * width):
             target[at + k, r1:r1 + COARSE] = beside.high(offset + k)
             target[at + k, r1 + COARSE:] = beside.low(offset + k)
         for k in range(n1):
             target[COARSE + k, :r1] = own[k]
-        for k in range(width):
+        for k in range(width - known):
             target[at + k, :r1] = across.low(base + k)
-            target[COARSE + n1 + k, :r1] = across.high(base + k)
+            target[COARSE + n1 + known + k, :r1] = across.high(base + k)
+        for k in range(known):
+            target[COARSE - known + k, :r1] = local[k]
+            target[COARSE + n1 + k, :r1] = local[known + k]
 
     def spaced(ref):
         return lambda p, j, t: ref[p, pl.ds(j, 8, stride=count), :]
 
-    fill(field, b1, 0, 0, SOURCE)
-    fill(c, c1, SOURCE, n1 + 2 * SOURCE, COARSE)
+    fill(field, b1, 0, 0, SOURCE, 0)
+    fill(c, c1, SOURCE, n1 + 2 * SOURCE, COARSE, LOCAL)
     for p in range(planes1):
         for j in range(count):
             w[p, j, 0] = spaced(c)(p, j, 0)
@@ -460,8 +480,9 @@
         ref[last, j, 0] = roll(ref[1, j, 0], -depth, 1)
 
 
-def regroup(depth):
-    source, target = iota((2 * LANES, LANES), 0), iota((2 * LANES, LANES), 1)
+def regroup(depth, back=False):
+    dims = (LANES, 2 * LANES) if back else (2 * LANES, LANES)
+    source, target = iota(dims, int(back)), iota(dims, 1 - int(back))
     group, lane = source // LANES, source % LANES
     block, z = lane // depth, lane % depth
     return (2 * block + group) * (depth // 2) + z // 2 == target
@@ -545,10 +566,9 @@
 
     def up(coarse, fine, depth):
         count, rows = fine.shape[0] - 2, fine.shape[1]
-        matrix = jnp.where(regroup(depth), 1.0, 0.0).astype(F32)
+        matrix = jnp.where(regroup(depth, True), 1.0, 0.0).astype(F32)
         x = jnp.concatenate([coarse[1 + m, j, 0] for m in range(count // 4) for j in range(rows // 2)], 0)
-        x = lax.dot_general(x, matrix, (((1,), (1,)), ((), ())), precision=lax.Precision.HIGHEST,
-                            preferred_element_type=F32)
+        x = dot(x, matrix)
         at = 0
         for m in range(count // 4):
             for j in range(rows // 2):
@@ -661,7 +681,7 @@
         wide.append(jnp.where(sub < 2, e1[k, r1:r1 + 8], roll(e1[k, r1 + 8:r1 + 16], 4, 0)))
     matrix = jnp.where(iota((lanes1, nz), 0) == iota((lanes1, nz), 1) // 2, 1.0, 0.0).astype(F32)
     wide = dot(jnp.concatenate(wide, 0), matrix)
-    base = SOURCE + COARSE
+    base = SOURCE + COARSE - LOCAL
     beyond = 2 * n1 + 2 * SOURCE + 2 * COARSE
     for k in range(n1 + 4):
         at = k * (r1 + 8)
@@ -774,16 +794,17 @@
 
     block0 = (planes0, rows0 // 8, pieces, 8, LANES)
     plain0 = (planes0, pieces, rows0, LANES)
-    message = (SOURCE + COARSE + 4 * SENT, r1, z1)
-    v0, *level0, first, second, b1 = call(
+    message = (SOURCE + COARSE - LOCAL + 4 * SENT, r1, z1)
+    v0, *level0, first, second, b1, local = call(
         fine_pre_kernel,
-        (shape(nx + 2, ny, nz),) + (shape(*block0),) * 5 + (shape(*message),) * 2 + (shape(n1, r1, z1),),
+        (shape(nx + 2, ny, nz),) + (shape(*block0),) * 5 + (shape(*message),) * 2 + (shape(n1, r1, z1), shape(2 * LOCAL, r1, z1)),
         [vmem(*plain0)] * 3 + [vmem(*block0)] * 3 + [vmem(n1 * rows0, LANES)] * pieces,
         *fields, c1, *across, *beside, specs=[None] * 8,
     )
     across = swap(first, second, GX)
     count = 3 * n1 + 2 * SOURCE + 2 * COARSE + 2 * POST + n1
-    beside = swap(*call(rows_kernel, (shape(count, COARSE, z1),) * 2, (), b1, c1, v0, *across), GY)
+    rows = call(rows_kernel, (shape(count, COARSE, z1),) * 2, (), b1, c1, local, v0, *across)
+    beside = swap(*rows, GY)
 
     planes1, rows1 = n1 + 2 * COARSE, r1 + 2 * COARSE
     block1 = (planes1, rows1 // 8, 1, 8, z1)
@@ -792,7 +813,8 @@
         coarse_pre_kernel,
         (shape(*block1),) * 6 + (shape(gx * gy // 2, n2 // 2, r2, LANES),),
         [vmem(*plain1)] * 2 + [vmem(*block1)] * 2 + [vmem(n2 // 2 * r2, LANES)] * 2,
-        b1, c1, *across, *beside,
+        b1, c1, local, *across, *beside, rows[0],
+        specs=[None] * 7 + [pl.BlockSpec(memory_space=pl.ANY)],
     )
     gathered_b = spread(send)
 

time: 72.8 us -> 71.4 us (0.981)
  blocking collectives: 20.5 us -> 17.5 us
  starting transfers between devices: 21.8 us -> 24.5 us
  Pallas kernels: 17.2 us -> 16.3 us
    all_to_all x1, blocking collectives: 20.5 us -> 17.5 us  [spread(): found = lax.all_to_all(send, (GX, GY[0]), 0, 0)]
    ppermute x8, starting transfers between devices: 13.2 us -> 15.9 us  [swap(): return (lax.ppermute(first, axis, even), lax.ppermute(second, axis, odd))]
  transfers between devices with their start and end apart: 11 -> 11, of which waited for: 6 -> 6; matrix products, arithmetic and copies ran while one was open for 0% -> 0% of each run, Pallas kernels for 6% -> 5%
where the time goes in v5:
time: 71.4 us; the launch traced here: 71.1 us
  starting transfers between devices  24.5 us (34%)
  blocking collectives  17.5 us (25%)
  Pallas kernels  16.3 us (23%)
  waiting for transfers between devices  12.7 us (18%)
    all_to_all x1, blocking collectives, spread(): found = lax.all_to_all(send, (GX, GY[0]), 0, 0)  17.5 us
    ppermute x8, starting transfers between devices, swap(): return (lax.ppermute(first, axis, even), lax.ppermute(second, axis, odd))  15.9 us
    pallas_call x7, Pallas kernels, call(): pl.pallas_call(kernel, grid=(1,) if any((spec and spec.block_shape for sp...  9.37 us
    ppermute x8, waiting for transfers between devices, swap(): return (lax.ppermute(first, axis, even), lax.ppermute(second, axis, odd))  8.91 us
    all_to_all x1, starting transfers between devices, spread(): found = lax.all_to_all(send, (GX, GY[0]), 0, 0)  8.63 us
    pallas_call x1, Pallas kernels, body(): pl.pallas_call(partial(solve_kernel, gx=gx, gy=gy), out_shape=(jax.ShapeD...  6.93 us
    ppermute x2, waiting for transfers between devices, spread(): return (found, lax.ppermute(found, GY[1], [(0, 1), (1, 0)]))  2.69 us
  transfers between devices with their start and end apart: 11, of which 6 were waited for; matrix products, arithmetic and copies ran while one was open for 0% of the time, Pallas kernels for 5%

profile of v5, /device:TPU:0, one launch (start us, length us, event | category | flops | bytes accessed | tf_op | source)
XLA Modules:
  0.0 71.1 jit_solution(6006311280698488199)
XLA Ops:
  0.0 1.2 %shard_map.38 = (f32[10,32,256]{2,1,0:T(8,128)S(1)}, f32[10,32,256]{2,1,0:T(8,128)S(1)}) custom-call(f32[16,32,256]{2,1,0:T(8,128)} %guess.3, f32[16,32,256]{2,1,0:T(8,128)} %guess.3, f32[16,32,256]{2,1,0:T(8,128)} %source.3, f32[16,32,256]{2,1,0:T(8,128)} %source.3, f32[16,32,256]{2,1,0:T(8,128)} %coef.3, f32[16,32,256]{2,1,0:T(8,128)} %coef.3), custom_call_target="tpu_custom_call" | custom-call | tf_op jit(solution)/shard_map/pallas_call | solution.py:740
  1.3 3.0 %collective-permute-start.1 = (f32[10,32,256]{2,1,0:T(8,128)S(1)}, f32[10,32,256]{2,1,0:T(8,128)S(1)}, u32[]{:S(2)}, u32[]{:S(2)}) collective-permute-start(f32[10,32,256]{2,1,0:T(8,128)S(1)} %get-tuple-element.38), channel_id=1, source_target_pairs={{0,4},{4,0},{8,12},{12,8},{16,20},{20,16},{24,28},{28,24},{1,5},{5... | collective-permute-start | bytes 983048 | tf_op jit(solution)/shard_map/ppermute | solution.py:759
  4.3 0.7 collective-permute-start.2
  4.9 2.4 %shard_map.37 = (f32[48,4,256]{2,1,0:T(4,128)S(1)}, f32[48,4,256]{2,1,0:T(4,128)S(1)}, f32[8,16,128]{2,1,0:T(8,128)S(1)}, f32[16,2,8,128]{3,2,1,0:T(8,128)}) custom-call(f32[16,32,256]{2,1,0:T(8,128)} %guess.3, f32[16,32,256]{2,1,0:T(8,128)} %source.3, f32[16,32,256]{2,1,0:T(8,128)} %coef.3), custom_call_target="tpu_custom_call" | custom-call | tf_op jit(solution)/shard_map/pallas_call | solution.py:740
  7.3 8.6 %all-to-all-start = ((f32[16,2,8,128]{3,2,1,0:T(8,128)}), f32[16,2,8,128]{3,2,1,0:T(8,128)S(1)}, u32[]{:S(2)}, u32[]{:S(2)}) async-start(f32[16,2,8,128]{3,2,1,0:T(8,128)} %get-tuple-element.35), calls=%async_computation | async-start | bytes 262144 | tf_op jit(solution)/shard_map/all_to_all | solution.py:763
  15.9 2.9 %collective-permute-done.1.one = f32[10,32,256]{2,1,0:T(8,128)S(1)} collective-permute-done((f32[10,32,256]{2,1,0:T(8,128)S(1)}, f32[10,32,256]{2,1,0:T(8,128)S(1)}, u32[]{:S(2)}, u32[]{:S(2)}) %collective-permute-start.1) | collective-permute-done | bytes 327712 | tf_op jit(solution)/shard_map/ppermute | solution.py:759
  18.8 0.0 collective-permute-done.2.two
  18.9 0.7 collective-permute-start.4
  19.6 3.1 %collective-permute-start.3 = (f32[68,4,256]{2,1,0:T(4,128)S(1)}, f32[68,4,256]{2,1,0:T(4,128)S(1)}, u32[]{:S(2)}, u32[]{:S(2)}) collective-permute-start(f32[68,4,256]{2,1,0:T(4,128)S(1)} %get-tuple-element.40.rest_1_), channel_id=1, source_target_pairs={{0,1},{1,0},{2,3},{3,2},{4,5},{5,4},{6,7},{7,6},{8,9},{9,8},{10,11... | collective-permute-start | bytes 835592 | tf_op jit(solution)/shard_map/ppermute | solution.py:759
  22.7 1.1 %all-to-all-done.mine_c = f32[16,2,8,128]{3,2,1,0:T(8,128)S(1)} async-done(((f32[16,2,8,128]{3,2,1,0:T(8,128)}), f32[16,2,8,128]{3,2,1,0:T(8,128)S(1)}, u32[]{:S(2)}, u32[]{:S(2)}) %all-to-all-start) | async-done | bytes 131104 | tf_op jit(solution)/shard_map/all_to_all | solution.py:763
  23.7 0.0 collective-permute-start
  23.7 1.3 %collective-permute-done.rest_0_.other_c = f32[16,2,8,128]{3,2,1,0:T(8,128)S(1)} collective-permute-done((f32[16,2,8,128]{3,2,1,0:T(8,128)S(1)}, f32[16,2,8,128]{3,2,1,0:T(8,128)S(1)}, u32[]{:S(2)}, u32[]{:S(2)}) %collective-permute-start) | collective-permute-done | bytes 131104 | tf_op jit(solution)/shard_map/ppermute | solution.py:764
  25.1 1.5 %shard_map.40 = (f32[16,32,256]{2,1,0:T(8,128)S(1)}, f32[16,32,256]{2,1,0:T(8,128)S(1)}, f32[16,32,256]{2,1,0:T(8,128)S(1)}) custom-call(f32[16,32,256]{2,1,0:T(8,128)} %guess.3, f32[16,32,256]{2,1,0:T(8,128)} %source.3, f32[16,32,256]{2,1,0:T(8,128)} %coef.3, f32[16,2,8,128]{3,2,1,0:T(8,128)S(1)} %collective-permute-done.rest_0_.other_c, ...), custom_call_target="tpu_custom_call" | custom-call | tf_op jit(solution)/shard_map/pallas_call | solution.py:740
  26.6 0.0 collective-permute-done.4.four
  26.6 0.0 collective-permute-done.3.three
  26.6 3.3 %shard_map.41 = (f32[18,32,256]{2,1,0:T(8,128)S(1)}, f32[24,5,2,8,128]{4,3,2,1,0:T(8,128)S(1)}, f32[24,5,2,8,128]{4,3,2,1,0:T(8,128)S(1)}, f32[24,5,2,8,128]{4,3...) custom-call(f32[16,32,256]{2,1,0:T(8,128)S(1)} %get-tuple-element.41, ...), custom_call_target="tpu_custom_call" | custom-call | tf_op jit(solution)/shard_map/pallas_call | solution.py:740
  29.9 1.6 %collective-permute-start.5 = (f32[21,16,128]{2,1,0:T(8,128)S(1)}, f32[21,16,128]{2,1,0:T(8,128)S(1)}, u32[]{:S(2)}, u32[]{:S(2)}) collective-permute-start(f32[21,16,128]{2,1,0:T(8,128)S(1)} %get-tuple-element.48), channel_id=1, source_target_pairs={{0,4},{4,0},{8,12},{12,8},{16,20},{20,16},{24,28},{28,24},{1,5},{5... | collective-permute-start | bytes 516104 | tf_op jit(solution)/shard_map/ppermute | solution.py:759
  31.5 0.7 collective-permute-start.6
  32.2 4.8 %collective-permute-done.5.one = f32[21,16,128]{2,1,0:T(8,128)S(1)} collective-permute-done((f32[21,16,128]{2,1,0:T(8,128)S(1)}, f32[21,16,128]{2,1,0:T(8,128)S(1)}, u32[]{:S(2)}, u32[]{:S(2)}) %collective-permute-start.5) | collective-permute-done | bytes 172064 | tf_op jit(solution)/shard_map/ppermute | solution.py:759
  37.0 0.0 collective-permute-done.6.two
  37.0 0.1 shard_map.42
  37.1 0.7 collective-permute-start.8
  37.8 5.4 %collective-permute-start.7 = (f32[68,8,128]{2,1,0:T(8,128)S(1)}, f32[68,8,128]{2,1,0:T(8,128)S(1)}, u32[]{:S(2)}, u32[]{:S(2)}) collective-permute-start(f32[68,8,128]{2,1,0:T(8,128)S(1)} %get-tuple-element.51.sent), channel_id=1, source_target_pairs={{0,1},{1,0},{2,3},{3,2},{4,5},{5,4},{6,7},{7,6},{8,9},{9,8},{10,11... | collective-permute-start | bytes 835592 | tf_op jit(solution)/shard_map/ppermute | solution.py:759
  43.2 0.0 collective-permute-done.8.four
  43.2 1.2 %collective-permute-done.7.three = f32[68,8,128]{2,1,0:T(8,128)S(1)} collective-permute-done((f32[68,8,128]{2,1,0:T(8,128)S(1)}, f32[68,8,128]{2,1,0:T(8,128)S(1)}, u32[]{:S(2)}, u32[]{:S(2)}) %collective-permute-start.7) | collective-permute-done | bytes 278560 | tf_op jit(solution)/shard_map/ppermute | solution.py:759
  44.4 0.9 %shard_map.43 = (f32[24,4,1,8,128]{4,3,2,1,0:T(8,128)S(1)}, f32[24,4,1,8,128]{4,3,2,1,0:T(8,128)S(1)}, f32[24,4,1,8,128]{4,3,2,1,0:T(8,128)S(1)}, f32[24,4,1,8,1...) custom-call(f32[8,16,128]{2,1,0:T(8,128)S(1)} %get-tuple-element.46., ...), custom_call_target="tpu_custom_call" | custom-call | tf_op jit(solution)/shard_map/pallas_call | solution.py:740
  45.3 17.5 %all_to_all.10.mine_b = f32[16,2,8,128]{3,2,1,0:T(8,128)S(1)} all-to-all(f32[16,2,8,128]{3,2,1,0:T(8,128)S(1)} %get-tuple-element.53), channel_id=1, replica_groups=mesh['gx'=8,'gy_far'=2,'gy_near'=2] {'gx','gy_far'}, dimensions={0} | all-to-all | bytes 262144 | tf_op jit(solution)/shard_map/all_to_all | solution.py:763
  62.8 0.0 collective-permute-start.9
  62.8 1.3 %collective-permute-done.9.other_b = f32[16,2,8,128]{3,2,1,0:T(8,128)S(1)} collective-permute-done((f32[16,2,8,128]{3,2,1,0:T(8,128)S(1)}, f32[16,2,8,128]{3,2,1,0:T(8,128)S(1)}, u32[]{:S(2)}, u32[]{:S(2)}) %collective-permute-start.9) | collective-permute-done | bytes 131104 | tf_op jit(solution)/shard_map/ppermute | solution.py:764
  64.1 6.9 %shard_map.44 = f32[16,32,256]{2,1,0:T(8,128)} custom-call(f32[16,2,8,128]{3,2,1,0:T(8,128)S(1)} %all_to_all.10.mine_b, f32[16,2,8,128]{3,2,1,0:T(8,128)S(1)} %collective-permute-done.9.other_b, f32[16,2,8,128]{3,2,1,0:T(8,128)S(1)} %all-to-all-done.mine_c, f32[16,2,8,128]{3,2,1,0:T(8,128)S(1)} %collective-permute-done.rest_0_.other_c, ...), custom_call_target="tpu_custom_call" | custom-call | tf_op jit(solution)/shard_map/pallas_call | solution.py:830
  (1 shorter events, 0.0 us)
Async XLA Ops:
  1.3 17.6 %collective-permute-start.1 = (f32[10,32,256]{2,1,0:T(8,128)S(1)}, f32[10,32,256]{2,1,0:T(8,128)S(1)}, u32[]{:S(2)}, u32[]{:S(2)}) collective-permute-start(f32[10,32,256]{2,1,0:T(8,128)S(1)} %get-tuple-element.38), channel_id=1, source_target_pairs={{0,4},{4,0},{8,12},{12,8},{16,20},{20,16},{24,28},{28,24},{1,5},{5... | collective-permute-start | bytes 983048 | tf_op jit(solution)/shard_map/ppermute | solution.py:759
  4.3 14.6 %collective-permute-start.2 = (f32[10,32,256]{2,1,0:T(8,128)S(1)}, f32[10,32,256]{2,1,0:T(8,128)S(1)}, u32[]{:S(2)}, u32[]{:S(2)}) collective-permute-start(f32[10,32,256]{2,1,0:T(8,128)S(1)} %get-tuple-element.39), channel_id=1, source_target_pairs={{4,8},{8,4},{12,16},{16,12},{20,24},{24,20},{5,9},{9,5},{13,17},{1... | collective-permute-start | bytes 983048 | tf_op jit(solution)/shard_map/ppermute | solution.py:759
  7.3 16.4 %all-to-all-start = ((f32[16,2,8,128]{3,2,1,0:T(8,128)}), f32[16,2,8,128]{3,2,1,0:T(8,128)S(1)}, u32[]{:S(2)}, u32[]{:S(2)}) async-start(f32[16,2,8,128]{3,2,1,0:T(8,128)} %get-tuple-element.35), calls=%async_computation | async-start | bytes 262144 | tf_op jit(solution)/shard_map/all_to_all | solution.py:763
  18.9 7.7 %collective-permute-start.4 = (f32[68,4,256]{2,1,0:T(4,128)S(1)}, f32[68,4,256]{2,1,0:T(4,128)S(1)}, u32[]{:S(2)}, u32[]{:S(2)}) collective-permute-start(f32[68,4,256]{2,1,0:T(4,128)S(1)} %get-tuple-element.45), channel_id=1, source_target_pairs={{1,2},{2,1},{5,6},{6,5},{9,10},{10,9},{13,14},{14,13},{17,18},{18,... | collective-permute-start | bytes 835592 | tf_op jit(solution)/shard_map/ppermute | solution.py:759
  19.6 7.0 %collective-permute-start.3 = (f32[68,4,256]{2,1,0:T(4,128)S(1)}, f32[68,4,256]{2,1,0:T(4,128)S(1)}, u32[]{:S(2)}, u32[]{:S(2)}) collective-permute-start(f32[68,4,256]{2,1,0:T(4,128)S(1)} %get-tuple-element.40.rest_1_), channel_id=1, source_target_pairs={{0,1},{1,0},{2,3},{3,2},{4,5},{5,4},{6,7},{7,6},{8,9},{9,8},{10,11... | collective-permute-start | bytes 835592 | tf_op jit(solution)/shard_map/ppermute | solution.py:759
  23.7 1.3 %collective-permute-start = (f32[16,2,8,128]{3,2,1,0:T(8,128)S(1)}, f32[16,2,8,128]{3,2,1,0:T(8,128)S(1)}, u32[]{:S(2)}, u32[]{:S(2)}) collective-permute-start(f32[16,2,8,128]{3,2,1,0:T(8,128)S(1)} %all-to-all-done.mine_c), channel_id=1, source_target_pairs={{0,1},{1,0},{2,3},{3,2},{4,5},{5,4},{6,7},{7,6},{8,9},{9,8},{10,11... | collective-permute-start | bytes 393224 | tf_op jit(solution)/shard_map/ppermute | solution.py:764
  29.9 7.2 %collective-permute-start.5 = (f32[21,16,128]{2,1,0:T(8,128)S(1)}, f32[21,16,128]{2,1,0:T(8,128)S(1)}, u32[]{:S(2)}, u32[]{:S(2)}) collective-permute-start(f32[21,16,128]{2,1,0:T(8,128)S(1)} %get-tuple-element.48), channel_id=1, source_target_pairs={{0,4},{4,0},{8,12},{12,8},{16,20},{20,16},{24,28},{28,24},{1,5},{5... | collective-permute-start | bytes 516104 | tf_op jit(solution)/shard_map/ppermute | solution.py:759
  31.5 5.5 %collective-permute-start.6 = (f32[21,16,128]{2,1,0:T(8,128)S(1)}, f32[21,16,128]{2,1,0:T(8,128)S(1)}, u32[]{:S(2)}, u32[]{:S(2)}) collective-permute-start(f32[21,16,128]{2,1,0:T(8,128)S(1)} %get-tuple-element.49), channel_id=1, source_target_pairs={{4,8},{8,4},{12,16},{16,12},{20,24},{24,20},{5,9},{9,5},{13,17},{1... | collective-permute-start | bytes 516104 | tf_op jit(solution)/shard_map/ppermute | solution.py:759
  37.1 6.1 %collective-permute-start.8 = (f32[68,8,128]{2,1,0:T(8,128)S(1)}, f32[68,8,128]{2,1,0:T(8,128)S(1)}, u32[]{:S(2)}, u32[]{:S(2)}) collective-permute-start(f32[68,8,128]{2,1,0:T(8,128)S(1)} %get-tuple-element.52), channel_id=1, source_target_pairs={{1,2},{2,1},{5,6},{6,5},{9,10},{10,9},{13,14},{14,13},{17,18},{18,... | collective-permute-start | bytes 835592 | tf_op jit(solution)/shard_map/ppermute | solution.py:759
  37.8 6.6 %collective-permute-start.7 = (f32[68,8,128]{2,1,0:T(8,128)S(1)}, f32[68,8,128]{2,1,0:T(8,128)S(1)}, u32[]{:S(2)}, u32[]{:S(2)}) collective-permute-start(f32[68,8,128]{2,1,0:T(8,128)S(1)} %get-tuple-element.51.sent), channel_id=1, source_target_pairs={{0,1},{1,0},{2,3},{3,2},{4,5},{5,4},{6,7},{7,6},{8,9},{9,8},{10,11... | collective-permute-start | bytes 835592 | tf_op jit(solution)/shard_map/ppermute | solution.py:759
  62.8 1.3 %collective-permute-start.9 = (f32[16,2,8,128]{3,2,1,0:T(8,128)S(1)}, f32[16,2,8,128]{3,2,1,0:T(8,128)S(1)}, u32[]{:S(2)}, u32[]{:S(2)}) collective-permute-start(f32[16,2,8,128]{3,2,1,0:T(8,128)S(1)} %all_to_all.10.mine_b), channel_id=1, source_target_pairs={{0,1},{1,0},{2,3},{3,2},{4,5},{5,4},{6,7},{7,6},{8,9},{9,8},{10,11... | collective-permute-start | bytes 393224 | tf_op jit(solution)/shard_map/ppermute | solution.py:764

commit v6 on v5

--- a/solution.py
+++ b/solution.py
@@ -397,15 +397,16 @@
 
         at = base = 0
         for own, width, known in ((b1, SOURCE, 0), (c1, COARSE, LOCAL)):
-            for k in range(width - known):
-                edge(lambda rows: sides.low(base + k, rows), at + k)
-                edge(lambda rows: sides.high(base + k, rows), at + width + n1 + known + k)
+            near = width - 1
+            for k in range(near - known):
+                edge(lambda rows: sides.low(base + 1 + k, rows), at + k)
+                edge(lambda rows: sides.high(base + k, rows), at + near + n1 + known + k)
             for k in range(known):
-                edge(lambda rows: local[k, rows, :], at + width - known + k)
-                edge(lambda rows: local[known + k, rows, :], at + width + n1 + k)
+                edge(lambda rows: local[k, rows, :], at + near - known + k)
+                edge(lambda rows: local[known + k, rows, :], at + near + n1 + k)
             for k in range(n1):
-                edge(lambda rows: own[k, rows, :], at + width + k)
-            at += n1 + 2 * width
+                edge(lambda rows: own[k, rows, :], at + near + k)
+            at += n1 + 2 * near
             base += width - known
         for j in range(2):
             rows, lanes = pl.ds(j * FINE, FINE), pl.ds(j * half, half)
@@ -433,9 +434,11 @@
 
     def fill(target, own, base, offset, width, known):
         at = COARSE - width
-        for k in range(n1 + 2 * width):
-            target[at + k, r1:r1 + COARSE] = beside.high(offset + k)
-            target[at + k, r1 + COARSE:] = beside.low(offset + k)
+        for k in range(n1 + 2 * width - 2):
+            target[at + 1 + k, r1:r1 + COARSE] = beside.high(offset + k)
+            target[at + 1 + k, r1 + COARSE:] = beside.low(offset + k)
+        for p in (at, COARSE + n1 + width - 1):
+            target[p, r1:] = jnp.zeros((2 * COARSE, lanes), F32)
         for k in range(n1):
             target[COARSE + k, :r1] = own[k]
         for k in range(width - known):
@@ -449,7 +452,7 @@
         return lambda p, j, t: ref[p, pl.ds(j, 8, stride=count), :]
 
     fill(field, b1, 0, 0, SOURCE, 0)
-    fill(c, c1, SOURCE, n1 + 2 * SOURCE, COARSE, LOCAL)
+    fill(c, c1, SOURCE, n1 + 2 * SOURCE - 2, COARSE, LOCAL)
     for p in range(planes1):
         for j in range(count):
             w[p, j, 0] = spaced(c)(p, j, 0)
@@ -682,7 +685,7 @@
     matrix = jnp.where(iota((lanes1, nz), 0) == iota((lanes1, nz), 1) // 2, 1.0, 0.0).astype(F32)
     wide = dot(jnp.concatenate(wide, 0), matrix)
     base = SOURCE + COARSE - LOCAL
-    beyond = 2 * n1 + 2 * SOURCE + 2 * COARSE
+    beyond = 2 * n1 + 2 * (SOURCE - 1) + 2 * (COARSE - 1)
     for k in range(n1 + 4):
         at = k * (r1 + 8)
         for t in range(pieces):
@@ -715,12 +718,14 @@
     planes(FINE - POST, FINE + nx + POST, arrange)
     sweep(reader(u0), t0, level0, FINE - 2, FINE + nx + 2)
     sweep(reader(t0), u0, level0, FINE - 1, FINE + nx + 1)
-    sweep(reader(u0), t0, level0, FINE, FINE + nx)
 
     def put(k):
+        def finish(j, t, v, total):
+            value = (1.0 - RELAX_WEIGHT) * v + gain0[FINE + k, j, t] * (scaled0[FINE + k, j, t] + total)
+            field[k, t, pl.ds(j, 8, stride=count0), :] = value
+
+        around(reader(u0), level0, FINE + k, finish)
         for t in range(pieces):
-            for j in range(count0):
-                field[k, t, pl.ds(j, 8, stride=count0), :] = t0[FINE + k, j, t]
             out[k, :, t * LANES:(t + 1) * LANES] = field[k, t, :ny]
 
     planes(0, nx, put)
@@ -802,7 +807,7 @@
         *fields, c1, *across, *beside, specs=[None] * 8,
     )
     across = swap(first, second, GX)
-    count = 3 * n1 + 2 * SOURCE + 2 * COARSE + 2 * POST + n1
+    count = 4 * n1 + 2 * (SOURCE - 1) + 2 * (COARSE - 1) + 2 * POST
     rows = call(rows_kernel, (shape(count, COARSE, z1),) * 2, (), b1, c1, local, v0, *across)
     beside = swap(*rows, GY)
 

time: 71.4 us -> 71.3 us (level)
  no operation moved by 1% of the time
where the time goes in v6:
time: 71.3 us; the launch traced here: 70.9 us
  starting transfers between devices  24.5 us (34%)
  blocking collectives  17.3 us (24%)
  Pallas kernels  16.3 us (23%)
  waiting for transfers between devices  12.7 us (18%)
    all_to_all x1, blocking collectives, spread(): found = lax.all_to_all(send, (GX, GY[0]), 0, 0)  17.3 us
    ppermute x8, starting transfers between devices, swap(): return (lax.ppermute(first, axis, even), lax.ppermute(second, axis, odd))  15.9 us
    pallas_call x7, Pallas kernels, call(): pl.pallas_call(kernel, grid=(1,) if any((spec and spec.block_shape for sp...  9.37 us
    ppermute x8, waiting for transfers between devices, swap(): return (lax.ppermute(first, axis, even), lax.ppermute(second, axis, odd))  8.89 us
    all_to_all x1, starting transfers between devices, spread(): found = lax.all_to_all(send, (GX, GY[0]), 0, 0)  8.63 us
    pallas_call x1, Pallas kernels, body(): pl.pallas_call(partial(solve_kernel, gx=gx, gy=gy), out_shape=(jax.ShapeD...  6.93 us
    ppermute x2, waiting for transfers between devices, spread(): return (found, lax.ppermute(found, GY[1], [(0, 1), (1, 0)]))  2.69 us
  transfers between devices with their start and end apart: 11, of which 6 were waited for; matrix products, arithmetic and copies ran while one was open for 0% of the time, Pallas kernels for 5%

profile of v6, /device:TPU:0, one launch (start us, length us, event | category | flops | bytes accessed | tf_op | source)
XLA Modules:
  0.0 70.9 jit_solution(18443455968644858302)
XLA Ops:
  0.0 1.2 %shard_map.38 = (f32[10,32,256]{2,1,0:T(8,128)S(1)}, f32[10,32,256]{2,1,0:T(8,128)S(1)}) custom-call(f32[16,32,256]{2,1,0:T(8,128)} %guess.3, f32[16,32,256]{2,1,0:T(8,128)} %guess.3, f32[16,32,256]{2,1,0:T(8,128)} %source.3, f32[16,32,256]{2,1,0:T(8,128)} %source.3, f32[16,32,256]{2,1,0:T(8,128)} %coef.3, f32[16,32,256]{2,1,0:T(8,128)} %coef.3), custom_call_target="tpu_custom_call" | custom-call | tf_op jit(solution)/shard_map/pallas_call | solution.py:745
  1.3 3.0 %collective-permute-start.1 = (f32[10,32,256]{2,1,0:T(8,128)S(1)}, f32[10,32,256]{2,1,0:T(8,128)S(1)}, u32[]{:S(2)}, u32[]{:S(2)}) collective-permute-start(f32[10,32,256]{2,1,0:T(8,128)S(1)} %get-tuple-element.38), channel_id=1, source_target_pairs={{0,4},{4,0},{8,12},{12,8},{16,20},{20,16},{24,28},{28,24},{1,5},{5... | collective-permute-start | bytes 983048 | tf_op jit(solution)/shard_map/ppermute | solution.py:764
  4.3 0.7 collective-permute-start.2
  4.9 2.4 %shard_map.37 = (f32[48,4,256]{2,1,0:T(4,128)S(1)}, f32[48,4,256]{2,1,0:T(4,128)S(1)}, f32[8,16,128]{2,1,0:T(8,128)S(1)}, f32[16,2,8,128]{3,2,1,0:T(8,128)}) custom-call(f32[16,32,256]{2,1,0:T(8,128)} %guess.3, f32[16,32,256]{2,1,0:T(8,128)} %source.3, f32[16,32,256]{2,1,0:T(8,128)} %coef.3), custom_call_target="tpu_custom_call" | custom-call | tf_op jit(solution)/shard_map/pallas_call | solution.py:745
  7.3 8.6 %all-to-all-start = ((f32[16,2,8,128]{3,2,1,0:T(8,128)}), f32[16,2,8,128]{3,2,1,0:T(8,128)S(1)}, u32[]{:S(2)}, u32[]{:S(2)}) async-start(f32[16,2,8,128]{3,2,1,0:T(8,128)} %get-tuple-element.35), calls=%async_computation | async-start | bytes 262144 | tf_op jit(solution)/shard_map/all_to_all | solution.py:768
  15.9 2.9 %collective-permute-done.1.one = f32[10,32,256]{2,1,0:T(8,128)S(1)} collective-permute-done((f32[10,32,256]{2,1,0:T(8,128)S(1)}, f32[10,32,256]{2,1,0:T(8,128)S(1)}, u32[]{:S(2)}, u32[]{:S(2)}) %collective-permute-start.1) | collective-permute-done | bytes 327712 | tf_op jit(solution)/shard_map/ppermute | solution.py:764
  18.8 0.0 collective-permute-done.2.two
  18.9 0.7 collective-permute-start.4
  19.6 3.1 %collective-permute-start.3 = (f32[68,4,256]{2,1,0:T(4,128)S(1)}, f32[68,4,256]{2,1,0:T(4,128)S(1)}, u32[]{:S(2)}, u32[]{:S(2)}) collective-permute-start(f32[68,4,256]{2,1,0:T(4,128)S(1)} %get-tuple-element.40.rest_1_), channel_id=1, source_target_pairs={{0,1},{1,0},{2,3},{3,2},{4,5},{5,4},{6,7},{7,6},{8,9},{9,8},{10,11... | collective-permute-start | bytes 835592 | tf_op jit(solution)/shard_map/ppermute | solution.py:764
  22.7 1.1 %all-to-all-done.mine_c = f32[16,2,8,128]{3,2,1,0:T(8,128)S(1)} async-done(((f32[16,2,8,128]{3,2,1,0:T(8,128)}), f32[16,2,8,128]{3,2,1,0:T(8,128)S(1)}, u32[]{:S(2)}, u32[]{:S(2)}) %all-to-all-start) | async-done | bytes 131104 | tf_op jit(solution)/shard_map/all_to_all | solution.py:768
  23.7 0.0 collective-permute-start
  23.7 1.3 %collective-permute-done.rest_0_.other_c = f32[16,2,8,128]{3,2,1,0:T(8,128)S(1)} collective-permute-done((f32[16,2,8,128]{3,2,1,0:T(8,128)S(1)}, f32[16,2,8,128]{3,2,1,0:T(8,128)S(1)}, u32[]{:S(2)}, u32[]{:S(2)}) %collective-permute-start) | collective-permute-done | bytes 131104 | tf_op jit(solution)/shard_map/ppermute | solution.py:769
  25.1 1.5 %shard_map.40 = (f32[16,32,256]{2,1,0:T(8,128)S(1)}, f32[16,32,256]{2,1,0:T(8,128)S(1)}, f32[16,32,256]{2,1,0:T(8,128)S(1)}) custom-call(f32[16,32,256]{2,1,0:T(8,128)} %guess.3, f32[16,32,256]{2,1,0:T(8,128)} %source.3, f32[16,32,256]{2,1,0:T(8,128)} %coef.3, f32[16,2,8,128]{3,2,1,0:T(8,128)S(1)} %collective-permute-done.rest_0_.other_c, ...), custom_call_target="tpu_custom_call" | custom-call | tf_op jit(solution)/shard_map/pallas_call | solution.py:745
  26.6 0.0 collective-permute-done.4.four
  26.6 0.0 collective-permute-done.3.three
  26.6 3.3 %shard_map.41 = (f32[18,32,256]{2,1,0:T(8,128)S(1)}, f32[24,5,2,8,128]{4,3,2,1,0:T(8,128)S(1)}, f32[24,5,2,8,128]{4,3,2,1,0:T(8,128)S(1)}, f32[24,5,2,8,128]{4,3...) custom-call(f32[16,32,256]{2,1,0:T(8,128)S(1)} %get-tuple-element.41, ...), custom_call_target="tpu_custom_call" | custom-call | tf_op jit(solution)/shard_map/pallas_call | solution.py:745
  29.9 1.6 %collective-permute-start.5 = (f32[21,16,128]{2,1,0:T(8,128)S(1)}, f32[21,16,128]{2,1,0:T(8,128)S(1)}, u32[]{:S(2)}, u32[]{:S(2)}) collective-permute-start(f32[21,16,128]{2,1,0:T(8,128)S(1)} %get-tuple-element.48), channel_id=1, source_target_pairs={{0,4},{4,0},{8,12},{12,8},{16,20},{20,16},{24,28},{28,24},{1,5},{5... | collective-permute-start | bytes 516104 | tf_op jit(solution)/shard_map/ppermute | solution.py:764
  31.5 0.7 collective-permute-start.6
  32.2 4.8 %collective-permute-done.5.one = f32[21,16,128]{2,1,0:T(8,128)S(1)} collective-permute-done((f32[21,16,128]{2,1,0:T(8,128)S(1)}, f32[21,16,128]{2,1,0:T(8,128)S(1)}, u32[]{:S(2)}, u32[]{:S(2)}) %collective-permute-start.5) | collective-permute-done | bytes 172064 | tf_op jit(solution)/shard_map/ppermute | solution.py:764
  37.0 0.0 collective-permute-done.6.two
  37.0 0.1 shard_map.42
  37.1 0.7 collective-permute-start.8
  37.8 5.4 %collective-permute-start.7 = (f32[64,8,128]{2,1,0:T(8,128)S(1)}, f32[64,8,128]{2,1,0:T(8,128)S(1)}, u32[]{:S(2)}, u32[]{:S(2)}) collective-permute-start(f32[64,8,128]{2,1,0:T(8,128)S(1)} %get-tuple-element.51.sent), channel_id=1, source_target_pairs={{0,1},{1,0},{2,3},{3,2},{4,5},{5,4},{6,7},{7,6},{8,9},{9,8},{10,11... | collective-permute-start | bytes 786440 | tf_op jit(solution)/shard_map/ppermute | solution.py:764
  43.2 0.0 collective-permute-done.8.four
  43.2 1.2 %collective-permute-done.7.three = f32[64,8,128]{2,1,0:T(8,128)S(1)} collective-permute-done((f32[64,8,128]{2,1,0:T(8,128)S(1)}, f32[64,8,128]{2,1,0:T(8,128)S(1)}, u32[]{:S(2)}, u32[]{:S(2)}) %collective-permute-start.7) | collective-permute-done | bytes 262176 | tf_op jit(solution)/shard_map/ppermute | solution.py:764
  44.4 0.9 %shard_map.43 = (f32[24,4,1,8,128]{4,3,2,1,0:T(8,128)S(1)}, f32[24,4,1,8,128]{4,3,2,1,0:T(8,128)S(1)}, f32[24,4,1,8,128]{4,3,2,1,0:T(8,128)S(1)}, f32[24,4,1,8,1...) custom-call(f32[8,16,128]{2,1,0:T(8,128)S(1)} %get-tuple-element.46., ...), custom_call_target="tpu_custom_call" | custom-call | tf_op jit(solution)/shard_map/pallas_call | solution.py:745
  45.3 17.3 %all_to_all.10.mine_b = f32[16,2,8,128]{3,2,1,0:T(8,128)S(1)} all-to-all(f32[16,2,8,128]{3,2,1,0:T(8,128)S(1)} %get-tuple-element.53), channel_id=1, replica_groups=mesh['gx'=8,'gy_far'=2,'gy_near'=2] {'gx','gy_far'}, dimensions={0} | all-to-all | bytes 262144 | tf_op jit(solution)/shard_map/all_to_all | solution.py:768
  62.6 0.0 collective-permute-start.9
  62.6 1.3 %collective-permute-done.9.other_b = f32[16,2,8,128]{3,2,1,0:T(8,128)S(1)} collective-permute-done((f32[16,2,8,128]{3,2,1,0:T(8,128)S(1)}, f32[16,2,8,128]{3,2,1,0:T(8,128)S(1)}, u32[]{:S(2)}, u32[]{:S(2)}) %collective-permute-start.9) | collective-permute-done | bytes 131104 | tf_op jit(solution)/shard_map/ppermute | solution.py:769
  64.0 6.9 %shard_map.44 = f32[16,32,256]{2,1,0:T(8,128)} custom-call(f32[16,2,8,128]{3,2,1,0:T(8,128)S(1)} %all_to_all.10.mine_b, f32[16,2,8,128]{3,2,1,0:T(8,128)S(1)} %collective-permute-done.9.other_b, f32[16,2,8,128]{3,2,1,0:T(8,128)S(1)} %all-to-all-done.mine_c, f32[16,2,8,128]{3,2,1,0:T(8,128)S(1)} %collective-permute-done.rest_0_.other_c, ...), custom_call_target="tpu_custom_call" | custom-call | tf_op jit(solution)/shard_map/pallas_call | solution.py:835
  (1 shorter events, 0.0 us)
Async XLA Ops:
  1.3 17.6 %collective-permute-start.1 = (f32[10,32,256]{2,1,0:T(8,128)S(1)}, f32[10,32,256]{2,1,0:T(8,128)S(1)}, u32[]{:S(2)}, u32[]{:S(2)}) collective-permute-start(f32[10,32,256]{2,1,0:T(8,128)S(1)} %get-tuple-element.38), channel_id=1, source_target_pairs={{0,4},{4,0},{8,12},{12,8},{16,20},{20,16},{24,28},{28,24},{1,5},{5... | collective-permute-start | bytes 983048 | tf_op jit(solution)/shard_map/ppermute | solution.py:764
  4.3 14.6 %collective-permute-start.2 = (f32[10,32,256]{2,1,0:T(8,128)S(1)}, f32[10,32,256]{2,1,0:T(8,128)S(1)}, u32[]{:S(2)}, u32[]{:S(2)}) collective-permute-start(f32[10,32,256]{2,1,0:T(8,128)S(1)} %get-tuple-element.39), channel_id=1, source_target_pairs={{4,8},{8,4},{12,16},{16,12},{20,24},{24,20},{5,9},{9,5},{13,17},{1... | collective-permute-start | bytes 983048 | tf_op jit(solution)/shard_map/ppermute | solution.py:764
  7.3 16.4 %all-to-all-start = ((f32[16,2,8,128]{3,2,1,0:T(8,128)}), f32[16,2,8,128]{3,2,1,0:T(8,128)S(1)}, u32[]{:S(2)}, u32[]{:S(2)}) async-start(f32[16,2,8,128]{3,2,1,0:T(8,128)} %get-tuple-element.35), calls=%async_computation | async-start | bytes 262144 | tf_op jit(solution)/shard_map/all_to_all | solution.py:768
  18.9 7.7 %collective-permute-start.4 = (f32[68,4,256]{2,1,0:T(4,128)S(1)}, f32[68,4,256]{2,1,0:T(4,128)S(1)}, u32[]{:S(2)}, u32[]{:S(2)}) collective-permute-start(f32[68,4,256]{2,1,0:T(4,128)S(1)} %get-tuple-element.45), channel_id=1, source_target_pairs={{1,2},{2,1},{5,6},{6,5},{9,10},{10,9},{13,14},{14,13},{17,18},{18,... | collective-permute-start | bytes 835592 | tf_op jit(solution)/shard_map/ppermute | solution.py:764
  19.6 7.0 %collective-permute-start.3 = (f32[68,4,256]{2,1,0:T(4,128)S(1)}, f32[68,4,256]{2,1,0:T(4,128)S(1)}, u32[]{:S(2)}, u32[]{:S(2)}) collective-permute-start(f32[68,4,256]{2,1,0:T(4,128)S(1)} %get-tuple-element.40.rest_1_), channel_id=1, source_target_pairs={{0,1},{1,0},{2,3},{3,2},{4,5},{5,4},{6,7},{7,6},{8,9},{9,8},{10,11... | collective-permute-start | bytes 835592 | tf_op jit(solution)/shard_map/ppermute | solution.py:764
  23.7 1.3 %collective-permute-start = (f32[16,2,8,128]{3,2,1,0:T(8,128)S(1)}, f32[16,2,8,128]{3,2,1,0:T(8,128)S(1)}, u32[]{:S(2)}, u32[]{:S(2)}) collective-permute-start(f32[16,2,8,128]{3,2,1,0:T(8,128)S(1)} %all-to-all-done.mine_c), channel_id=1, source_target_pairs={{0,1},{1,0},{2,3},{3,2},{4,5},{5,4},{6,7},{7,6},{8,9},{9,8},{10,11... | collective-permute-start | bytes 393224 | tf_op jit(solution)/shard_map/ppermute | solution.py:769
  29.9 7.2 %collective-permute-start.5 = (f32[21,16,128]{2,1,0:T(8,128)S(1)}, f32[21,16,128]{2,1,0:T(8,128)S(1)}, u32[]{:S(2)}, u32[]{:S(2)}) collective-permute-start(f32[21,16,128]{2,1,0:T(8,128)S(1)} %get-tuple-element.48), channel_id=1, source_target_pairs={{0,4},{4,0},{8,12},{12,8},{16,20},{20,16},{24,28},{28,24},{1,5},{5... | collective-permute-start | bytes 516104 | tf_op jit(solution)/shard_map/ppermute | solution.py:764
  31.5 5.5 %collective-permute-start.6 = (f32[21,16,128]{2,1,0:T(8,128)S(1)}, f32[21,16,128]{2,1,0:T(8,128)S(1)}, u32[]{:S(2)}, u32[]{:S(2)}) collective-permute-start(f32[21,16,128]{2,1,0:T(8,128)S(1)} %get-tuple-element.49), channel_id=1, source_target_pairs={{4,8},{8,4},{12,16},{16,12},{20,24},{24,20},{5,9},{9,5},{13,17},{1... | collective-permute-start | bytes 516104 | tf_op jit(solution)/shard_map/ppermute | solution.py:764
  37.1 6.1 %collective-permute-start.8 = (f32[64,8,128]{2,1,0:T(8,128)S(1)}, f32[64,8,128]{2,1,0:T(8,128)S(1)}, u32[]{:S(2)}, u32[]{:S(2)}) collective-permute-start(f32[64,8,128]{2,1,0:T(8,128)S(1)} %get-tuple-element.52), channel_id=1, source_target_pairs={{1,2},{2,1},{5,6},{6,5},{9,10},{10,9},{13,14},{14,13},{17,18},{18,... | collective-permute-start | bytes 786440 | tf_op jit(solution)/shard_map/ppermute | solution.py:764
  37.8 6.6 %collective-permute-start.7 = (f32[64,8,128]{2,1,0:T(8,128)S(1)}, f32[64,8,128]{2,1,0:T(8,128)S(1)}, u32[]{:S(2)}, u32[]{:S(2)}) collective-permute-start(f32[64,8,128]{2,1,0:T(8,128)S(1)} %get-tuple-element.51.sent), channel_id=1, source_target_pairs={{0,1},{1,0},{2,3},{3,2},{4,5},{5,4},{6,7},{7,6},{8,9},{9,8},{10,11... | collective-permute-start | bytes 786440 | tf_op jit(solution)/shard_map/ppermute | solution.py:764
  62.6 1.3 %collective-permute-start.9 = (f32[16,2,8,128]{3,2,1,0:T(8,128)S(1)}, f32[16,2,8,128]{3,2,1,0:T(8,128)S(1)}, u32[]{:S(2)}, u32[]{:S(2)}) collective-permute-start(f32[16,2,8,128]{3,2,1,0:T(8,128)S(1)} %all_to_all.10.mine_b), channel_id=1, source_target_pairs={{0,1},{1,0},{2,3},{3,2},{4,5},{5,4},{6,7},{7,6},{8,9},{9,8},{10,11... | collective-permute-start | bytes 393224 | tf_op jit(solution)/shard_map/ppermute | solution.py:769
